TPU v7x, 256 devices: a whole 4x4x8 slice. The times are simulated.
256 devices in a mesh: tm: 8 (over y, z_lo), space: 32 (over z_hi, x, core).
Axes of the slice: x: 4, y: 4, z: 8 (z_hi: 4, z_lo: 2; z = z_hi * 2 + z_lo), core: 2. Of those that a mesh axis runs over, the one named last changes fastest.
Arguments:
- queries: bfloat16 [8, 4096, 512], P('tm', 'space'), may hold values from -120 to 120
- keys: bfloat16 [8, 4096, 512], P('tm', 'space'), may hold values from -8 to 8
- values: bfloat16 [8, 4096, 512], P('tm', 'space'), may hold values from -6 to 6
- w_query: bfloat16 [512, 512], replicated, may hold values from -0.25 to 0.25
- w_key: bfloat16 [512, 512], replicated, may hold values from -0.25 to 0.25
- w_value: bfloat16 [512, 512], replicated, may hold values from -0.25 to 0.25
- grad_out: bfloat16 [8, 4096, 512], P('tm', 'space'), may hold values from -6 to 6
- tile_list: int32 [8, 32, 8, 2], replicated, may hold values from 0 to 63, as said below
- tile_count: int32 [8, 32, 8], replicated, may hold values from 1 to 2
Outputs:
- mixed: bfloat16 [8, 4096, 512], P('tm', 'space')
- grad_queries: bfloat16 [8, 4096, 512], P('tm', 'space')
- grad_keys: bfloat16 [8, 4096, 512], P('tm', 'space')
- grad_values: bfloat16 [8, 4096, 512], P('tm', 'space')
Inputs may be any that keep to these rules, and one draw needn't show every extreme that they name: For one query frame t and the query blocks of one index s of space (blocks s * 1 to (s + 1) * 1 - 1), the entries of tile_list for all key frames and slots, live or not, name tiles whose owner, tile // 2, occurs at most once; in every query frame one owner (the same for all indices s) is named exactly once by the lists of every index s.
All inputs are finite; a program needn't handle non-finite values.
Results may differ from a plain program's by a relative error of at most 0.015.
Values may be sent and summed in bfloat16 or wider, within the bound.
No kernel may reach another device: no remote copies, remote signals or barrier semaphores. Data moves between devices by JAX's collectives and lax.ppermute only.
A program may use at most 64 MiB of HBM per device.

v0:
```python
import functools

import jax
import jax.numpy as jnp
from jax import lax
from jax.experimental import pallas as pl
from jax.experimental.pallas import tpu as pltpu
from jax.sharding import Mesh
from jax.sharding import PartitionSpec as P

HEAD = 64
HEADS = 8
TILE = 64
FRAMES = 8
SLOTS = 2
WIDTH = 512
PAIRS = 4
ROWS = 128
SCALE = 0.125
PIECES = 8
TM = ("y", "zl")
SPACE = ("zh", "x", "c")
VMEM_LIMIT = 56 * 1024 * 1024


def params():
    return pltpu.CompilerParams(vmem_limit_bytes=VMEM_LIMIT)


def whole():
    return pl.BlockSpec()


def smem():
    return pl.BlockSpec(memory_space=pltpu.SMEM)


def hbm():
    return pl.BlockSpec(memory_space=pl.ANY)


def shift(value, axis, step):
    size = lax.axis_size(axis)
    return lax.ppermute(value, axis, [(i, (i + step) % size) for i in range(size)])


def after(value, *others):
    return lax.optimization_barrier((value,) + others)[0]


def swap(pieces):
    return [shift(piece, "c", 1) for piece in pieces]


def spread(value, axis):
    far = shift(value, axis, 2)
    return [shift(value, axis, -1), far, shift(value, axis, 1)]


def gather_frames(keys, values):
    column_k = jnp.concatenate([keys] + spread(keys, "zh"), axis=0)
    column_v = jnp.concatenate([values] + spread(values, "zh"), axis=0)
    rows_k = spread(column_k, "x")
    rows_v = spread(column_v, "x")
    rows_k = lax.optimization_barrier(tuple(rows_k) + (column_v,))[:3]
    pieces_k = [column_k, *rows_k]
    pieces_v = [column_v, *rows_v]
    return pieces_k + swap(pieces_k), pieces_v + swap(pieces_v), rows_v[1]


def select_kernel(piece_ref, row_ref, *refs):
    pieces, out_ref, sems = refs[:PIECES], refs[PIECES], refs[PIECES + 1]

    @pl.loop(0, FRAMES * SLOTS)
    def _(slot):
        which = piece_ref[slot]
        row = row_ref[slot]
        for number, piece in enumerate(pieces):

            @pl.when(which == number)
            def _():
                pltpu.make_async_copy(
                    piece.at[pl.ds(row, 1)], out_ref.at[pl.ds(slot, 1)], sems.at[slot]
                ).start()

    @pl.loop(0, FRAMES * SLOTS)
    def _(slot):
        pltpu.make_async_copy(
            pieces[0].at[pl.ds(0, 1)], out_ref.at[pl.ds(slot, 1)], sems.at[slot]
        ).wait()


def select_tiles(piece_ids, piece_rows, pieces):
    return pl.pallas_call(
        select_kernel,
        out_shape=jax.ShapeDtypeStruct((FRAMES * SLOTS, TILE, WIDTH), jnp.bfloat16),
        in_specs=[smem(), smem()] + [hbm()] * PIECES,
        out_specs=whole(),
        scratch_shapes=[pltpu.SemaphoreType.DMA((FRAMES * SLOTS,))],
        compiler_params=params(),
        name="select_tiles",
    )(piece_ids, piece_rows, *pieces)


def split_heads(pair):
    rows = lax.broadcasted_iota(jnp.int32, pair.shape, 0)
    zero = jnp.zeros_like(pair)
    return jnp.concatenate(
        [jnp.where(rows < HEAD, pair, zero), jnp.where(rows >= HEAD, pair, zero)], axis=1
    )


def join_heads(both):
    return jnp.concatenate([both[:HEAD, :ROWS], both[HEAD:, ROWS:]], axis=0)


def dot_nn(a, b):
    return jnp.dot(a, b, preferred_element_type=jnp.float32)


def dot_tn(a, b):
    return lax.dot_general(a, b, (((0,), (0,)), ((), ())), preferred_element_type=jnp.float32)


def dot_nt(a, b):
    return lax.dot_general(a, b, (((1,), (1,)), ((), ())), preferred_element_type=jnp.float32)


def weights_kernel(count_ref, query_ref, key_ref, weight_ref, narrow_ref):
    frame = pl.program_id(0)
    limit = count_ref[frame] * TILE
    rows = lax.broadcasted_iota(jnp.int32, (ROWS, 2 * ROWS), 0)
    live = rows < limit
    for pair in range(PAIRS):
        lanes = slice(pair * 128, pair * 128 + 128)
        scores = dot_nn(key_ref[0, :, lanes], split_heads(query_ref[lanes, :])) * SCALE
        scores = jnp.where(live, scores, -jnp.inf)
        raised = jnp.exp(scores - jnp.max(scores, axis=0, keepdims=True))
        weights = raised / jnp.sum(raised, axis=0, keepdims=True)
        weight_ref[0, pair] = weights
        narrow_ref[0, pair] = weights.astype(jnp.bfloat16)


def attend_weights(counts, query_t, keys):
    return pl.pallas_call(
        weights_kernel,
        grid=(FRAMES,),
        out_shape=(
            jax.ShapeDtypeStruct((FRAMES, PAIRS, ROWS, 2 * ROWS), jnp.float32),
            jax.ShapeDtypeStruct((FRAMES, PAIRS, ROWS, 2 * ROWS), jnp.bfloat16),
        ),
        in_specs=[
            smem(),
            pl.BlockSpec((WIDTH, ROWS), lambda f: (0, 0)),
            pl.BlockSpec((1, ROWS, WIDTH), lambda f: (f, 0, 0)),
        ],
        out_specs=(pl.BlockSpec((1, PAIRS, ROWS, 2 * ROWS), lambda f: (f, 0, 0, 0)),) * 2,
        compiler_params=params(),
        name="attend_weights",
    )(counts, query_t, keys)


def pool_kernel(
    frame_ref,
    weight_ref,
    value_ref,
    wq_ref,
    wk_ref,
    wv_ref,
    wqt_ref,
    wkt_ref,
    wvt_ref,
    go_ref,
    mixed_ref,
    gt_ref,
    dv_ref,
    traj,
    pooled_k,
    pooled_v,
    pooled_q,
    grad_pk,
    grad_pv,
    grad_pq,
    total,
):
    for frame in range(FRAMES):
        for pair in range(PAIRS):
            lanes = slice(pair * 128, pair * 128 + 128)
            both = dot_tn(value_ref[frame, :, lanes], weight_ref[frame, pair])
            traj[lanes, frame * ROWS : (frame + 1) * ROWS] = join_heads(both).astype(jnp.bfloat16)
    own = pl.ds(pl.multiple_of(frame_ref[0] * ROWS, ROWS), ROWS)
    pooled_q[...] = dot_nn(wqt_ref[...], traj[:, own])
    pooled_k[...] = dot_nn(wkt_ref[...], traj[...])
    pooled_v[...] = dot_nn(wvt_ref[...], traj[...])
    for head in range(HEADS):
        rows = slice(head * HEAD, (head + 1) * HEAD)
        query = pooled_q[rows, :]
        upstream = go_ref[rows, :].astype(jnp.float32)
        columns = [slice(f * ROWS, (f + 1) * ROWS) for f in range(FRAMES)]
        logits = jnp.concatenate(
            [
                jnp.sum(query * pooled_k[rows, columns[f]], axis=0, keepdims=True)
                for f in range(FRAMES)
            ],
            axis=0,
        )
        raised = jnp.exp(logits * SCALE)
        fw = raised / jnp.sum(raised, axis=0, keepdims=True)
        grad_fw = jnp.concatenate(
            [
                jnp.sum(upstream * pooled_v[rows, columns[f]], axis=0, keepdims=True)
                for f in range(FRAMES)
            ],
            axis=0,
        )
        inner = jnp.sum(fw * grad_fw, axis=0, keepdims=True)
        grad_logit = fw * (grad_fw - inner) * SCALE
        mixed = jnp.zeros((HEAD, ROWS), jnp.float32)
        grad_query = jnp.zeros((HEAD, ROWS), jnp.float32)
        for f in range(FRAMES):
            weight = fw[f : f + 1, :]
            slope = grad_logit[f : f + 1, :]
            mixed = mixed + weight * pooled_v[rows, columns[f]]
            grad_query = grad_query + slope * pooled_k[rows, columns[f]]
            grad_pk[rows, columns[f]] = (slope * query).astype(jnp.bfloat16)
            grad_pv[rows, columns[f]] = (weight * upstream).astype(jnp.bfloat16)
        pooled_q[rows, :] = mixed
        grad_pq[rows, :] = grad_query.astype(jnp.bfloat16)
    mixed_ref[...] = pooled_q[...].T.astype(jnp.bfloat16)
    total[...] = dot_nn(wk_ref[...], grad_pk[...]) + dot_nn(wv_ref[...], grad_pv[...])
    total[:, own] += dot_nn(wq_ref[...], grad_pq[...])
    for frame in range(FRAMES):
        gt_ref[frame] = total[:, frame * ROWS : (frame + 1) * ROWS].astype(jnp.bfloat16)
        for pair in range(PAIRS):
            lanes = slice(pair * 128, pair * 128 + 128)
            dv_ref[frame, :, lanes] = dot_nt(
                weight_ref[frame, pair], split_heads(gt_ref[frame, lanes, :])
            ).astype(jnp.bfloat16)


def pool_frames(frame_now, weights, values, w_query, w_key, w_value, upstream_t):
    wide = (WIDTH, FRAMES * ROWS)
    return pl.pallas_call(
        pool_kernel,
        out_shape=(
            jax.ShapeDtypeStruct((ROWS, WIDTH), jnp.bfloat16),
            jax.ShapeDtypeStruct((FRAMES, WIDTH, ROWS), jnp.bfloat16),
            jax.ShapeDtypeStruct((FRAMES, ROWS, WIDTH), jnp.bfloat16),
        ),
        in_specs=[smem()] + [whole()] * 9,
        out_specs=(whole(), whole(), whole()),
        scratch_shapes=[
            pltpu.VMEM(wide, jnp.bfloat16),
            pltpu.VMEM(wide, jnp.float32),
            pltpu.VMEM(wide, jnp.float32),
            pltpu.VMEM((WIDTH, ROWS), jnp.float32),
            pltpu.VMEM(wide, jnp.bfloat16),
            pltpu.VMEM(wide, jnp.bfloat16),
            pltpu.VMEM((WIDTH, ROWS), jnp.bfloat16),
            pltpu.VMEM(wide, jnp.float32),
        ],
        compiler_params=params(),
        name="pool_frames",
    )(
        frame_now.reshape(1),
        weights,
        values,
        w_query,
        w_key,
        w_value,
        w_query.T,
        w_key.T,
        w_value.T,
        upstream_t,
    )


def back_kernel(query_ref, key_ref, value_ref, weight_ref, gt_ref, gq_ref, dk_ref, total):
    frame = pl.program_id(0)

    @pl.when(frame == 0)
    def _():
        total[...] = jnp.zeros_like(total)

    for pair in range(PAIRS):
        lanes = slice(pair * 128, pair * 128 + 128)
        weight = weight_ref[0, pair]
        grad_w = dot_nn(value_ref[0, :, lanes], split_heads(gt_ref[0, lanes, :]))
        inner = jnp.sum(weight * grad_w, axis=0, keepdims=True)
        grad_s = (weight * (grad_w - inner) * SCALE).astype(jnp.bfloat16)
        dk_ref[0, :, lanes] = dot_nt(grad_s, split_heads(query_ref[lanes, :])).astype(jnp.bfloat16)
        total[lanes, :] += join_heads(dot_tn(key_ref[0, :, lanes], grad_s))

    @pl.when(frame == FRAMES - 1)
    def _():
        gq_ref[...] = total[...].T.astype(jnp.bfloat16)


def attend_back(query_t, keys, values, weights, grad_traj):
    by_frame = pl.BlockSpec((1, ROWS, WIDTH), lambda f: (f, 0, 0))
    fixed = pl.BlockSpec((WIDTH, ROWS), lambda f: (0, 0))
    return pl.pallas_call(
        back_kernel,
        grid=(FRAMES,),
        out_shape=(
            jax.ShapeDtypeStruct((ROWS, WIDTH), jnp.bfloat16),
            jax.ShapeDtypeStruct((FRAMES, ROWS, WIDTH), jnp.bfloat16),
        ),
        in_specs=[
            fixed,
            by_frame,
            by_frame,
            pl.BlockSpec((1, PAIRS, ROWS, 2 * ROWS), lambda f: (f, 0, 0, 0)),
            pl.BlockSpec((1, WIDTH, ROWS), lambda f: (f, 0, 0)),
        ],
        out_specs=(pl.BlockSpec((ROWS, WIDTH), lambda f: (0, 0)), by_frame),
        scratch_shapes=[pltpu.VMEM((WIDTH, ROWS), jnp.float32)],
        compiler_params=params(),
        name="attend_back",
    )(query_t, keys, values, weights, grad_traj)


def merge_kernel(place_ref, mine_ref, theirs_ref, *refs):
    outs, acc = refs[:5], refs[5]
    acc[...] = jnp.zeros_like(acc)
    for source, ref in enumerate((mine_ref, theirs_ref)):

        @pl.loop(0, FRAMES * SLOTS)
        def _(slot):
            place = place_ref[source * FRAMES * SLOTS + slot]

            @pl.when(place >= 0)
            def _():
                acc[place] += ref[slot].astype(jnp.float32)

    at = 0
    for out in outs:
        size = out.shape[0]
        out[...] = acc[at : at + size].astype(jnp.bfloat16)
        at += size


def merge_slots(places, mine, theirs):
    sizes = (8, 8, 4, 4, 8)
    return pl.pallas_call(
        merge_kernel,
        out_shape=tuple(jax.ShapeDtypeStruct((n, TILE, WIDTH), jnp.bfloat16) for n in sizes),
        in_specs=[smem(), whole(), whole()],
        out_specs=(whole(),) * 5,
        scratch_shapes=[pltpu.VMEM((32, TILE, WIDTH), jnp.float32)],
        compiler_params=params(),
        name="merge_slots",
    )(places, mine, theirs)


def add_wide(*terms):
    total = terms[0].astype(jnp.float32)
    for term in terms[1:]:
        total = total + term.astype(jnp.float32)
    return total.astype(jnp.bfloat16)


def scatter_rows(merged):
    to_right, to_left, keep_right, keep_left, own = merged
    from_left = shift(to_right, "x", 1)
    from_right = shift(to_left, "x", -1)
    return keep_right, keep_left, own, from_left, from_right


def scatter_across(state):
    keep_right, keep_left, own, from_left, from_right = state
    low = shift(add_wide(keep_right, from_left[0:4]), "x", 1)
    high = shift(add_wide(keep_left, from_right[0:4]), "x", -1)
    return own, from_left, from_right, low, high


def scatter_column(state):
    own, from_left, from_right, low, high = state
    here = add_wide(own[0:2], from_right[4:6], low[0:2])
    up = add_wide(own[2:4], from_right[6:8], low[2:4])
    far = add_wide(own[4:6], from_left[4:6], high[0:2])
    down = add_wide(own[6:8], from_left[6:8], high[2:4])
    return add_wide(here, shift(up, "zh", 1), shift(far, "zh", 2), shift(down, "zh", -1))


def per_device(queries, keys, values, w_query, w_key, w_value, grad_out, tile_list, tile_count):
    frame_now = lax.axis_index("y") * 2 + lax.axis_index("zl")
    at_z, at_x, at_c = (lax.axis_index(a) for a in SPACE)
    my_space = (at_z * 4 + at_x) * 2 + at_c
    pair_space = (at_z * 4 + at_x) * 2

    wanted = lax.dynamic_slice(
        tile_list, (0, pair_space, frame_now, 0), (FRAMES, 2, 1, SLOTS)
    ).reshape(FRAMES, 2, SLOTS)
    wanted = wanted.transpose(1, 0, 2).reshape(2, FRAMES * SLOTS)
    mine_wanted = lax.dynamic_index_in_dim(wanted, at_c, 0, keepdims=False)
    their_wanted = lax.dynamic_index_in_dim(wanted, 1 - at_c, 0, keepdims=False)

    def locate(tiles):
        owner = tiles // 2
        z_rel = (owner // 8 - at_z) % 4
        x_rel = (owner // 2 % 4 - at_x) % 4
        other = (owner % 2 != at_c).astype(jnp.int32)
        return z_rel * 2 + tiles % 2, x_rel, other

    inside, x_rel, other = locate(mine_wanted)
    piece_ids = x_rel + 4 * other

    def placing(tiles):
        inside, x_rel, other = locate(tiles)
        high = inside >= 4
        low_part = inside % 4
        place = jnp.where(
            x_rel == 0,
            24 + inside,
            jnp.where(
                x_rel == 1,
                jnp.where(high, 4 + low_part, 16 + low_part),
                jnp.where(
                    x_rel == 2,
                    jnp.where(high, 8 + low_part, low_part),
                    jnp.where(high, 20 + low_part, 12 + low_part),
                ),
            ),
        )
        return jnp.where(other == 1, -1, place)

    places = jnp.concatenate([placing(mine_wanted), placing(their_wanted)])

    def exchange(chosen):
        return lax.all_to_all(
            chosen.reshape(FRAMES, SLOTS * TILE, WIDTH), TM, split_axis=0, concat_axis=0, tiled=True
        )

    counts = lax.dynamic_slice(tile_count, (frame_now, my_space, 0), (1, 1, FRAMES)).reshape(FRAMES)
    query_t = queries.reshape(ROWS, WIDTH).T
    upstream_t = grad_out.reshape(ROWS, WIDTH).T
    own_shape = (2, TILE, WIDTH)
    key_pieces, value_pieces, far_v = gather_frames(keys.reshape(own_shape), values.reshape(own_shape))
    key_slots = exchange(after(select_tiles(piece_ids, inside, key_pieces), far_v))
    value_slots = exchange(select_tiles(piece_ids, inside, value_pieces))
    weights, narrow = attend_weights(counts, query_t, key_slots)
    mixed, grad_traj, slot_dv = pool_frames(
        frame_now, narrow, value_slots, w_query, w_key, w_value, upstream_t
    )
    grad_queries, slot_dk = attend_back(query_t, key_slots, value_slots, weights, grad_traj)
    owned_v = exchange(slot_dv).reshape(FRAMES * SLOTS, TILE, WIDTH)
    merged_v = merge_slots(places, owned_v, shift(owned_v, "c", 1))
    owned_k = exchange(slot_dk).reshape(FRAMES * SLOTS, TILE, WIDTH)
    owned_k = after(owned_k, *merged_v)
    state_v = scatter_rows(merged_v)
    merged_k = merge_slots(places, owned_k, shift(owned_k, "c", 1))
    state_k = scatter_rows(merged_k)
    state_v = lax.optimization_barrier(state_v + (merged_k[0],))[:5]
    state_v = scatter_across(state_v)
    state_k = scatter_across(state_k)
    sum_values = scatter_column(state_v)
    sum_keys = scatter_column(state_k)
    shape = (1, ROWS, WIDTH)
    return (
        mixed.reshape(shape),
        grad_queries.reshape(shape),
        sum_keys.reshape(shape),
        sum_values.reshape(shape),
    )


def solution(mesh):
    fine = Mesh(mesh.devices.reshape(4, 2, 4, 4, 2), TM + SPACE)
    rows = P(TM, SPACE, None)
    return jax.shard_map(
        per_device,
        mesh=fine,
        in_specs=(rows, rows, rows, P(), P(), P(), rows, P(), P()),
        out_specs=(rows, rows, rows, rows),
        check_vma=False,
    )
```

profile of v0, /device:TPU:1, one launch (start us, length us, event | category | flops | bytes accessed | tf_op | source)
XLA Modules:
  0.0 218.9 jit_solution(5565271073447770051)
XLA Ops:
  0.6 3.9 %collective-permute-start.2 = (bf16[2,64,512]{2,1,0:T(8,128)(2,1)}, bf16[2,64,512]{2,1,0:T(8,128)(2,1)S(1)}, u32[]{:S(2)}, u32[]{:S(2)}) collective-permute-start(bf16[2,64,512]{2,1,0:T(8,128)(2,1)} %bitcast.69), channel_id=1, source_target_pairs={{0,8},{8,16},{16,24},{24,0},{1,9},{9,17},{17,25},{25,1},{2,10},{10... | collective-permute-start | bytes 393224 | tf_op jit(solution)/shard_map/ppermute | solution.py:44
  4.5 5.1 %collective-permute-start.1 = (bf16[2,64,512]{2,1,0:T(8,128)(2,1)}, bf16[2,64,512]{2,1,0:T(8,128)(2,1)S(1)}, u32[]{:S(2)}, u32[]{:S(2)}) collective-permute-start(bf16[2,64,512]{2,1,0:T(8,128)(2,1)} %bitcast.70), channel_id=1, source_target_pairs={{0,16},{8,24},{16,0},{24,8},{1,17},{9,25},{17,1},{25,9},{2,18},{10... | collective-permute-start | bytes 393224 | tf_op jit(solution)/shard_map/ppermute | solution.py:44
  9.7 2.4 %collective-permute-start = (bf16[2,64,512]{2,1,0:T(8,128)(2,1)}, bf16[2,64,512]{2,1,0:T(8,128)(2,1)S(1)}, u32[]{:S(2)}, u32[]{:S(2)}) collective-permute-start(bf16[2,64,512]{2,1,0:T(8,128)(2,1)} %bitcast.71), channel_id=1, source_target_pairs={{0,24},{8,0},{16,8},{24,16},{1,25},{9,1},{17,9},{25,17},{2,26},{10... | collective-permute-start | bytes 393224 | tf_op jit(solution)/shard_map/ppermute | solution.py:44
  12.0 6.4 %collective-permute-done.1 = bf16[2,64,512]{2,1,0:T(8,128)(2,1)S(1)} collective-permute-done((bf16[2,64,512]{2,1,0:T(8,128)(2,1)}, bf16[2,64,512]{2,1,0:T(8,128)(2,1)S(1)}, u32[]{:S(2)}, u32[]{:S(2)}) %collective-permute-start.1) | collective-permute-done | bytes 131104 | tf_op jit(solution)/shard_map/ppermute | solution.py:44
  18.5 4.3 %collective-permute-done = bf16[2,64,512]{2,1,0:T(8,128)(2,1)S(1)} collective-permute-done((bf16[2,64,512]{2,1,0:T(8,128)(2,1)}, bf16[2,64,512]{2,1,0:T(8,128)(2,1)S(1)}, u32[]{:S(2)}, u32[]{:S(2)}) %collective-permute-start) | collective-permute-done | bytes 131104 | tf_op jit(solution)/shard_map/ppermute | solution.py:44
  22.8 1.0 pad_maximum_fusion.refs_0_
  23.8 1.3 collective-permute-start.5
  25.1 2.5 %collective-permute-start.4 = (bf16[8,64,512]{2,1,0:T(8,128)(2,1)S(1)}, bf16[8,64,512]{2,1,0:T(8,128)(2,1)S(1)}, u32[]{:S(2)}, u32[]{:S(2)}) collective-permute-start(bf16[8,64,512]{2,1,0:T(8,128)(2,1)S(1)} %pad_maximum_fusion.refs_0_), channel_id=1, source_target_pairs={{0,4},{2,6},{4,0},{6,2},{1,5},{3,7},{5,1},{7,3},{8,12},{10,14},{12... | collective-permute-start | bytes 1572872 | tf_op jit(solution)/shard_map/ppermute | solution.py:44
  27.5 1.2 collective-permute-start.3
  29.6 4.5 %collective-permute-start.7 = (bf16[2,64,512]{2,1,0:T(8,128)(2,1)}, bf16[2,64,512]{2,1,0:T(8,128)(2,1)S(1)}, u32[]{:S(2)}, u32[]{:S(2)}) collective-permute-start(bf16[2,64,512]{2,1,0:T(8,128)(2,1)} %bitcast.74), channel_id=1, source_target_pairs={{0,16},{8,24},{16,0},{24,8},{1,17},{9,25},{17,1},{25,9},{2,18},{10... | collective-permute-start | bytes 393224 | tf_op jit(solution)/shard_map/ppermute | solution.py:44
  34.1 2.5 %collective-permute-done.8 = bf16[2,64,512]{2,1,0:T(8,128)(2,1)S(1)} collective-permute-done((bf16[2,64,512]{2,1,0:T(8,128)(2,1)}, bf16[2,64,512]{2,1,0:T(8,128)(2,1)S(1)}, u32[]{:S(2)}, u32[]{:S(2)}) %collective-permute-start.8) | collective-permute-done | bytes 131104 | tf_op jit(solution)/shard_map/ppermute | solution.py:44
  36.6 1.3 collective-permute-start.6
  37.9 3.7 %collective-permute-done.7 = bf16[2,64,512]{2,1,0:T(8,128)(2,1)S(1)} collective-permute-done((bf16[2,64,512]{2,1,0:T(8,128)(2,1)}, bf16[2,64,512]{2,1,0:T(8,128)(2,1)S(1)}, u32[]{:S(2)}, u32[]{:S(2)}) %collective-permute-start.7) | collective-permute-done | bytes 131104 | tf_op jit(solution)/shard_map/ppermute | solution.py:44
  41.6 2.2 %collective-permute-start.9 = (bf16[8,64,512]{2,1,0:T(8,128)(2,1)S(1)}, bf16[8,64,512]{2,1,0:T(8,128)(2,1)}, u32[]{:S(2)}, u32[]{:S(2)}) collective-permute-start(bf16[8,64,512]{2,1,0:T(8,128)(2,1)S(1)} %pad_maximum_fusion.refs_0_), channel_id=1, source_target_pairs={{0,1},{1,0},{2,3},{3,2},{4,5},{5,4},{6,7},{7,6},{8,9},{9,8},{10,11... | collective-permute-start | bytes 1572872 | tf_op jit(solution)/shard_map/ppermute | solution.py:44
  43.8 1.0 pad_maximum_fusion.1.refs_0_
  45.1 5.2 %collective-permute-done.4.refs_2_ = bf16[8,64,512]{2,1,0:T(8,128)(2,1)S(1)} collective-permute-done((bf16[8,64,512]{2,1,0:T(8,128)(2,1)S(1)}, bf16[8,64,512]{2,1,0:T(8,128)(2,1)S(1)}, u32[]{:S(2)}, u32[]{:S(2)}) %collective-permute-start.4) | collective-permute-done | bytes 524320 | tf_op jit(solution)/shard_map/ppermute | solution.py:44
  50.3 2.3 %collective-permute-start.10 = (bf16[8,64,512]{2,1,0:T(8,128)(2,1)S(1)}, bf16[8,64,512]{2,1,0:T(8,128)(2,1)}, u32[]{:S(2)}, u32[]{:S(2)}) collective-permute-start(bf16[8,64,512]{2,1,0:T(8,128)(2,1)S(1)} %collective-permute-done.3.refs_1_), channel_id=1, source_target_pairs={{0,1},{1,0},{2,3},{3,2},{4,5},{5,4},{6,7},{7,6},{8,9},{9,8},{10,11... | collective-permute-start | bytes 1572872 | tf_op jit(solution)/shard_map/ppermute | solution.py:44
  55.8 3.1 %select_tiles.2 = bf16[16,64,512]{2,1,0:T(8,128)(2,1)} custom-call(s32[16]{0:T(128)} %fusion.2.piece_ref, s32[16]{0:T(128)} %get-tuple-element.59.row_ref, bf16[8,64,512]{2,1,0:T(8,128)(2,1)} %copy-done.7, bf16[8,64,512]{2,1,0:T(8,128)(2,1)} %copy-done.15, bf16[8,64,512]{2,1,0:T(8,128)(2,1)} %copy-done.14, bf16[8,64,512]{2,1,0:T(8,128)(2,1)} %copy-done.13, ...), custom_call_target="tpu_custom_call" | custom-call | tf_op jit(solution)/shard_map/select_tiles/pallas_call | solution.py:94
  59.0 2.6 %collective-permute-done.13.refs_2_ = bf16[8,64,512]{2,1,0:T(8,128)(2,1)S(1)} collective-permute-done((bf16[8,64,512]{2,1,0:T(8,128)(2,1)S(1)}, bf16[8,64,512]{2,1,0:T(8,128)(2,1)S(1)}, u32[]{:S(2)}, u32[]{:S(2)}) %collective-permute-start.13) | collective-permute-done | bytes 524320 | tf_op jit(solution)/shard_map/ppermute | solution.py:44
  61.5 4.2 %all-to-all-start = ((bf16[8,128,512]{2,1,0:T(8,128)(2,1)}), bf16[8,128,512]{2,1,0:T(8,128)(2,1)S(1)}, u32[]{:S(2)}, u32[]{:S(2)}) async-start(bf16[8,128,512]{2,1,0:T(8,128)(2,1)} %bitcast.59), calls=%async_computation | async-start | bytes 2097152 | tf_op jit(solution)/shard_map/all_to_all | solution.py:431
  65.8 1.6 collective-permute-start.15
  67.3 1.2 collective-permute-start.14
  68.5 2.2 collective-permute-start.16
  70.7 8.2 %collective-permute-done.15.refs_3_ = bf16[8,64,512]{2,1,0:T(8,128)(2,1)S(1)} collective-permute-done((bf16[8,64,512]{2,1,0:T(8,128)(2,1)S(1)}, bf16[8,64,512]{2,1,0:T(8,128)(2,1)S(1)}, u32[]{:S(2)}, u32[]{:S(2)}) %collective-permute-start.15) | collective-permute-done | bytes 524320 | tf_op jit(solution)/shard_map/ppermute | solution.py:44
  78.9 2.5 %collective-permute-start.19 = (bf16[8,64,512]{2,1,0:T(8,128)(2,1)S(1)}, bf16[8,64,512]{2,1,0:T(8,128)(2,1)S(1)}, u32[]{:S(2)}, u32[]{:S(2)}) collective-permute-start(bf16[8,64,512]{2,1,0:T(8,128)(2,1)S(1)} %collective-permute-done.15.refs_3_), channel_id=1, source_target_pairs={{0,1},{1,0},{2,3},{3,2},{4,5},{5,4},{6,7},{7,6},{8,9},{9,8},{10,11... | collective-permute-start | bytes 1572872 | tf_op jit(solution)/shard_map/ppermute | solution.py:44
  81.9 1.0 collective-permute-done.19.refs_7_
  85.3 3.1 %select_tiles.3 = bf16[16,64,512]{2,1,0:T(8,128)(2,1)} custom-call(s32[16]{0:T(128)} %fusion.2.piece_ref, s32[16]{0:T(128)} %get-tuple-element.59.row_ref, bf16[8,64,512]{2,1,0:T(8,128)(2,1)} %copy-done.8, bf16[8,64,512]{2,1,0:T(8,128)(2,1)} %copy-done.18, bf16[8,64,512]{2,1,0:T(8,128)(2,1)} %copy-done.16, bf16[8,64,512]{2,1,0:T(8,128)(2,1)} %copy-done.17, ...), custom_call_target="tpu_custom_call" | custom-call | tf_op jit(solution)/shard_map/select_tiles/pallas_call | solution.py:94
  88.4 5.1 %all-to-all-start.1 = ((bf16[8,128,512]{2,1,0:T(8,128)(2,1)}), bf16[8,128,512]{2,1,0:T(8,128)(2,1)S(1)}, u32[]{:S(2)}, u32[]{:S(2)}) async-start(bf16[8,128,512]{2,1,0:T(8,128)(2,1)} %bitcast.60), calls=%async_computation.1 | async-start | bytes 2097152 | tf_op jit(solution)/shard_map/all_to_all | solution.py:431
  95.1 1.0 copy.23
  96.1 1.0 copy.24
  97.1 2.1 copy.25
  99.2 1.4 dynamic-slice_reduce_fusion.count_ref
  100.6 7.5 %attend_weights.1 = (f32[8,4,128,256]{3,2,1,0:T(8,128)}, bf16[8,4,128,256]{3,2,1,0:T(8,128)(2,1)}) custom-call(s32[8]{0:T(128)} %dynamic-slice_reduce_fusion.count_ref, bf16[512,128]{1,0:T(8,128)(2,1)} %bitcast.64, bf16[8,128,512]{2,1,0:T(8,128)(2,1)} %copy-done.2), custom_call_target="tpu_custom_call" | custom-call | tf_op jit(solution)/shard_map/attend_weights/pallas_call | solution.py:145
  108.8 1.0 copy-done.1
  109.8 8.2 %pool_frames.1 = (bf16[128,512]{1,0:T(8,128)(2,1)}, bf16[8,512,128]{2,1,0:T(8,128)(2,1)}, bf16[8,128,512]{2,1,0:T(8,128)(2,1)}) custom-call(s32[1]{0:T(128)} %bitcast.frame_ref, bf16[8,4,128,256]{3,2,1,0:T(8,128)(2,1)} %get-tuple-element.35.weight_ref, bf16[8,128,512]{2,1,0:T(8,128)(2,1)} %copy-done.1, bf16[512,512]{1,0:T(8,128)(2,1)} %wq_ref.1, ...), custom_call_target="tpu_custom_call" | custom-call | tf_op jit(solution)/shard_map/pool_frames/pallas_call | solution.py:243
  117.9 4.5 %all-to-all-start.3 = ((bf16[8,128,512]{2,1,0:T(8,128)(2,1)}), bf16[8,128,512]{2,1,0:T(8,128)(2,1)S(1)}, u32[]{:S(2)}, u32[]{:S(2)}) async-start(bf16[8,128,512]{2,1,0:T(8,128)(2,1)} %get-tuple-element.41), calls=%async_computation.3 | async-start | bytes 2097152 | tf_op jit(solution)/shard_map/all_to_all | solution.py:431
  122.4 10.6 %attend_back.1 = (bf16[128,512]{1,0:T(8,128)(2,1)}, bf16[8,128,512]{2,1,0:T(8,128)(2,1)}) custom-call(bf16[512,128]{1,0:T(8,128)(2,1)} %bitcast.65, bf16[8,128,512]{2,1,0:T(8,128)(2,1)} %copy-done.2, bf16[8,128,512]{2,1,0:T(8,128)(2,1)} %copy-done.1, f32[8,4,128,256]{3,2,1,0:T(8,128)} %get-tuple-element.37.weight_ref, ...), custom_call_target="tpu_custom_call" | custom-call | tf_op jit(solution)/shard_map/attend_back/pallas_call | solution.py:302
  133.0 3.6 %all-to-all-done.3 = bf16[8,128,512]{2,1,0:T(8,128)(2,1)S(1)} async-done(((bf16[8,128,512]{2,1,0:T(8,128)(2,1)}), bf16[8,128,512]{2,1,0:T(8,128)(2,1)S(1)}, u32[]{:S(2)}, u32[]{:S(2)}) %all-to-all-start.3) | async-done | bytes 1048608 | tf_op jit(solution)/shard_map/all_to_all | solution.py:431
  136.6 4.2 %all-to-all-start.2 = ((bf16[8,128,512]{2,1,0:T(8,128)(2,1)}), bf16[8,128,512]{2,1,0:T(8,128)(2,1)S(1)}, u32[]{:S(2)}, u32[]{:S(2)}) async-start(bf16[8,128,512]{2,1,0:T(8,128)(2,1)} %get-tuple-element.40), calls=%async_computation.2 | async-start | bytes 2097152 | tf_op jit(solution)/shard_map/all_to_all | solution.py:431
  140.9 1.9 collective-permute-start.20
  143.4 1.6 collective-permute-done.20.theirs_ref
  145.0 1.0 copy-done.9
  146.0 3.8 %merge_slots.2 = (bf16[8,64,512]{2,1,0:T(8,128)(2,1)}, bf16[8,64,512]{2,1,0:T(8,128)(2,1)}, bf16[4,64,512]{2,1,0:T(8,128)(2,1)}, bf16[4,64,512]{2,1,0:T(8,128)(2,1)}, bf16[8,64,512]{2,1,0:T(8,128)(2,1)}) custom-call(s32[32]{0:T(128)} %pad_add_fusion.place_ref, bf16[16,64,512]{2,1,0:T(8,128)(2,1)} %bitcast.58, bf16[16,64,512]{2,1,0:T(8,128)(2,1)} %copy-done.9), custom_call_target="tpu_custom_call" | custom-call | tf_op jit(solution)/shard_map/merge_slots/pallas_call | solution.py:345
  149.8 5.1 %all-to-all-done.2 = bf16[8,128,512]{2,1,0:T(8,128)(2,1)S(1)} async-done(((bf16[8,128,512]{2,1,0:T(8,128)(2,1)}), bf16[8,128,512]{2,1,0:T(8,128)(2,1)S(1)}, u32[]{:S(2)}, u32[]{:S(2)}) %all-to-all-start.2) | async-done | bytes 1048608 | tf_op jit(solution)/shard_map/all_to_all | solution.py:431
  154.9 2.6 %collective-permute-start.21 = (bf16[16,64,512]{2,1,0:T(8,128)(2,1)S(1)}, bf16[16,64,512]{2,1,0:T(8,128)(2,1)S(1)}, u32[]{:S(2)}, u32[]{:S(2)}) collective-permute-start(bf16[16,64,512]{2,1,0:T(8,128)(2,1)S(1)} %bitcast.55), channel_id=1, source_target_pairs={{0,1},{1,0},{2,3},{3,2},{4,5},{5,4},{6,7},{7,6},{8,9},{9,8},{10,11... | collective-permute-start | bytes 3145736 | tf_op jit(solution)/shard_map/ppermute | solution.py:44
  157.8 2.4 %collective-permute-start.30 = (bf16[8,64,512]{2,1,0:T(8,128)(2,1)}, bf16[8,64,512]{2,1,0:T(8,128)(2,1)S(1)}, u32[]{:S(2)}, u32[]{:S(2)}) collective-permute-start(bf16[8,64,512]{2,1,0:T(8,128)(2,1)} %get-tuple-element.43), channel_id=1, source_target_pairs={{0,6},{2,0},{4,2},{6,4},{1,7},{3,1},{5,3},{7,5},{8,14},{10,8},{12,... | collective-permute-start | bytes 1572872 | tf_op jit(solution)/shard_map/ppermute | solution.py:44
  160.2 1.0 copy-done.10
  161.2 3.8 %merge_slots.3 = (bf16[8,64,512]{2,1,0:T(8,128)(2,1)}, bf16[8,64,512]{2,1,0:T(8,128)(2,1)}, bf16[4,64,512]{2,1,0:T(8,128)(2,1)}, bf16[4,64,512]{2,1,0:T(8,128)(2,1)}, bf16[8,64,512]{2,1,0:T(8,128)(2,1)}) custom-call(s32[32]{0:T(128)} %pad_add_fusion.place_ref, bf16[16,64,512]{2,1,0:T(8,128)(2,1)} %bitcast.56, bf16[16,64,512]{2,1,0:T(8,128)(2,1)} %copy-done.10), custom_call_target="tpu_custom_call" | custom-call | tf_op jit(solution)/shard_map/merge_slots/pallas_call | solution.py:345
  164.9 1.6 collective-permute-start.22
  166.5 6.0 %collective-permute-done.29 = bf16[8,64,512]{2,1,0:T(8,128)(2,1)S(1)} collective-permute-done((bf16[8,64,512]{2,1,0:T(8,128)(2,1)}, bf16[8,64,512]{2,1,0:T(8,128)(2,1)S(1)}, u32[]{:S(2)}, u32[]{:S(2)}) %collective-permute-start.29) | collective-permute-done | bytes 524320 | tf_op jit(solution)/shard_map/ppermute | solution.py:44
  172.5 1.0 add_convert_fusion
  173.5 2.4 %collective-permute-start.33 = (bf16[4,64,512]{2,1,0:T(8,128)(2,1)S(1)}, bf16[4,64,512]{2,1,0:T(8,128)(2,1)S(1)}, u32[]{:S(2)}, u32[]{:S(2)}) collective-permute-start(bf16[4,64,512]{2,1,0:T(8,128)(2,1)S(1)} %add_convert_fusion), channel_id=1, source_target_pairs={{0,6},{2,0},{4,2},{6,4},{1,7},{3,1},{5,3},{7,5},{8,14},{10,8},{12,... | collective-permute-start | bytes 786440 | tf_op jit(solution)/shard_map/ppermute | solution.py:44
  176.0 1.0 add_convert_fusion.1
  177.1 5.7 %collective-permute-done.22 = bf16[8,64,512]{2,1,0:T(8,128)(2,1)S(1)} collective-permute-done((bf16[8,64,512]{2,1,0:T(8,128)(2,1)}, bf16[8,64,512]{2,1,0:T(8,128)(2,1)S(1)}, u32[]{:S(2)}, u32[]{:S(2)}) %collective-permute-start.22) | collective-permute-done | bytes 524320 | tf_op jit(solution)/shard_map/ppermute | solution.py:44
  182.8 1.0 add_convert_fusion.2
  183.8 3.4 %collective-permute-start.26 = (bf16[4,64,512]{2,1,0:T(8,128)(2,1)S(1)}, bf16[4,64,512]{2,1,0:T(8,128)(2,1)S(1)}, u32[]{:S(2)}, u32[]{:S(2)}) collective-permute-start(bf16[4,64,512]{2,1,0:T(8,128)(2,1)S(1)} %add_convert_fusion.2), channel_id=1, source_target_pairs={{0,6},{2,0},{4,2},{6,4},{1,7},{3,1},{5,3},{7,5},{8,14},{10,8},{12,... | collective-permute-start | bytes 786440 | tf_op jit(solution)/shard_map/ppermute | solution.py:44
  187.2 1.0 add_convert_fusion.3
  188.3 1.0 collective-permute-done.31
  189.5 2.6 %collective-permute-start.34 = (bf16[2,64,512]{2,1,0:T(8,128)(2,1)S(1)}, bf16[2,64,512]{2,1,0:T(8,128)(2,1)S(1)}, u32[]{:S(2)}, u32[]{:S(2)}) collective-permute-start(bf16[2,64,512]{2,1,0:T(8,128)(2,1)S(1)} %get-tuple-element.62), channel_id=1, source_target_pairs={{0,16},{8,24},{16,0},{24,8},{1,17},{9,25},{17,1},{25,9},{2,18},{10... | collective-permute-start | bytes 393224 | tf_op jit(solution)/shard_map/ppermute | solution.py:44
  193.0 2.0 collective-permute-start.32
  195.4 3.2 %collective-permute-start.27 = (bf16[2,64,512]{2,1,0:T(8,128)(2,1)S(1)}, bf16[2,64,512]{2,1,0:T(8,128)(2,1)S(1)}, u32[]{:S(2)}, u32[]{:S(2)}) collective-permute-start(bf16[2,64,512]{2,1,0:T(8,128)(2,1)S(1)} %get-tuple-element.64), channel_id=1, source_target_pairs={{0,16},{8,24},{16,0},{24,8},{1,17},{9,25},{17,1},{25,9},{2,18},{10... | collective-permute-start | bytes 393224 | tf_op jit(solution)/shard_map/ppermute | solution.py:44
  198.6 3.6 %collective-permute-start.28 = (bf16[2,64,512]{2,1,0:T(8,128)(2,1)S(1)}, bf16[2,64,512]{2,1,0:T(8,128)(2,1)S(1)}, u32[]{:S(2)}, u32[]{:S(2)}) collective-permute-start(bf16[2,64,512]{2,1,0:T(8,128)(2,1)S(1)} %get-tuple-element.65), channel_id=1, source_target_pairs={{0,24},{8,0},{16,8},{24,16},{1,25},{9,1},{17,9},{25,17},{2,26},{10... | collective-permute-start | bytes 393224 | tf_op jit(solution)/shard_map/ppermute | solution.py:44
  202.1 13.2 %collective-permute-done.35 = bf16[2,64,512]{2,1,0:T(8,128)(2,1)S(1)} collective-permute-done((bf16[2,64,512]{2,1,0:T(8,128)(2,1)S(1)}, bf16[2,64,512]{2,1,0:T(8,128)(2,1)S(1)}, u32[]{:S(2)}, u32[]{:S(2)}) %collective-permute-start.35) | collective-permute-done | bytes 131104 | tf_op jit(solution)/shard_map/ppermute | solution.py:44
  216.1 2.0 collective-permute-done.28
  (97 shorter events, 13.8 us)
Async XLA Ops:
  0.6 37.2 %copy-start = (s32[8,32,8,2]{1,3,2,0:T(2,128)S(1)}, s32[8,32,8,2]{1,3,2,0:T(2,128)}, u32[]{:S(2)}) copy-start(s32[8,32,8,2]{1,3,2,0:T(2,128)} %param.16) | copy-start | bytes 49156
  0.6 11.4 %collective-permute-start.2 = (bf16[2,64,512]{2,1,0:T(8,128)(2,1)}, bf16[2,64,512]{2,1,0:T(8,128)(2,1)S(1)}, u32[]{:S(2)}, u32[]{:S(2)}) collective-permute-start(bf16[2,64,512]{2,1,0:T(8,128)(2,1)} %bitcast.69), channel_id=1, source_target_pairs={{0,8},{8,16},{16,24},{24,0},{1,9},{9,17},{17,25},{25,1},{2,10},{10... | collective-permute-start | bytes 393224 | tf_op jit(solution)/shard_map/ppermute | solution.py:44
  4.5 13.9 %collective-permute-start.1 = (bf16[2,64,512]{2,1,0:T(8,128)(2,1)}, bf16[2,64,512]{2,1,0:T(8,128)(2,1)S(1)}, u32[]{:S(2)}, u32[]{:S(2)}) collective-permute-start(bf16[2,64,512]{2,1,0:T(8,128)(2,1)} %bitcast.70), channel_id=1, source_target_pairs={{0,16},{8,24},{16,0},{24,8},{1,17},{9,25},{17,1},{25,9},{2,18},{10... | collective-permute-start | bytes 393224 | tf_op jit(solution)/shard_map/ppermute | solution.py:44
  9.7 13.1 %collective-permute-start = (bf16[2,64,512]{2,1,0:T(8,128)(2,1)}, bf16[2,64,512]{2,1,0:T(8,128)(2,1)S(1)}, u32[]{:S(2)}, u32[]{:S(2)}) collective-permute-start(bf16[2,64,512]{2,1,0:T(8,128)(2,1)} %bitcast.71), channel_id=1, source_target_pairs={{0,24},{8,0},{16,8},{24,16},{1,25},{9,1},{17,9},{25,17},{2,26},{10... | collective-permute-start | bytes 393224 | tf_op jit(solution)/shard_map/ppermute | solution.py:44
  23.8 32.1 %copy-start.7 = (bf16[8,64,512]{2,1,0:T(8,128)(2,1)}, bf16[8,64,512]{2,1,0:T(8,128)(2,1)S(1)}, u32[]{:S(2)}) copy-start(bf16[8,64,512]{2,1,0:T(8,128)(2,1)S(1)} %pad_maximum_fusion.refs_0_) | copy-start | bytes 1572868
  23.8 21.3 %collective-permute-start.5 = (bf16[8,64,512]{2,1,0:T(8,128)(2,1)S(1)}, bf16[8,64,512]{2,1,0:T(8,128)(2,1)S(1)}, u32[]{:S(2)}, u32[]{:S(2)}) collective-permute-start(bf16[8,64,512]{2,1,0:T(8,128)(2,1)S(1)} %pad_maximum_fusion.refs_0_), channel_id=1, source_target_pairs={{0,2},{2,4},{4,6},{6,0},{1,3},{3,5},{5,7},{7,1},{8,10},{10,12},{12... | collective-permute-start | bytes 1572872 | tf_op jit(solution)/shard_map/ppermute | solution.py:44
  25.1 25.2 %collective-permute-start.4 = (bf16[8,64,512]{2,1,0:T(8,128)(2,1)S(1)}, bf16[8,64,512]{2,1,0:T(8,128)(2,1)S(1)}, u32[]{:S(2)}, u32[]{:S(2)}) collective-permute-start(bf16[8,64,512]{2,1,0:T(8,128)(2,1)S(1)} %pad_maximum_fusion.refs_0_), channel_id=1, source_target_pairs={{0,4},{2,6},{4,0},{6,2},{1,5},{3,7},{5,1},{7,3},{8,12},{10,14},{12... | collective-permute-start | bytes 1572872 | tf_op jit(solution)/shard_map/ppermute | solution.py:44
  27.5 22.8 %collective-permute-start.3 = (bf16[8,64,512]{2,1,0:T(8,128)(2,1)S(1)}, bf16[8,64,512]{2,1,0:T(8,128)(2,1)S(1)}, u32[]{:S(2)}, u32[]{:S(2)}) collective-permute-start(bf16[8,64,512]{2,1,0:T(8,128)(2,1)S(1)} %pad_maximum_fusion.refs_0_), channel_id=1, source_target_pairs={{0,6},{2,0},{4,2},{6,4},{1,7},{3,1},{5,3},{7,5},{8,14},{10,8},{12,... | collective-permute-start | bytes 1572872 | tf_op jit(solution)/shard_map/ppermute | solution.py:44
  28.7 7.9 %collective-permute-start.8 = (bf16[2,64,512]{2,1,0:T(8,128)(2,1)}, bf16[2,64,512]{2,1,0:T(8,128)(2,1)S(1)}, u32[]{:S(2)}, u32[]{:S(2)}) collective-permute-start(bf16[2,64,512]{2,1,0:T(8,128)(2,1)} %bitcast.73), channel_id=1, source_target_pairs={{0,8},{8,16},{16,24},{24,0},{1,9},{9,17},{17,25},{25,1},{2,10},{10... | collective-permute-start | bytes 393224 | tf_op jit(solution)/shard_map/ppermute | solution.py:44
  29.6 12.0 %collective-permute-start.7 = (bf16[2,64,512]{2,1,0:T(8,128)(2,1)}, bf16[2,64,512]{2,1,0:T(8,128)(2,1)S(1)}, u32[]{:S(2)}, u32[]{:S(2)}) collective-permute-start(bf16[2,64,512]{2,1,0:T(8,128)(2,1)} %bitcast.74), channel_id=1, source_target_pairs={{0,16},{8,24},{16,0},{24,8},{1,17},{9,25},{17,1},{25,9},{2,18},{10... | collective-permute-start | bytes 393224 | tf_op jit(solution)/shard_map/ppermute | solution.py:44
  36.6 7.2 %collective-permute-start.6 = (bf16[2,64,512]{2,1,0:T(8,128)(2,1)}, bf16[2,64,512]{2,1,0:T(8,128)(2,1)S(1)}, u32[]{:S(2)}, u32[]{:S(2)}) collective-permute-start(bf16[2,64,512]{2,1,0:T(8,128)(2,1)} %bitcast.75), channel_id=1, source_target_pairs={{0,24},{8,0},{16,8},{24,16},{1,25},{9,1},{17,9},{25,17},{2,26},{10... | collective-permute-start | bytes 393224 | tf_op jit(solution)/shard_map/ppermute | solution.py:44
  41.6 12.8 %collective-permute-start.9 = (bf16[8,64,512]{2,1,0:T(8,128)(2,1)S(1)}, bf16[8,64,512]{2,1,0:T(8,128)(2,1)}, u32[]{:S(2)}, u32[]{:S(2)}) collective-permute-start(bf16[8,64,512]{2,1,0:T(8,128)(2,1)S(1)} %pad_maximum_fusion.refs_0_), channel_id=1, source_target_pairs={{0,1},{1,0},{2,3},{3,2},{4,5},{5,4},{6,7},{7,6},{8,9},{9,8},{10,11... | collective-permute-start | bytes 1572872 | tf_op jit(solution)/shard_map/ppermute | solution.py:44
  44.8 39.7 %copy-start.8 = (bf16[8,64,512]{2,1,0:T(8,128)(2,1)}, bf16[8,64,512]{2,1,0:T(8,128)(2,1)S(1)}, u32[]{:S(2)}) copy-start(bf16[8,64,512]{2,1,0:T(8,128)(2,1)S(1)} %pad_maximum_fusion.1.refs_0_) | copy-start | bytes 1572868
  44.8 16.7 %collective-permute-start.13 = (bf16[8,64,512]{2,1,0:T(8,128)(2,1)S(1)}, bf16[8,64,512]{2,1,0:T(8,128)(2,1)S(1)}, u32[]{:S(2)}, u32[]{:S(2)}) collective-permute-start(bf16[8,64,512]{2,1,0:T(8,128)(2,1)S(1)} %pad_maximum_fusion.1.refs_0_), channel_id=1, source_target_pairs={{0,4},{2,6},{4,0},{6,2},{1,5},{3,7},{5,1},{7,3},{8,12},{10,14},{12... | collective-permute-start | bytes 1572872 | tf_op jit(solution)/shard_map/ppermute | solution.py:44
  45.1 10.7 %copy-start.13 = (bf16[8,64,512]{2,1,0:T(8,128)(2,1)}, bf16[8,64,512]{2,1,0:T(8,128)(2,1)S(1)}, u32[]{:S(2)}) copy-start(bf16[8,64,512]{2,1,0:T(8,128)(2,1)S(1)} %collective-permute-done.5.refs_3_) | copy-start | bytes 1572868
  50.3 5.5 %copy-start.14 = (bf16[8,64,512]{2,1,0:T(8,128)(2,1)}, bf16[8,64,512]{2,1,0:T(8,128)(2,1)S(1)}, u32[]{:S(2)}) copy-start(bf16[8,64,512]{2,1,0:T(8,128)(2,1)S(1)} %collective-permute-done.4.refs_2_) | copy-start | bytes 1572868
  50.3 5.5 %copy-start.15 = (bf16[8,64,512]{2,1,0:T(8,128)(2,1)}, bf16[8,64,512]{2,1,0:T(8,128)(2,1)S(1)}, u32[]{:S(2)}) copy-start(bf16[8,64,512]{2,1,0:T(8,128)(2,1)S(1)} %collective-permute-done.3.refs_1_) | copy-start | bytes 1572868
  50.3 4.1 %collective-permute-start.10 = (bf16[8,64,512]{2,1,0:T(8,128)(2,1)S(1)}, bf16[8,64,512]{2,1,0:T(8,128)(2,1)}, u32[]{:S(2)}, u32[]{:S(2)}) collective-permute-start(bf16[8,64,512]{2,1,0:T(8,128)(2,1)S(1)} %collective-permute-done.3.refs_1_), channel_id=1, source_target_pairs={{0,1},{1,0},{2,3},{3,2},{4,5},{5,4},{6,7},{7,6},{8,9},{9,8},{10,11... | collective-permute-start | bytes 1572872 | tf_op jit(solution)/shard_map/ppermute | solution.py:44
  52.7 2.4 %collective-permute-start.11 = (bf16[8,64,512]{2,1,0:T(8,128)(2,1)S(1)}, bf16[8,64,512]{2,1,0:T(8,128)(2,1)}, u32[]{:S(2)}, u32[]{:S(2)}) collective-permute-start(bf16[8,64,512]{2,1,0:T(8,128)(2,1)S(1)} %collective-permute-done.4.refs_2_), channel_id=1, source_target_pairs={{0,1},{1,0},{2,3},{3,2},{4,5},{5,4},{6,7},{7,6},{8,9},{9,8},{10,11... | collective-permute-start | bytes 1572872 | tf_op jit(solution)/shard_map/ppermute | solution.py:44
  52.8 3.1 %collective-permute-start.12 = (bf16[8,64,512]{2,1,0:T(8,128)(2,1)S(1)}, bf16[8,64,512]{2,1,0:T(8,128)(2,1)}, u32[]{:S(2)}, u32[]{:S(2)}) collective-permute-start(bf16[8,64,512]{2,1,0:T(8,128)(2,1)S(1)} %collective-permute-done.5.refs_3_), channel_id=1, source_target_pairs={{0,1},{1,0},{2,3},{3,2},{4,5},{5,4},{6,7},{7,6},{8,9},{9,8},{10,11... | collective-permute-start | bytes 1572872 | tf_op jit(solution)/shard_map/ppermute | solution.py:44
  61.5 22.9 %copy-start.16 = (bf16[8,64,512]{2,1,0:T(8,128)(2,1)}, bf16[8,64,512]{2,1,0:T(8,128)(2,1)S(1)}, u32[]{:S(2)}) copy-start(bf16[8,64,512]{2,1,0:T(8,128)(2,1)S(1)} %collective-permute-done.13.refs_2_) | copy-start | bytes 1572868
  61.5 26.9 %all-to-all-start = ((bf16[8,128,512]{2,1,0:T(8,128)(2,1)}), bf16[8,128,512]{2,1,0:T(8,128)(2,1)S(1)}, u32[]{:S(2)}, u32[]{:S(2)}) async-start(bf16[8,128,512]{2,1,0:T(8,128)(2,1)} %bitcast.59), calls=%async_computation | async-start | bytes 2097152 | tf_op jit(solution)/shard_map/all_to_all | solution.py:431
  65.7 27.9 %copy-start.23 = (bf16[1,128,512]{2,1,0:T(8,128)(2,1)S(1)}, bf16[1,128,512]{2,1,0:T(8,128)(2,1)}, u32[]{:S(2)}) copy-start(bf16[1,128,512]{2,1,0:T(8,128)(2,1)} %param.9) | copy-start | bytes 393220
  65.7 28.6 %copy-start.24 = (bf16[1,128,512]{2,1,0:T(8,128)(2,1)S(1)}, bf16[1,128,512]{2,1,0:T(8,128)(2,1)}, u32[]{:S(2)}) copy-start(bf16[1,128,512]{2,1,0:T(8,128)(2,1)} %param.15) | copy-start | bytes 393220
  65.7 29.4 %copy-start.5 = (bf16[512,512]{1,0:T(8,128)(2,1)S(1)}, bf16[512,512]{1,0:T(8,128)(2,1)}, u32[]{:S(2)}) copy-start(bf16[512,512]{1,0:T(8,128)(2,1)} %wq_ref.1) | copy-start | bytes 1572868
  65.7 30.4 %copy-start.6 = (bf16[512,512]{1,0:T(8,128)(2,1)S(1)}, bf16[512,512]{1,0:T(8,128)(2,1)}, u32[]{:S(2)}) copy-start(bf16[512,512]{1,0:T(8,128)(2,1)} %wk_ref.1) | copy-start | bytes 1572868
  65.8 13.1 %collective-permute-start.15 = (bf16[8,64,512]{2,1,0:T(8,128)(2,1)S(1)}, bf16[8,64,512]{2,1,0:T(8,128)(2,1)S(1)}, u32[]{:S(2)}, u32[]{:S(2)}) collective-permute-start(bf16[8,64,512]{2,1,0:T(8,128)(2,1)S(1)} %pad_maximum_fusion.1.refs_0_), channel_id=1, source_target_pairs={{0,2},{2,4},{4,6},{6,0},{1,3},{3,5},{5,7},{7,1},{8,10},{10,12},{12... | collective-permute-start | bytes 1572872 | tf_op jit(solution)/shard_map/ppermute | solution.py:44
  67.3 14.1 %collective-permute-start.14 = (bf16[8,64,512]{2,1,0:T(8,128)(2,1)S(1)}, bf16[8,64,512]{2,1,0:T(8,128)(2,1)S(1)}, u32[]{:S(2)}, u32[]{:S(2)}) collective-permute-start(bf16[8,64,512]{2,1,0:T(8,128)(2,1)S(1)} %pad_maximum_fusion.1.refs_0_), channel_id=1, source_target_pairs={{0,6},{2,0},{4,2},{6,4},{1,7},{3,1},{5,3},{7,5},{8,14},{10,8},{12,... | collective-permute-start | bytes 1572872 | tf_op jit(solution)/shard_map/ppermute | solution.py:44
  68.5 13.4 %collective-permute-start.16 = (bf16[8,64,512]{2,1,0:T(8,128)(2,1)S(1)}, bf16[8,64,512]{2,1,0:T(8,128)(2,1)S(1)}, u32[]{:S(2)}, u32[]{:S(2)}) collective-permute-start(bf16[8,64,512]{2,1,0:T(8,128)(2,1)S(1)} %pad_maximum_fusion.1.refs_0_), channel_id=1, source_target_pairs={{0,1},{1,0},{2,3},{3,2},{4,5},{5,4},{6,7},{7,6},{8,9},{9,8},{10,11... | collective-permute-start | bytes 1572872 | tf_op jit(solution)/shard_map/ppermute | solution.py:44
  78.8 5.6 %copy-start.17 = (bf16[8,64,512]{2,1,0:T(8,128)(2,1)}, bf16[8,64,512]{2,1,0:T(8,128)(2,1)S(1)}, u32[]{:S(2)}) copy-start(bf16[8,64,512]{2,1,0:T(8,128)(2,1)S(1)} %collective-permute-done.15.refs_3_) | copy-start | bytes 1572868
  78.9 4.1 %collective-permute-start.19 = (bf16[8,64,512]{2,1,0:T(8,128)(2,1)S(1)}, bf16[8,64,512]{2,1,0:T(8,128)(2,1)S(1)}, u32[]{:S(2)}, u32[]{:S(2)}) collective-permute-start(bf16[8,64,512]{2,1,0:T(8,128)(2,1)S(1)} %collective-permute-done.15.refs_3_), channel_id=1, source_target_pairs={{0,1},{1,0},{2,3},{3,2},{4,5},{5,4},{6,7},{7,6},{8,9},{9,8},{10,11... | collective-permute-start | bytes 1572872 | tf_op jit(solution)/shard_map/ppermute | solution.py:44
  81.4 3.0 %copy-start.18 = (bf16[8,64,512]{2,1,0:T(8,128)(2,1)}, bf16[8,64,512]{2,1,0:T(8,128)(2,1)S(1)}, u32[]{:S(2)}) copy-start(bf16[8,64,512]{2,1,0:T(8,128)(2,1)S(1)} %collective-permute-done.14.refs_1_) | copy-start | bytes 1572868
  81.4 2.3 %collective-permute-start.17 = (bf16[8,64,512]{2,1,0:T(8,128)(2,1)S(1)}, bf16[8,64,512]{2,1,0:T(8,128)(2,1)S(1)}, u32[]{:S(2)}, u32[]{:S(2)}) collective-permute-start(bf16[8,64,512]{2,1,0:T(8,128)(2,1)S(1)} %collective-permute-done.14.refs_1_), channel_id=1, source_target_pairs={{0,1},{1,0},{2,3},{3,2},{4,5},{5,4},{6,7},{7,6},{8,9},{9,8},{10,11... | collective-permute-start | bytes 1572872 | tf_op jit(solution)/shard_map/ppermute | solution.py:44
  81.7 2.7 %collective-permute-start.18 = (bf16[8,64,512]{2,1,0:T(8,128)(2,1)S(1)}, bf16[8,64,512]{2,1,0:T(8,128)(2,1)S(1)}, u32[]{:S(2)}, u32[]{:S(2)}) collective-permute-start(bf16[8,64,512]{2,1,0:T(8,128)(2,1)S(1)} %collective-permute-done.13.refs_2_), channel_id=1, source_target_pairs={{0,1},{1,0},{2,3},{3,2},{4,5},{5,4},{6,7},{7,6},{8,9},{9,8},{10,11... | collective-permute-start | bytes 1572872 | tf_op jit(solution)/shard_map/ppermute | solution.py:44
  81.9 2.5 %copy-start.19 = (bf16[8,64,512]{2,1,0:T(8,128)(2,1)}, bf16[8,64,512]{2,1,0:T(8,128)(2,1)S(1)}, u32[]{:S(2)}) copy-start(bf16[8,64,512]{2,1,0:T(8,128)(2,1)S(1)} %collective-permute-done.16.refs_4_) | copy-start | bytes 1572868
  82.9 1.5 copy-start.20
  84.5 0.8 copy-start.22
  88.4 12.2 %copy-start.2 = (bf16[8,128,512]{2,1,0:T(8,128)(2,1)}, bf16[8,128,512]{2,1,0:T(8,128)(2,1)S(1)}, u32[]{:S(2)}) copy-start(bf16[8,128,512]{2,1,0:T(8,128)(2,1)S(1)} %all-to-all-done.key_ref) | copy-start | bytes 3145732
  88.4 20.3 %all-to-all-start.1 = ((bf16[8,128,512]{2,1,0:T(8,128)(2,1)}), bf16[8,128,512]{2,1,0:T(8,128)(2,1)S(1)}, u32[]{:S(2)}, u32[]{:S(2)}) async-start(bf16[8,128,512]{2,1,0:T(8,128)(2,1)} %bitcast.60), calls=%async_computation.1 | async-start | bytes 2097152 | tf_op jit(solution)/shard_map/all_to_all | solution.py:431
  108.8 1.0 copy-start.1
  117.9 18.7 %all-to-all-start.3 = ((bf16[8,128,512]{2,1,0:T(8,128)(2,1)}), bf16[8,128,512]{2,1,0:T(8,128)(2,1)S(1)}, u32[]{:S(2)}, u32[]{:S(2)}) async-start(bf16[8,128,512]{2,1,0:T(8,128)(2,1)} %get-tuple-element.41), calls=%async_computation.3 | async-start | bytes 2097152 | tf_op jit(solution)/shard_map/all_to_all | solution.py:431
  136.6 8.4 %copy-start.4 = (bf16[8,128,512]{2,1,0:T(8,128)(2,1)}, bf16[8,128,512]{2,1,0:T(8,128)(2,1)S(1)}, u32[]{:S(2)}) copy-start(bf16[8,128,512]{2,1,0:T(8,128)(2,1)S(1)} %all-to-all-done.3) | copy-start | bytes 3145732
  136.6 18.2 %all-to-all-start.2 = ((bf16[8,128,512]{2,1,0:T(8,128)(2,1)}), bf16[8,128,512]{2,1,0:T(8,128)(2,1)S(1)}, u32[]{:S(2)}, u32[]{:S(2)}) async-start(bf16[8,128,512]{2,1,0:T(8,128)(2,1)} %get-tuple-element.40), calls=%async_computation.2 | async-start | bytes 2097152 | tf_op jit(solution)/shard_map/all_to_all | solution.py:431
  140.9 4.2 %collective-permute-start.20 = (bf16[16,64,512]{2,1,0:T(8,128)(2,1)S(1)}, bf16[16,64,512]{2,1,0:T(8,128)(2,1)S(1)}, u32[]{:S(2)}, u32[]{:S(2)}) collective-permute-start(bf16[16,64,512]{2,1,0:T(8,128)(2,1)S(1)} %bitcast.57), channel_id=1, source_target_pairs={{0,1},{1,0},{2,3},{3,2},{4,5},{5,4},{6,7},{7,6},{8,9},{9,8},{10,11... | collective-permute-start | bytes 3145736 | tf_op jit(solution)/shard_map/ppermute | solution.py:44
  145.0 1.0 copy-start.9
  149.8 39.6 %copy-start.11 = (bf16[8,64,512]{2,1,0:T(8,128)(2,1)S(1)}, bf16[8,64,512]{2,1,0:T(8,128)(2,1)}, u32[]{:S(2)}) copy-start(bf16[8,64,512]{2,1,0:T(8,128)(2,1)} %get-tuple-element.53) | copy-start | bytes 1572868
  154.9 5.3 %copy-start.3 = (bf16[8,128,512]{2,1,0:T(8,128)(2,1)}, bf16[8,128,512]{2,1,0:T(8,128)(2,1)S(1)}, u32[]{:S(2)}) copy-start(bf16[8,128,512]{2,1,0:T(8,128)(2,1)S(1)} %all-to-all-done.2) | copy-start | bytes 3145732
  154.9 5.3 %collective-permute-start.21 = (bf16[16,64,512]{2,1,0:T(8,128)(2,1)S(1)}, bf16[16,64,512]{2,1,0:T(8,128)(2,1)S(1)}, u32[]{:S(2)}, u32[]{:S(2)}) collective-permute-start(bf16[16,64,512]{2,1,0:T(8,128)(2,1)S(1)} %bitcast.55), channel_id=1, source_target_pairs={{0,1},{1,0},{2,3},{3,2},{4,5},{5,4},{6,7},{7,6},{8,9},{9,8},{10,11... | collective-permute-start | bytes 3145736 | tf_op jit(solution)/shard_map/ppermute | solution.py:44
  157.5 15.0 %collective-permute-start.29 = (bf16[8,64,512]{2,1,0:T(8,128)(2,1)}, bf16[8,64,512]{2,1,0:T(8,128)(2,1)S(1)}, u32[]{:S(2)}, u32[]{:S(2)}) collective-permute-start(bf16[8,64,512]{2,1,0:T(8,128)(2,1)} %get-tuple-element.42), channel_id=1, source_target_pairs={{0,2},{2,4},{4,6},{6,0},{1,3},{3,5},{5,7},{7,1},{8,10},{10,12},{12... | collective-permute-start | bytes 1572872 | tf_op jit(solution)/shard_map/ppermute | solution.py:44
  157.8 14.7 %collective-permute-start.30 = (bf16[8,64,512]{2,1,0:T(8,128)(2,1)}, bf16[8,64,512]{2,1,0:T(8,128)(2,1)S(1)}, u32[]{:S(2)}, u32[]{:S(2)}) collective-permute-start(bf16[8,64,512]{2,1,0:T(8,128)(2,1)} %get-tuple-element.43), channel_id=1, source_target_pairs={{0,6},{2,0},{4,2},{6,4},{1,7},{3,1},{5,3},{7,5},{8,14},{10,8},{12,... | collective-permute-start | bytes 1572872 | tf_op jit(solution)/shard_map/ppermute | solution.py:44
  160.2 1.0 copy-start.10
  164.9 30.3 %copy-start.12 = (bf16[8,64,512]{2,1,0:T(8,128)(2,1)S(1)}, bf16[8,64,512]{2,1,0:T(8,128)(2,1)}, u32[]{:S(2)}) copy-start(bf16[8,64,512]{2,1,0:T(8,128)(2,1)} %get-tuple-element.48) | copy-start | bytes 1572868
  164.9 17.8 %collective-permute-start.22 = (bf16[8,64,512]{2,1,0:T(8,128)(2,1)}, bf16[8,64,512]{2,1,0:T(8,128)(2,1)S(1)}, u32[]{:S(2)}, u32[]{:S(2)}) collective-permute-start(bf16[8,64,512]{2,1,0:T(8,128)(2,1)} %get-tuple-element.49), channel_id=1, source_target_pairs={{0,6},{2,0},{4,2},{6,4},{1,7},{3,1},{5,3},{7,5},{8,14},{10,8},{12,... | collective-permute-start | bytes 1572872 | tf_op jit(solution)/shard_map/ppermute | solution.py:44
  166.5 20.7 %collective-permute-start.23 = (bf16[8,64,512]{2,1,0:T(8,128)(2,1)}, bf16[8,64,512]{2,1,0:T(8,128)(2,1)S(1)}, u32[]{:S(2)}, u32[]{:S(2)}) collective-permute-start(bf16[8,64,512]{2,1,0:T(8,128)(2,1)} %get-tuple-element.51), channel_id=1, source_target_pairs={{0,2},{2,4},{4,6},{6,0},{1,3},{3,5},{5,7},{7,1},{8,10},{10,12},{12... | collective-permute-start | bytes 1572872 | tf_op jit(solution)/shard_map/ppermute | solution.py:44
  173.5 14.8 %collective-permute-start.33 = (bf16[4,64,512]{2,1,0:T(8,128)(2,1)S(1)}, bf16[4,64,512]{2,1,0:T(8,128)(2,1)S(1)}, u32[]{:S(2)}, u32[]{:S(2)}) collective-permute-start(bf16[4,64,512]{2,1,0:T(8,128)(2,1)S(1)} %add_convert_fusion), channel_id=1, source_target_pairs={{0,6},{2,0},{4,2},{6,4},{1,7},{3,1},{5,3},{7,5},{8,14},{10,8},{12,... | collective-permute-start | bytes 786440 | tf_op jit(solution)/shard_map/ppermute | solution.py:44
  177.0 12.4 %collective-permute-start.31 = (bf16[4,64,512]{2,1,0:T(8,128)(2,1)S(1)}, bf16[4,64,512]{2,1,0:T(8,128)(2,1)S(1)}, u32[]{:S(2)}, u32[]{:S(2)}) collective-permute-start(bf16[4,64,512]{2,1,0:T(8,128)(2,1)S(1)} %add_convert_fusion.1), channel_id=1, source_target_pairs={{0,2},{2,4},{4,6},{6,0},{1,3},{3,5},{5,7},{7,1},{8,10},{10,12},{12... | collective-permute-start | bytes 786440 | tf_op jit(solution)/shard_map/ppermute | solution.py:44
  183.8 11.2 %collective-permute-start.26 = (bf16[4,64,512]{2,1,0:T(8,128)(2,1)S(1)}, bf16[4,64,512]{2,1,0:T(8,128)(2,1)S(1)}, u32[]{:S(2)}, u32[]{:S(2)}) collective-permute-start(bf16[4,64,512]{2,1,0:T(8,128)(2,1)S(1)} %add_convert_fusion.2), channel_id=1, source_target_pairs={{0,6},{2,0},{4,2},{6,4},{1,7},{3,1},{5,3},{7,5},{8,14},{10,8},{12,... | collective-permute-start | bytes 786440 | tf_op jit(solution)/shard_map/ppermute | solution.py:44
  188.2 7.0 %collective-permute-start.24 = (bf16[4,64,512]{2,1,0:T(8,128)(2,1)S(1)}, bf16[4,64,512]{2,1,0:T(8,128)(2,1)S(1)}, u32[]{:S(2)}, u32[]{:S(2)}) collective-permute-start(bf16[4,64,512]{2,1,0:T(8,128)(2,1)S(1)} %add_convert_fusion.3), channel_id=1, source_target_pairs={{0,2},{2,4},{4,6},{6,0},{1,3},{3,5},{5,7},{7,1},{8,10},{10,12},{12... | collective-permute-start | bytes 786440 | tf_op jit(solution)/shard_map/ppermute | solution.py:44
  189.5 12.6 %collective-permute-start.34 = (bf16[2,64,512]{2,1,0:T(8,128)(2,1)S(1)}, bf16[2,64,512]{2,1,0:T(8,128)(2,1)S(1)}, u32[]{:S(2)}, u32[]{:S(2)}) collective-permute-start(bf16[2,64,512]{2,1,0:T(8,128)(2,1)S(1)} %get-tuple-element.62), channel_id=1, source_target_pairs={{0,16},{8,24},{16,0},{24,8},{1,17},{9,25},{17,1},{25,9},{2,18},{10... | collective-permute-start | bytes 393224 | tf_op jit(solution)/shard_map/ppermute | solution.py:44
  192.1 23.2 %collective-permute-start.35 = (bf16[2,64,512]{2,1,0:T(8,128)(2,1)S(1)}, bf16[2,64,512]{2,1,0:T(8,128)(2,1)S(1)}, u32[]{:S(2)}, u32[]{:S(2)}) collective-permute-start(bf16[2,64,512]{2,1,0:T(8,128)(2,1)S(1)} %get-tuple-element.63), channel_id=1, source_target_pairs={{0,24},{8,0},{16,8},{24,16},{1,25},{9,1},{17,9},{25,17},{2,26},{10... | collective-permute-start | bytes 393224 | tf_op jit(solution)/shard_map/ppermute | solution.py:44
  193.0 22.3 %collective-permute-start.32 = (bf16[2,64,512]{2,1,0:T(8,128)(2,1)S(1)}, bf16[2,64,512]{2,1,0:T(8,128)(2,1)S(1)}, u32[]{:S(2)}, u32[]{:S(2)}) collective-permute-start(bf16[2,64,512]{2,1,0:T(8,128)(2,1)S(1)} %get-tuple-element.66), channel_id=1, source_target_pairs={{0,8},{8,16},{16,24},{24,0},{1,9},{9,17},{17,25},{25,1},{2,10},{10... | collective-permute-start | bytes 393224 | tf_op jit(solution)/shard_map/ppermute | solution.py:44
  195.4 20.7 %collective-permute-start.27 = (bf16[2,64,512]{2,1,0:T(8,128)(2,1)S(1)}, bf16[2,64,512]{2,1,0:T(8,128)(2,1)S(1)}, u32[]{:S(2)}, u32[]{:S(2)}) collective-permute-start(bf16[2,64,512]{2,1,0:T(8,128)(2,1)S(1)} %get-tuple-element.64), channel_id=1, source_target_pairs={{0,16},{8,24},{16,0},{24,8},{1,17},{9,25},{17,1},{25,9},{2,18},{10... | collective-permute-start | bytes 393224 | tf_op jit(solution)/shard_map/ppermute | solution.py:44
  198.6 19.6 %collective-permute-start.28 = (bf16[2,64,512]{2,1,0:T(8,128)(2,1)S(1)}, bf16[2,64,512]{2,1,0:T(8,128)(2,1)S(1)}, u32[]{:S(2)}, u32[]{:S(2)}) collective-permute-start(bf16[2,64,512]{2,1,0:T(8,128)(2,1)S(1)} %get-tuple-element.65), channel_id=1, source_target_pairs={{0,24},{8,0},{16,8},{24,16},{1,25},{9,1},{17,9},{25,17},{2,26},{10... | collective-permute-start | bytes 393224 | tf_op jit(solution)/shard_map/ppermute | solution.py:44
  202.1 16.0 %collective-permute-start.25 = (bf16[2,64,512]{2,1,0:T(8,128)(2,1)S(1)}, bf16[2,64,512]{2,1,0:T(8,128)(2,1)S(1)}, u32[]{:S(2)}, u32[]{:S(2)}) collective-permute-start(bf16[2,64,512]{2,1,0:T(8,128)(2,1)S(1)} %get-tuple-element.67), channel_id=1, source_target_pairs={{0,8},{8,16},{16,24},{24,0},{1,9},{9,17},{17,25},{25,1},{2,10},{10... | collective-permute-start | bytes 393224 | tf_op jit(solution)/shard_map/ppermute | solution.py:44
  (1 other events, 0.8 us)
where the time goes:
time: 220 us; the launch traced here: 219 us
  starting transfers between devices  81.3 us (37%)
  waiting for transfers between devices  75.9 us (35%)
  Pallas kernels  40 us (18%)
  local copies, waits for them, and re-layouts  11.2 us (5%)
  other arithmetic  9.53 us (4%)
    ppermute x36, waiting for transfers between devices, shift(): lax.ppermute(value, axis, [(i, (i + step) % size) for i in range(size)])  66.6 us
    ppermute x36, starting transfers between devices, shift(): lax.ppermute(value, axis, [(i, (i + step) % size) for i in range(size)])  63.3 us
    all_to_all x4, starting transfers between devices, exchange(): lax.all_to_all(chosen.reshape(FRAMES, SLOTS * TILE, WIDTH), TM, split_axi...  18 us
    pallas_call x1, Pallas kernels, attend_back(): pl.pallas_call(back_kernel, grid=(FRAMES,), out_shape=(jax.ShapeDtypeStru...  10.6 us
    unnamed x57, local copies, waits for them, and re-layouts  9.69 us
    all_to_all x4, waiting for transfers between devices, exchange(): lax.all_to_all(chosen.reshape(FRAMES, SLOTS * TILE, WIDTH), TM, split_axi...  9.37 us
    pallas_call x1, Pallas kernels, pool_frames(): pl.pallas_call(pool_kernel, out_shape=(jax.ShapeDtypeStruct((ROWS, WIDTH)...  8.17 us
    pallas_call x2, Pallas kernels, merge_slots(): pl.pallas_call(merge_kernel, out_shape=tuple((jax.ShapeDtypeStruct((n, TI...  7.53 us
  transfers between devices with their start and end apart: 40, of which 22 were waited for; matrix products, arithmetic and copies ran while one was open for 7% of the time, Pallas kernels for 15%

commit v1 on v0

--- a/solution.py
+++ b/solution.py
@@ -17,14 +17,17 @@
 PAIRS = 4
 ROWS = 128
 SCALE = 0.125
-PIECES = 8
 TM = ("y", "zl")
 SPACE = ("zh", "x", "c")
-VMEM_LIMIT = 56 * 1024 * 1024
-
-
-def params():
-    return pltpu.CompilerParams(vmem_limit_bytes=VMEM_LIMIT)
+VMEM_LIMIT = 63 * 1024 * 1024
+
+
+def params(size=VMEM_LIMIT):
+    return pltpu.CompilerParams(vmem_limit_bytes=size)
+
+
+def cost(micros):
+    return pl.CostEstimate(flops=micros * 1000000000, bytes_accessed=0, transcendentals=0)
 
 
 def whole():
@@ -65,11 +68,11 @@
     rows_k = lax.optimization_barrier(tuple(rows_k) + (column_v,))[:3]
     pieces_k = [column_k, *rows_k]
     pieces_v = [column_v, *rows_v]
-    return pieces_k + swap(pieces_k), pieces_v + swap(pieces_v), rows_v[1]
+    return pieces_k + swap(pieces_k), pieces_v + swap(pieces_v)
 
 
 def select_kernel(piece_ref, row_ref, *refs):
-    pieces, out_ref, sems = refs[:PIECES], refs[PIECES], refs[PIECES + 1]
+    pieces, out_ref, sems = refs[:-2], refs[-2], refs[-1]
 
     @pl.loop(0, FRAMES * SLOTS)
     def _(slot):
@@ -90,14 +93,15 @@
         ).wait()
 
 
-def select_tiles(piece_ids, piece_rows, pieces):
+def select_tiles(piece_ids, piece_rows, pieces, micros=0):
     return pl.pallas_call(
         select_kernel,
         out_shape=jax.ShapeDtypeStruct((FRAMES * SLOTS, TILE, WIDTH), jnp.bfloat16),
-        in_specs=[smem(), smem()] + [hbm()] * PIECES,
+        in_specs=[smem(), smem()] + [hbm()] * len(pieces),
         out_specs=whole(),
         scratch_shapes=[pltpu.SemaphoreType.DMA((FRAMES * SLOTS,))],
-        compiler_params=params(),
+        compiler_params=params(6 * 1024 * 1024),
+        cost_estimate=cost(micros),
         name="select_tiles",
     )(piece_ids, piece_rows, *pieces)
 
@@ -126,14 +130,19 @@
     return lax.dot_general(a, b, (((1,), (1,)), ((), ())), preferred_element_type=jnp.float32)
 
 
-def weights_kernel(count_ref, query_ref, key_ref, weight_ref, narrow_ref):
+def weights_kernel(count_ref, query_ref, key_ref, weight_ref, narrow_ref, turned):
     frame = pl.program_id(0)
+
+    @pl.when(frame == 0)
+    def _():
+        turned[...] = query_ref[...].T
+
     limit = count_ref[frame] * TILE
     rows = lax.broadcasted_iota(jnp.int32, (ROWS, 2 * ROWS), 0)
     live = rows < limit
     for pair in range(PAIRS):
         lanes = slice(pair * 128, pair * 128 + 128)
-        scores = dot_nn(key_ref[0, :, lanes], split_heads(query_ref[lanes, :])) * SCALE
+        scores = dot_nn(key_ref[0, :, lanes], split_heads(turned[lanes, :])) * SCALE
         scores = jnp.where(live, scores, -jnp.inf)
         raised = jnp.exp(scores - jnp.max(scores, axis=0, keepdims=True))
         weights = raised / jnp.sum(raised, axis=0, keepdims=True)
@@ -141,7 +150,7 @@
         narrow_ref[0, pair] = weights.astype(jnp.bfloat16)
 
 
-def attend_weights(counts, query_t, keys):
+def attend_weights(counts, queries, keys):
     return pl.pallas_call(
         weights_kernel,
         grid=(FRAMES,),
@@ -151,13 +160,14 @@
         ),
         in_specs=[
             smem(),
-            pl.BlockSpec((WIDTH, ROWS), lambda f: (0, 0)),
+            pl.BlockSpec((ROWS, WIDTH), lambda f: (0, 0)),
             pl.BlockSpec((1, ROWS, WIDTH), lambda f: (f, 0, 0)),
         ],
         out_specs=(pl.BlockSpec((1, PAIRS, ROWS, 2 * ROWS), lambda f: (f, 0, 0, 0)),) * 2,
+        scratch_shapes=[pltpu.VMEM((WIDTH, ROWS), jnp.bfloat16)],
         compiler_params=params(),
         name="attend_weights",
-    )(counts, query_t, keys)
+    )(counts, queries, keys)
 
 
 def pool_kernel(
@@ -167,9 +177,6 @@
     wq_ref,
     wk_ref,
     wv_ref,
-    wqt_ref,
-    wkt_ref,
-    wvt_ref,
     go_ref,
     mixed_ref,
     gt_ref,
@@ -189,13 +196,14 @@
             both = dot_tn(value_ref[frame, :, lanes], weight_ref[frame, pair])
             traj[lanes, frame * ROWS : (frame + 1) * ROWS] = join_heads(both).astype(jnp.bfloat16)
     own = pl.ds(pl.multiple_of(frame_ref[0] * ROWS, ROWS), ROWS)
-    pooled_q[...] = dot_nn(wqt_ref[...], traj[:, own])
-    pooled_k[...] = dot_nn(wkt_ref[...], traj[...])
-    pooled_v[...] = dot_nn(wvt_ref[...], traj[...])
+    pooled_q[...] = dot_tn(wq_ref[...], traj[:, own])
+    pooled_k[...] = dot_tn(wk_ref[...], traj[...])
+    pooled_v[...] = dot_tn(wv_ref[...], traj[...])
+    upstream_t = go_ref[...].astype(jnp.float32).T
     for head in range(HEADS):
         rows = slice(head * HEAD, (head + 1) * HEAD)
         query = pooled_q[rows, :]
-        upstream = go_ref[rows, :].astype(jnp.float32)
+        upstream = upstream_t[rows, :]
         columns = [slice(f * ROWS, (f + 1) * ROWS) for f in range(FRAMES)]
         logits = jnp.concatenate(
             [
@@ -238,7 +246,7 @@
             ).astype(jnp.bfloat16)
 
 
-def pool_frames(frame_now, weights, values, w_query, w_key, w_value, upstream_t):
+def pool_frames(frame_now, weights, values, w_query, w_key, w_value, upstream):
     wide = (WIDTH, FRAMES * ROWS)
     return pl.pallas_call(
         pool_kernel,
@@ -247,7 +255,7 @@
             jax.ShapeDtypeStruct((FRAMES, WIDTH, ROWS), jnp.bfloat16),
             jax.ShapeDtypeStruct((FRAMES, ROWS, WIDTH), jnp.bfloat16),
         ),
-        in_specs=[smem()] + [whole()] * 9,
+        in_specs=[smem()] + [whole()] * 6,
         out_specs=(whole(), whole(), whole()),
         scratch_shapes=[
             pltpu.VMEM(wide, jnp.bfloat16),
@@ -268,19 +276,17 @@
         w_query,
         w_key,
         w_value,
-        w_query.T,
-        w_key.T,
-        w_value.T,
-        upstream_t,
+        upstream,
     )
 
 
-def back_kernel(query_ref, key_ref, value_ref, weight_ref, gt_ref, gq_ref, dk_ref, total):
+def back_kernel(query_ref, key_ref, value_ref, weight_ref, gt_ref, gq_ref, dk_ref, turned, total):
     frame = pl.program_id(0)
 
     @pl.when(frame == 0)
     def _():
         total[...] = jnp.zeros_like(total)
+        turned[...] = query_ref[...].T
 
     for pair in range(PAIRS):
         lanes = slice(pair * 128, pair * 128 + 128)
@@ -288,7 +294,7 @@
         grad_w = dot_nn(value_ref[0, :, lanes], split_heads(gt_ref[0, lanes, :]))
         inner = jnp.sum(weight * grad_w, axis=0, keepdims=True)
         grad_s = (weight * (grad_w - inner) * SCALE).astype(jnp.bfloat16)
-        dk_ref[0, :, lanes] = dot_nt(grad_s, split_heads(query_ref[lanes, :])).astype(jnp.bfloat16)
+        dk_ref[0, :, lanes] = dot_nt(grad_s, split_heads(turned[lanes, :])).astype(jnp.bfloat16)
         total[lanes, :] += join_heads(dot_tn(key_ref[0, :, lanes], grad_s))
 
     @pl.when(frame == FRAMES - 1)
@@ -296,9 +302,9 @@
         gq_ref[...] = total[...].T.astype(jnp.bfloat16)
 
 
-def attend_back(query_t, keys, values, weights, grad_traj):
+def attend_back(queries, keys, values, weights, grad_traj):
     by_frame = pl.BlockSpec((1, ROWS, WIDTH), lambda f: (f, 0, 0))
-    fixed = pl.BlockSpec((WIDTH, ROWS), lambda f: (0, 0))
+    fixed = pl.BlockSpec((ROWS, WIDTH), lambda f: (0, 0))
     return pl.pallas_call(
         back_kernel,
         grid=(FRAMES,),
@@ -313,11 +319,14 @@
             pl.BlockSpec((1, PAIRS, ROWS, 2 * ROWS), lambda f: (f, 0, 0, 0)),
             pl.BlockSpec((1, WIDTH, ROWS), lambda f: (f, 0, 0)),
         ],
-        out_specs=(pl.BlockSpec((ROWS, WIDTH), lambda f: (0, 0)), by_frame),
-        scratch_shapes=[pltpu.VMEM((WIDTH, ROWS), jnp.float32)],
+        out_specs=(fixed, by_frame),
+        scratch_shapes=[
+            pltpu.VMEM((WIDTH, ROWS), jnp.bfloat16),
+            pltpu.VMEM((WIDTH, ROWS), jnp.float32),
+        ],
         compiler_params=params(),
         name="attend_back",
-    )(query_t, keys, values, weights, grad_traj)
+    )(queries, keys, values, weights, grad_traj)
 
 
 def merge_kernel(place_ref, mine_ref, theirs_ref, *refs):
@@ -433,18 +442,19 @@
         )
 
     counts = lax.dynamic_slice(tile_count, (frame_now, my_space, 0), (1, 1, FRAMES)).reshape(FRAMES)
-    query_t = queries.reshape(ROWS, WIDTH).T
-    upstream_t = grad_out.reshape(ROWS, WIDTH).T
+    query_rows = queries.reshape(ROWS, WIDTH)
+    upstream_rows = grad_out.reshape(ROWS, WIDTH)
     own_shape = (2, TILE, WIDTH)
-    key_pieces, value_pieces, far_v = gather_frames(keys.reshape(own_shape), values.reshape(own_shape))
-    key_slots = exchange(after(select_tiles(piece_ids, inside, key_pieces), far_v))
-    value_slots = exchange(select_tiles(piece_ids, inside, value_pieces))
-    weights, narrow = attend_weights(counts, query_t, key_slots)
+    key_pieces, value_pieces = gather_frames(keys.reshape(own_shape), values.reshape(own_shape))
+    key_slots = exchange(select_tiles(piece_ids, inside, key_pieces))
+    value_slots = exchange(select_tiles(piece_ids, inside, value_pieces, 13))
+    weights, narrow = attend_weights(counts, query_rows, key_slots)
     mixed, grad_traj, slot_dv = pool_frames(
-        frame_now, narrow, value_slots, w_query, w_key, w_value, upstream_t
+        frame_now, narrow, value_slots, w_query, w_key, w_value, upstream_rows
     )
-    grad_queries, slot_dk = attend_back(query_t, key_slots, value_slots, weights, grad_traj)
+    grad_queries, slot_dk = attend_back(query_rows, key_slots, value_slots, weights, grad_traj)
     owned_v = exchange(slot_dv).reshape(FRAMES * SLOTS, TILE, WIDTH)
+    owned_v = after(owned_v, slot_dk)
     merged_v = merge_slots(places, owned_v, shift(owned_v, "c", 1))
     owned_k = exchange(slot_dk).reshape(FRAMES * SLOTS, TILE, WIDTH)
     owned_k = after(owned_k, *merged_v)

time: 220 us -> 217 us (0.986)
  local copies, waits for them, and re-layouts: 11.2 us -> 1.71 us
  waiting for transfers between devices: 75.9 us -> 80.5 us
    unnamed x57 -> x6, local copies, waits for them, and re-layouts: 9.69 us -> 0.17 us
    all_to_all x4, waiting for transfers between devices: 9.37 us -> 13.1 us  [exchange(): lax.all_to_all(chosen.reshape(FRAMES, SLOTS * TILE, WIDTH), TM, split_axi...]
  transfers between devices with their start and end apart: 40 -> 40, of which waited for: 22 -> 19; matrix products, arithmetic and copies ran while one was open for 7% -> 5% of each run, Pallas kernels for 15% -> 15%
where the time goes in v1:
time: 217 us; the launch traced here: 216 us
  starting transfers between devices  80.8 us (37%)
  waiting for transfers between devices  80.5 us (37%)
  Pallas kernels  41 us (19%)
  other arithmetic  10.7 us (5%)
    ppermute x36, waiting for transfers between devices, shift(): lax.ppermute(value, axis, [(i, (i + step) % size) for i in range(size)])  67.4 us
    ppermute x36, starting transfers between devices, shift(): lax.ppermute(value, axis, [(i, (i + step) % size) for i in range(size)])  63.7 us
    all_to_all x4, starting transfers between devices, exchange(): lax.all_to_all(chosen.reshape(FRAMES, SLOTS * TILE, WIDTH), TM, split_axi...  17 us
    all_to_all x4, waiting for transfers between devices, exchange(): lax.all_to_all(chosen.reshape(FRAMES, SLOTS * TILE, WIDTH), TM, split_axi...  13.1 us
    pallas_call x1, Pallas kernels, attend_back(): pl.pallas_call(back_kernel, grid=(FRAMES,), out_shape=(jax.ShapeDtypeStru...  10.8 us
    convert_element_type x8, other arithmetic, add_wide(): return total.astype(jnp.bfloat16)  8.04 us
    pallas_call x1, Pallas kernels, pool_frames(): pl.pallas_call(pool_kernel, out_shape=(jax.ShapeDtypeStruct((ROWS, WIDTH)...  7.69 us
    pallas_call x1, Pallas kernels, attend_weights(): pl.pallas_call(weights_kernel, grid=(FRAMES,), out_shape=(jax.ShapeDtypeS...  7.59 us
  transfers between devices with their start and end apart: 40, of which 19 were waited for; matrix products, arithmetic and copies ran while one was open for 5% of the time, Pallas kernels for 15%

profile of v1, /device:TPU:1, one launch (start us, length us, event | category | flops | bytes accessed | tf_op | source)
XLA Modules:
  0.0 215.5 jit_solution(700229538245149164)
XLA Ops:
  0.6 3.9 %collective-permute-start.2 = (bf16[2,64,512]{2,1,0:T(8,128)(2,1)}, bf16[2,64,512]{2,1,0:T(8,128)(2,1)S(1)}, u32[]{:S(2)}, u32[]{:S(2)}) collective-permute-start(bf16[2,64,512]{2,1,0:T(8,128)(2,1)} %bitcast.53), channel_id=1, source_target_pairs={{0,8},{8,16},{16,24},{24,0},{1,9},{9,17},{17,25},{25,1},{2,10},{10... | collective-permute-start | bytes 393224 | tf_op jit(solution)/shard_map/ppermute | solution.py:47
  4.5 5.1 %collective-permute-start.1 = (bf16[2,64,512]{2,1,0:T(8,128)(2,1)}, bf16[2,64,512]{2,1,0:T(8,128)(2,1)S(1)}, u32[]{:S(2)}, u32[]{:S(2)}) collective-permute-start(bf16[2,64,512]{2,1,0:T(8,128)(2,1)} %bitcast.54), channel_id=1, source_target_pairs={{0,16},{8,24},{16,0},{24,8},{1,17},{9,25},{17,1},{25,9},{2,18},{10... | collective-permute-start | bytes 393224 | tf_op jit(solution)/shard_map/ppermute | solution.py:47
  9.7 2.4 %collective-permute-start = (bf16[2,64,512]{2,1,0:T(8,128)(2,1)}, bf16[2,64,512]{2,1,0:T(8,128)(2,1)S(1)}, u32[]{:S(2)}, u32[]{:S(2)}) collective-permute-start(bf16[2,64,512]{2,1,0:T(8,128)(2,1)} %bitcast.55), channel_id=1, source_target_pairs={{0,24},{8,0},{16,8},{24,16},{1,25},{9,1},{17,9},{25,17},{2,26},{10... | collective-permute-start | bytes 393224 | tf_op jit(solution)/shard_map/ppermute | solution.py:47
  12.0 6.4 %collective-permute-done.1 = bf16[2,64,512]{2,1,0:T(8,128)(2,1)S(1)} collective-permute-done((bf16[2,64,512]{2,1,0:T(8,128)(2,1)}, bf16[2,64,512]{2,1,0:T(8,128)(2,1)S(1)}, u32[]{:S(2)}, u32[]{:S(2)}) %collective-permute-start.1) | collective-permute-done | bytes 131104 | tf_op jit(solution)/shard_map/ppermute | solution.py:47
  18.5 4.3 %collective-permute-done = bf16[2,64,512]{2,1,0:T(8,128)(2,1)S(1)} collective-permute-done((bf16[2,64,512]{2,1,0:T(8,128)(2,1)}, bf16[2,64,512]{2,1,0:T(8,128)(2,1)S(1)}, u32[]{:S(2)}, u32[]{:S(2)}) %collective-permute-start) | collective-permute-done | bytes 131104 | tf_op jit(solution)/shard_map/ppermute | solution.py:47
  22.8 1.0 pad_maximum_fusion.refs_0_
  23.8 1.3 collective-permute-start.5
  25.1 2.5 %collective-permute-start.4 = (bf16[8,64,512]{2,1,0:T(8,128)(2,1)S(1)}, bf16[8,64,512]{2,1,0:T(8,128)(2,1)S(1)}, u32[]{:S(2)}, u32[]{:S(2)}) collective-permute-start(bf16[8,64,512]{2,1,0:T(8,128)(2,1)S(1)} %pad_maximum_fusion.refs_0_), channel_id=1, source_target_pairs={{0,4},{2,6},{4,0},{6,2},{1,5},{3,7},{5,1},{7,3},{8,12},{10,14},{12... | collective-permute-start | bytes 1572872 | tf_op jit(solution)/shard_map/ppermute | solution.py:47
  27.5 1.2 collective-permute-start.3
  28.7 0.9 collective-permute-start.8
  29.6 4.5 %collective-permute-start.7 = (bf16[2,64,512]{2,1,0:T(8,128)(2,1)}, bf16[2,64,512]{2,1,0:T(8,128)(2,1)S(1)}, u32[]{:S(2)}, u32[]{:S(2)}) collective-permute-start(bf16[2,64,512]{2,1,0:T(8,128)(2,1)} %bitcast.58), channel_id=1, source_target_pairs={{0,16},{8,24},{16,0},{24,8},{1,17},{9,25},{17,1},{25,9},{2,18},{10... | collective-permute-start | bytes 393224 | tf_op jit(solution)/shard_map/ppermute | solution.py:47
  34.1 2.5 %collective-permute-done.8 = bf16[2,64,512]{2,1,0:T(8,128)(2,1)S(1)} collective-permute-done((bf16[2,64,512]{2,1,0:T(8,128)(2,1)}, bf16[2,64,512]{2,1,0:T(8,128)(2,1)S(1)}, u32[]{:S(2)}, u32[]{:S(2)}) %collective-permute-start.8) | collective-permute-done | bytes 131104 | tf_op jit(solution)/shard_map/ppermute | solution.py:47
  36.6 1.3 collective-permute-start.6
  37.8 3.7 %collective-permute-done.7 = bf16[2,64,512]{2,1,0:T(8,128)(2,1)S(1)} collective-permute-done((bf16[2,64,512]{2,1,0:T(8,128)(2,1)}, bf16[2,64,512]{2,1,0:T(8,128)(2,1)S(1)}, u32[]{:S(2)}, u32[]{:S(2)}) %collective-permute-start.7) | collective-permute-done | bytes 131104 | tf_op jit(solution)/shard_map/ppermute | solution.py:47
  41.6 2.2 %collective-permute-start.9 = (bf16[8,64,512]{2,1,0:T(8,128)(2,1)S(1)}, bf16[8,64,512]{2,1,0:T(8,128)(2,1)}, u32[]{:S(2)}, u32[]{:S(2)}) collective-permute-start(bf16[8,64,512]{2,1,0:T(8,128)(2,1)S(1)} %pad_maximum_fusion.refs_0_), channel_id=1, source_target_pairs={{0,1},{1,0},{2,3},{3,2},{4,5},{5,4},{6,7},{7,6},{8,9},{9,8},{10,11... | collective-permute-start | bytes 1572872 | tf_op jit(solution)/shard_map/ppermute | solution.py:47
  43.8 1.0 pad_maximum_fusion.1.refs_0_
  44.8 5.5 %collective-permute-done.4.refs_2_ = bf16[8,64,512]{2,1,0:T(8,128)(2,1)S(1)} collective-permute-done((bf16[8,64,512]{2,1,0:T(8,128)(2,1)S(1)}, bf16[8,64,512]{2,1,0:T(8,128)(2,1)S(1)}, u32[]{:S(2)}, u32[]{:S(2)}) %collective-permute-start.4) | collective-permute-done | bytes 524320 | tf_op jit(solution)/shard_map/ppermute | solution.py:47
  50.3 1.3 collective-permute-start.10
  52.4 1.1 collective-permute-start.15
  53.5 2.1 collective-permute-start.14
  55.6 1.3 collective-permute-start.13
  57.0 3.6 %select_tiles.2 = bf16[16,64,512]{2,1,0:T(8,128)(2,1)} custom-call(s32[16]{0:T(128)S(1)} %fusion.2.piece_ref, s32[16]{0:T(128)S(1)} %get-tuple-element.59.row_ref, bf16[8,64,512]{2,1,0:T(8,128)(2,1)S(1)} %pad_maximum_fusion.refs_0_, bf16[8,64,512]{2,1,0:T(8,128)(2,1)S(1)} %collective-permute-done.3.refs_1_, ...), custom_call_target="tpu_custom_call" | custom-call | tf_op jit(solution)/shard_map/select_tiles/pallas_call | solution.py:97
  60.6 4.3 %all-to-all-start = ((bf16[8,128,512]{2,1,0:T(8,128)(2,1)}), bf16[8,128,512]{2,1,0:T(8,128)(2,1)}, u32[]{:S(2)}, u32[]{:S(2)}) async-start(bf16[8,128,512]{2,1,0:T(8,128)(2,1)} %bitcast.9), calls=%async_computation | async-start | bytes 2097152 | tf_op jit(solution)/shard_map/all_to_all | solution.py:440
  64.9 1.2 collective-permute-start.16
  66.0 1.2 collective-permute-done.15.refs_3_
  67.2 0.9 collective-permute-start.19
  68.1 10.8 %collective-permute-done.14.refs_2_ = bf16[8,64,512]{2,1,0:T(8,128)(2,1)} collective-permute-done((bf16[8,64,512]{2,1,0:T(8,128)(2,1)S(1)}, bf16[8,64,512]{2,1,0:T(8,128)(2,1)}, u32[]{:S(2)}, u32[]{:S(2)}) %collective-permute-start.14) | collective-permute-done | bytes 524320 | tf_op jit(solution)/shard_map/ppermute | solution.py:47
  78.9 0.9 collective-permute-start.18
  79.9 1.6 collective-permute-done.18.refs_6_
  82.3 3.8 %select_tiles.3 = bf16[16,64,512]{2,1,0:T(8,128)(2,1)} custom-call(s32[16]{0:T(128)S(1)} %fusion.2.piece_ref, s32[16]{0:T(128)S(1)} %get-tuple-element.59.row_ref, bf16[8,64,512]{2,1,0:T(8,128)(2,1)S(1)} %pad_maximum_fusion.1.refs_0_, bf16[8,64,512]{2,1,0:T(8,128)(2,1)} %collective-permute-done.13.refs_1_, ...), custom_call_target="tpu_custom_call" | custom-call | flops 12999999488 | tf_op jit(solution)/shard_map/select_tiles/pallas_call | solution.py:97
  86.1 4.3 %all-to-all-start.1 = ((bf16[8,128,512]{2,1,0:T(8,128)(2,1)}), bf16[8,128,512]{2,1,0:T(8,128)(2,1)}, u32[]{:S(2)}, u32[]{:S(2)}) async-start(bf16[8,128,512]{2,1,0:T(8,128)(2,1)} %bitcast.10), calls=%async_computation.1 | async-start | bytes 2097152 | tf_op jit(solution)/shard_map/all_to_all | solution.py:440
  90.4 1.4 dynamic-slice_reduce_fusion.count_ref
  91.8 7.6 %attend_weights.1 = (f32[8,4,128,256]{3,2,1,0:T(8,128)}, bf16[8,4,128,256]{3,2,1,0:T(8,128)(2,1)}) custom-call(s32[8]{0:T(128)} %dynamic-slice_reduce_fusion.count_ref, bf16[128,512]{1,0:T(8,128)(2,1)} %bitcast.48, bf16[8,128,512]{2,1,0:T(8,128)(2,1)} %all-to-all-done.key_ref), custom_call_target="tpu_custom_call" | custom-call | tf_op jit(solution)/shard_map/attend_weights/pallas_call | solution.py:154
  99.4 5.9 %all-to-all-done.1.value_ref = bf16[8,128,512]{2,1,0:T(8,128)(2,1)} async-done(((bf16[8,128,512]{2,1,0:T(8,128)(2,1)}), bf16[8,128,512]{2,1,0:T(8,128)(2,1)}, u32[]{:S(2)}, u32[]{:S(2)}) %all-to-all-start.1) | async-done | bytes 1048608 | tf_op jit(solution)/shard_map/all_to_all | solution.py:440
  105.3 7.7 %pool_frames.1 = (bf16[128,512]{1,0:T(8,128)(2,1)}, bf16[8,512,128]{2,1,0:T(8,128)(2,1)}, bf16[8,128,512]{2,1,0:T(8,128)(2,1)}) custom-call(s32[1]{0:T(128)} %bitcast.frame_ref, bf16[8,4,128,256]{3,2,1,0:T(8,128)(2,1)} %get-tuple-element.34.weight_ref, bf16[8,128,512]{2,1,0:T(8,128)(2,1)} %all-to-all-done.1.value_ref, bf16[512,512]{1,0:T(8,128)(2,1)} %wq_ref.1, ...), custom_call_target="tpu_custom_call" | custom-call | tf_op jit(solution)/shard_map/pool_frames/pallas_call | solution.py:251
  113.0 4.3 %all-to-all-start.3 = ((bf16[8,128,512]{2,1,0:T(8,128)(2,1)}), bf16[8,128,512]{2,1,0:T(8,128)(2,1)}, u32[]{:S(2)}, u32[]{:S(2)}) async-start(bf16[8,128,512]{2,1,0:T(8,128)(2,1)} %get-tuple-element.40), calls=%async_computation.3 | async-start | bytes 2097152 | tf_op jit(solution)/shard_map/all_to_all | solution.py:440
  117.3 10.8 %attend_back.1 = (bf16[128,512]{1,0:T(8,128)(2,1)}, bf16[8,128,512]{2,1,0:T(8,128)(2,1)}) custom-call(bf16[128,512]{1,0:T(8,128)(2,1)} %bitcast.49, bf16[8,128,512]{2,1,0:T(8,128)(2,1)} %all-to-all-done.key_ref, bf16[8,128,512]{2,1,0:T(8,128)(2,1)} %all-to-all-done.1.value_ref, f32[8,4,128,256]{3,2,1,0:T(8,128)} %get-tuple-element.36.weight_ref, ...), custom_call_target="tpu_custom_call" | custom-call | tf_op jit(solution)/shard_map/attend_back/pallas_call | solution.py:308
  128.1 3.1 %all-to-all-done.3 = bf16[8,128,512]{2,1,0:T(8,128)(2,1)} async-done(((bf16[8,128,512]{2,1,0:T(8,128)(2,1)}), bf16[8,128,512]{2,1,0:T(8,128)(2,1)}, u32[]{:S(2)}, u32[]{:S(2)}) %all-to-all-start.3) | async-done | bytes 1048608 | tf_op jit(solution)/shard_map/all_to_all | solution.py:440
  131.3 4.2 %all-to-all-start.2 = ((bf16[8,128,512]{2,1,0:T(8,128)(2,1)}), bf16[8,128,512]{2,1,0:T(8,128)(2,1)}, u32[]{:S(2)}, u32[]{:S(2)}) async-start(bf16[8,128,512]{2,1,0:T(8,128)(2,1)} %get-tuple-element.39), calls=%async_computation.2 | async-start | bytes 2097152 | tf_op jit(solution)/shard_map/all_to_all | solution.py:440
  135.5 2.8 %collective-permute-start.20 = (bf16[16,64,512]{2,1,0:T(8,128)(2,1)}, bf16[16,64,512]{2,1,0:T(8,128)(2,1)}, u32[]{:S(2)}, u32[]{:S(2)}) collective-permute-start(bf16[16,64,512]{2,1,0:T(8,128)(2,1)} %bitcast.17.mine_ref), channel_id=1, source_target_pairs={{0,1},{1,0},{2,3},{3,2},{4,5},{5,4},{6,7},{7,6},{8,9},{9,8},{10,11... | collective-permute-start | bytes 3145736 | tf_op jit(solution)/shard_map/ppermute | solution.py:47
  139.0 1.9 collective-permute-done.20.theirs_ref
  140.9 3.7 %merge_slots.2 = (bf16[8,64,512]{2,1,0:T(8,128)(2,1)}, bf16[8,64,512]{2,1,0:T(8,128)(2,1)}, bf16[4,64,512]{2,1,0:T(8,128)(2,1)}, bf16[4,64,512]{2,1,0:T(8,128)(2,1)}, bf16[8,64,512]{2,1,0:T(8,128)(2,1)}) custom-call(s32[32]{0:T(128)} %pad_add_fusion.place_ref, bf16[16,64,512]{2,1,0:T(8,128)(2,1)} %bitcast.17.mine_ref, ...), custom_call_target="tpu_custom_call" | custom-call | tf_op jit(solution)/shard_map/merge_slots/pallas_call | solution.py:354
  144.6 4.0 %all-to-all-done.2 = bf16[8,128,512]{2,1,0:T(8,128)(2,1)} async-done(((bf16[8,128,512]{2,1,0:T(8,128)(2,1)}), bf16[8,128,512]{2,1,0:T(8,128)(2,1)}, u32[]{:S(2)}, u32[]{:S(2)}) %all-to-all-start.2) | async-done | bytes 1048608 | tf_op jit(solution)/shard_map/all_to_all | solution.py:440
  148.6 3.6 %collective-permute-start.21 = (bf16[16,64,512]{2,1,0:T(8,128)(2,1)}, bf16[16,64,512]{2,1,0:T(8,128)(2,1)}, u32[]{:S(2)}, u32[]{:S(2)}) collective-permute-start(bf16[16,64,512]{2,1,0:T(8,128)(2,1)} %bitcast.16.mine_ref), channel_id=1, source_target_pairs={{0,1},{1,0},{2,3},{3,2},{4,5},{5,4},{6,7},{7,6},{8,9},{9,8},{10,11... | collective-permute-start | bytes 3145736 | tf_op jit(solution)/shard_map/ppermute | solution.py:47
  152.3 1.0 collective-permute-start.29
  153.3 1.7 collective-permute-start.30
  155.0 3.8 %merge_slots.3 = (bf16[8,64,512]{2,1,0:T(8,128)(2,1)}, bf16[8,64,512]{2,1,0:T(8,128)(2,1)}, bf16[4,64,512]{2,1,0:T(8,128)(2,1)}, bf16[4,64,512]{2,1,0:T(8,128)(2,1)}, bf16[8,64,512]{2,1,0:T(8,128)(2,1)}) custom-call(s32[32]{0:T(128)} %pad_add_fusion.place_ref, bf16[16,64,512]{2,1,0:T(8,128)(2,1)} %bitcast.16.mine_ref, ...), custom_call_target="tpu_custom_call" | custom-call | tf_op jit(solution)/shard_map/merge_slots/pallas_call | solution.py:354
  158.7 1.8 collective-permute-start.22
  160.5 6.9 %collective-permute-done.29 = bf16[8,64,512]{2,1,0:T(8,128)(2,1)} collective-permute-done((bf16[8,64,512]{2,1,0:T(8,128)(2,1)}, bf16[8,64,512]{2,1,0:T(8,128)(2,1)}, u32[]{:S(2)}, u32[]{:S(2)}) %collective-permute-start.29) | collective-permute-done | bytes 524320 | tf_op jit(solution)/shard_map/ppermute | solution.py:47
  167.4 1.0 add_convert_fusion
  168.4 2.3 %collective-permute-start.33 = (bf16[4,64,512]{2,1,0:T(8,128)(2,1)S(1)}, bf16[4,64,512]{2,1,0:T(8,128)(2,1)S(1)}, u32[]{:S(2)}, u32[]{:S(2)}) collective-permute-start(bf16[4,64,512]{2,1,0:T(8,128)(2,1)S(1)} %add_convert_fusion), channel_id=1, source_target_pairs={{0,6},{2,0},{4,2},{6,4},{1,7},{3,1},{5,3},{7,5},{8,14},{10,8},{12,... | collective-permute-start | bytes 786440 | tf_op jit(solution)/shard_map/ppermute | solution.py:47
  170.7 1.1 add_convert_fusion.1
  171.9 6.1 %collective-permute-done.22 = bf16[8,64,512]{2,1,0:T(8,128)(2,1)S(1)} collective-permute-done((bf16[8,64,512]{2,1,0:T(8,128)(2,1)}, bf16[8,64,512]{2,1,0:T(8,128)(2,1)S(1)}, u32[]{:S(2)}, u32[]{:S(2)}) %collective-permute-start.22) | collective-permute-done | bytes 524320 | tf_op jit(solution)/shard_map/ppermute | solution.py:47
  178.0 1.0 add_convert_fusion.2
  179.0 2.9 %collective-permute-start.26 = (bf16[4,64,512]{2,1,0:T(8,128)(2,1)S(1)}, bf16[4,64,512]{2,1,0:T(8,128)(2,1)S(1)}, u32[]{:S(2)}, u32[]{:S(2)}) collective-permute-start(bf16[4,64,512]{2,1,0:T(8,128)(2,1)S(1)} %add_convert_fusion.2), channel_id=1, source_target_pairs={{0,6},{2,0},{4,2},{6,4},{1,7},{3,1},{5,3},{7,5},{8,14},{10,8},{12,... | collective-permute-start | bytes 786440 | tf_op jit(solution)/shard_map/ppermute | solution.py:47
  181.9 1.0 add_convert_fusion.3
  184.1 1.3 add_convert_fusion.6
  185.4 4.1 %collective-permute-start.34 = (bf16[2,64,512]{2,1,0:T(8,128)(2,1)S(1)}, bf16[2,64,512]{2,1,0:T(8,128)(2,1)S(1)}, u32[]{:S(2)}, u32[]{:S(2)}) collective-permute-start(bf16[2,64,512]{2,1,0:T(8,128)(2,1)S(1)} %get-tuple-element.62), channel_id=1, source_target_pairs={{0,16},{8,24},{16,0},{24,8},{1,17},{9,25},{17,1},{25,9},{2,18},{10... | collective-permute-start | bytes 393224 | tf_op jit(solution)/shard_map/ppermute | solution.py:47
  190.2 1.7 collective-permute-start.32
  192.1 2.6 %collective-permute-start.27 = (bf16[2,64,512]{2,1,0:T(8,128)(2,1)S(1)}, bf16[2,64,512]{2,1,0:T(8,128)(2,1)S(1)}, u32[]{:S(2)}, u32[]{:S(2)}) collective-permute-start(bf16[2,64,512]{2,1,0:T(8,128)(2,1)S(1)} %get-tuple-element.64), channel_id=1, source_target_pairs={{0,16},{8,24},{16,0},{24,8},{1,17},{9,25},{17,1},{25,9},{2,18},{10... | collective-permute-start | bytes 393224 | tf_op jit(solution)/shard_map/ppermute | solution.py:47
  194.7 3.6 %collective-permute-start.28 = (bf16[2,64,512]{2,1,0:T(8,128)(2,1)S(1)}, bf16[2,64,512]{2,1,0:T(8,128)(2,1)S(1)}, u32[]{:S(2)}, u32[]{:S(2)}) collective-permute-start(bf16[2,64,512]{2,1,0:T(8,128)(2,1)S(1)} %get-tuple-element.65), channel_id=1, source_target_pairs={{0,24},{8,0},{16,8},{24,16},{1,25},{9,1},{17,9},{25,17},{2,26},{10... | collective-permute-start | bytes 393224 | tf_op jit(solution)/shard_map/ppermute | solution.py:47
  198.4 13.5 %collective-permute-done.35 = bf16[2,64,512]{2,1,0:T(8,128)(2,1)S(1)} collective-permute-done((bf16[2,64,512]{2,1,0:T(8,128)(2,1)S(1)}, bf16[2,64,512]{2,1,0:T(8,128)(2,1)S(1)}, u32[]{:S(2)}, u32[]{:S(2)}) %collective-permute-start.35) | collective-permute-done | bytes 131104 | tf_op jit(solution)/shard_map/ppermute | solution.py:47
  211.9 1.7 add_convert_fusion.4
  213.6 1.1 collective-permute-done.28
  (46 shorter events, 5.5 us)
Async XLA Ops:
  0.6 51.0 %copy-start = (s32[8,32,8,2]{1,3,2,0:T(2,128)S(1)}, s32[8,32,8,2]{1,3,2,0:T(2,128)}, u32[]{:S(2)}) copy-start(s32[8,32,8,2]{1,3,2,0:T(2,128)} %param.16) | copy-start | bytes 49156
  0.6 11.4 %collective-permute-start.2 = (bf16[2,64,512]{2,1,0:T(8,128)(2,1)}, bf16[2,64,512]{2,1,0:T(8,128)(2,1)S(1)}, u32[]{:S(2)}, u32[]{:S(2)}) collective-permute-start(bf16[2,64,512]{2,1,0:T(8,128)(2,1)} %bitcast.53), channel_id=1, source_target_pairs={{0,8},{8,16},{16,24},{24,0},{1,9},{9,17},{17,25},{25,1},{2,10},{10... | collective-permute-start | bytes 393224 | tf_op jit(solution)/shard_map/ppermute | solution.py:47
  4.5 13.9 %collective-permute-start.1 = (bf16[2,64,512]{2,1,0:T(8,128)(2,1)}, bf16[2,64,512]{2,1,0:T(8,128)(2,1)S(1)}, u32[]{:S(2)}, u32[]{:S(2)}) collective-permute-start(bf16[2,64,512]{2,1,0:T(8,128)(2,1)} %bitcast.54), channel_id=1, source_target_pairs={{0,16},{8,24},{16,0},{24,8},{1,17},{9,25},{17,1},{25,9},{2,18},{10... | collective-permute-start | bytes 393224 | tf_op jit(solution)/shard_map/ppermute | solution.py:47
  9.7 13.1 %collective-permute-start = (bf16[2,64,512]{2,1,0:T(8,128)(2,1)}, bf16[2,64,512]{2,1,0:T(8,128)(2,1)S(1)}, u32[]{:S(2)}, u32[]{:S(2)}) collective-permute-start(bf16[2,64,512]{2,1,0:T(8,128)(2,1)} %bitcast.55), channel_id=1, source_target_pairs={{0,24},{8,0},{16,8},{24,16},{1,25},{9,1},{17,9},{25,17},{2,26},{10... | collective-permute-start | bytes 393224 | tf_op jit(solution)/shard_map/ppermute | solution.py:47
  23.8 21.0 %collective-permute-start.5 = (bf16[8,64,512]{2,1,0:T(8,128)(2,1)S(1)}, bf16[8,64,512]{2,1,0:T(8,128)(2,1)S(1)}, u32[]{:S(2)}, u32[]{:S(2)}) collective-permute-start(bf16[8,64,512]{2,1,0:T(8,128)(2,1)S(1)} %pad_maximum_fusion.refs_0_), channel_id=1, source_target_pairs={{0,2},{2,4},{4,6},{6,0},{1,3},{3,5},{5,7},{7,1},{8,10},{10,12},{12... | collective-permute-start | bytes 1572872 | tf_op jit(solution)/shard_map/ppermute | solution.py:47
  25.1 25.2 %collective-permute-start.4 = (bf16[8,64,512]{2,1,0:T(8,128)(2,1)S(1)}, bf16[8,64,512]{2,1,0:T(8,128)(2,1)S(1)}, u32[]{:S(2)}, u32[]{:S(2)}) collective-permute-start(bf16[8,64,512]{2,1,0:T(8,128)(2,1)S(1)} %pad_maximum_fusion.refs_0_), channel_id=1, source_target_pairs={{0,4},{2,6},{4,0},{6,2},{1,5},{3,7},{5,1},{7,3},{8,12},{10,14},{12... | collective-permute-start | bytes 1572872 | tf_op jit(solution)/shard_map/ppermute | solution.py:47
  27.5 22.8 %collective-permute-start.3 = (bf16[8,64,512]{2,1,0:T(8,128)(2,1)S(1)}, bf16[8,64,512]{2,1,0:T(8,128)(2,1)S(1)}, u32[]{:S(2)}, u32[]{:S(2)}) collective-permute-start(bf16[8,64,512]{2,1,0:T(8,128)(2,1)S(1)} %pad_maximum_fusion.refs_0_), channel_id=1, source_target_pairs={{0,6},{2,0},{4,2},{6,4},{1,7},{3,1},{5,3},{7,5},{8,14},{10,8},{12,... | collective-permute-start | bytes 1572872 | tf_op jit(solution)/shard_map/ppermute | solution.py:47
  28.7 7.9 %collective-permute-start.8 = (bf16[2,64,512]{2,1,0:T(8,128)(2,1)}, bf16[2,64,512]{2,1,0:T(8,128)(2,1)S(1)}, u32[]{:S(2)}, u32[]{:S(2)}) collective-permute-start(bf16[2,64,512]{2,1,0:T(8,128)(2,1)} %bitcast.57), channel_id=1, source_target_pairs={{0,8},{8,16},{16,24},{24,0},{1,9},{9,17},{17,25},{25,1},{2,10},{10... | collective-permute-start | bytes 393224 | tf_op jit(solution)/shard_map/ppermute | solution.py:47
  29.6 12.0 %collective-permute-start.7 = (bf16[2,64,512]{2,1,0:T(8,128)(2,1)}, bf16[2,64,512]{2,1,0:T(8,128)(2,1)S(1)}, u32[]{:S(2)}, u32[]{:S(2)}) collective-permute-start(bf16[2,64,512]{2,1,0:T(8,128)(2,1)} %bitcast.58), channel_id=1, source_target_pairs={{0,16},{8,24},{16,0},{24,8},{1,17},{9,25},{17,1},{25,9},{2,18},{10... | collective-permute-start | bytes 393224 | tf_op jit(solution)/shard_map/ppermute | solution.py:47
  36.6 7.2 %collective-permute-start.6 = (bf16[2,64,512]{2,1,0:T(8,128)(2,1)}, bf16[2,64,512]{2,1,0:T(8,128)(2,1)S(1)}, u32[]{:S(2)}, u32[]{:S(2)}) collective-permute-start(bf16[2,64,512]{2,1,0:T(8,128)(2,1)} %bitcast.59), channel_id=1, source_target_pairs={{0,24},{8,0},{16,8},{24,16},{1,25},{9,1},{17,9},{25,17},{2,26},{10... | collective-permute-start | bytes 393224 | tf_op jit(solution)/shard_map/ppermute | solution.py:47
  41.6 11.9 %collective-permute-start.9 = (bf16[8,64,512]{2,1,0:T(8,128)(2,1)S(1)}, bf16[8,64,512]{2,1,0:T(8,128)(2,1)}, u32[]{:S(2)}, u32[]{:S(2)}) collective-permute-start(bf16[8,64,512]{2,1,0:T(8,128)(2,1)S(1)} %pad_maximum_fusion.refs_0_), channel_id=1, source_target_pairs={{0,1},{1,0},{2,3},{3,2},{4,5},{5,4},{6,7},{7,6},{8,9},{9,8},{10,11... | collective-permute-start | bytes 1572872 | tf_op jit(solution)/shard_map/ppermute | solution.py:47
  50.3 5.3 %collective-permute-start.10 = (bf16[8,64,512]{2,1,0:T(8,128)(2,1)S(1)}, bf16[8,64,512]{2,1,0:T(8,128)(2,1)}, u32[]{:S(2)}, u32[]{:S(2)}) collective-permute-start(bf16[8,64,512]{2,1,0:T(8,128)(2,1)S(1)} %collective-permute-done.3.refs_1_), channel_id=1, source_target_pairs={{0,1},{1,0},{2,3},{3,2},{4,5},{5,4},{6,7},{7,6},{8,9},{9,8},{10,11... | collective-permute-start | bytes 1572872 | tf_op jit(solution)/shard_map/ppermute | solution.py:47
  51.7 5.2 %collective-permute-start.11 = (bf16[8,64,512]{2,1,0:T(8,128)(2,1)S(1)}, bf16[8,64,512]{2,1,0:T(8,128)(2,1)}, u32[]{:S(2)}, u32[]{:S(2)}) collective-permute-start(bf16[8,64,512]{2,1,0:T(8,128)(2,1)S(1)} %collective-permute-done.4.refs_2_), channel_id=1, source_target_pairs={{0,1},{1,0},{2,3},{3,2},{4,5},{5,4},{6,7},{7,6},{8,9},{9,8},{10,11... | collective-permute-start | bytes 1572872 | tf_op jit(solution)/shard_map/ppermute | solution.py:47
  51.7 5.2 %collective-permute-start.12 = (bf16[8,64,512]{2,1,0:T(8,128)(2,1)S(1)}, bf16[8,64,512]{2,1,0:T(8,128)(2,1)}, u32[]{:S(2)}, u32[]{:S(2)}) collective-permute-start(bf16[8,64,512]{2,1,0:T(8,128)(2,1)S(1)} %collective-permute-done.5.refs_3_), channel_id=1, source_target_pairs={{0,1},{1,0},{2,3},{3,2},{4,5},{5,4},{6,7},{7,6},{8,9},{9,8},{10,11... | collective-permute-start | bytes 1572872 | tf_op jit(solution)/shard_map/ppermute | solution.py:47
  52.4 14.8 %collective-permute-start.15 = (bf16[8,64,512]{2,1,0:T(8,128)(2,1)S(1)}, bf16[8,64,512]{2,1,0:T(8,128)(2,1)}, u32[]{:S(2)}, u32[]{:S(2)}) collective-permute-start(bf16[8,64,512]{2,1,0:T(8,128)(2,1)S(1)} %pad_maximum_fusion.1.refs_0_), channel_id=1, source_target_pairs={{0,2},{2,4},{4,6},{6,0},{1,3},{3,5},{5,7},{7,1},{8,10},{10,12},{12... | collective-permute-start | bytes 1572872 | tf_op jit(solution)/shard_map/ppermute | solution.py:47
  53.5 25.4 %collective-permute-start.14 = (bf16[8,64,512]{2,1,0:T(8,128)(2,1)S(1)}, bf16[8,64,512]{2,1,0:T(8,128)(2,1)}, u32[]{:S(2)}, u32[]{:S(2)}) collective-permute-start(bf16[8,64,512]{2,1,0:T(8,128)(2,1)S(1)} %pad_maximum_fusion.1.refs_0_), channel_id=1, source_target_pairs={{0,4},{2,6},{4,0},{6,2},{1,5},{3,7},{5,1},{7,3},{8,12},{10,14},{12... | collective-permute-start | bytes 1572872 | tf_op jit(solution)/shard_map/ppermute | solution.py:47
  55.6 24.2 %collective-permute-start.13 = (bf16[8,64,512]{2,1,0:T(8,128)(2,1)S(1)}, bf16[8,64,512]{2,1,0:T(8,128)(2,1)}, u32[]{:S(2)}, u32[]{:S(2)}) collective-permute-start(bf16[8,64,512]{2,1,0:T(8,128)(2,1)S(1)} %pad_maximum_fusion.1.refs_0_), channel_id=1, source_target_pairs={{0,6},{2,0},{4,2},{6,4},{1,7},{3,1},{5,3},{7,5},{8,14},{10,8},{12,... | collective-permute-start | bytes 1572872 | tf_op jit(solution)/shard_map/ppermute | solution.py:47
  60.6 25.5 %all-to-all-start = ((bf16[8,128,512]{2,1,0:T(8,128)(2,1)}), bf16[8,128,512]{2,1,0:T(8,128)(2,1)}, u32[]{:S(2)}, u32[]{:S(2)}) async-start(bf16[8,128,512]{2,1,0:T(8,128)(2,1)} %bitcast.9), calls=%async_computation | async-start | bytes 2097152 | tf_op jit(solution)/shard_map/all_to_all | solution.py:440
  64.9 15.1 %collective-permute-start.16 = (bf16[8,64,512]{2,1,0:T(8,128)(2,1)S(1)}, bf16[8,64,512]{2,1,0:T(8,128)(2,1)S(1)}, u32[]{:S(2)}, u32[]{:S(2)}) collective-permute-start(bf16[8,64,512]{2,1,0:T(8,128)(2,1)S(1)} %pad_maximum_fusion.1.refs_0_), channel_id=1, source_target_pairs={{0,1},{1,0},{2,3},{3,2},{4,5},{5,4},{6,7},{7,6},{8,9},{9,8},{10,11... | collective-permute-start | bytes 1572872 | tf_op jit(solution)/shard_map/ppermute | solution.py:47
  67.2 12.7 %collective-permute-start.19 = (bf16[8,64,512]{2,1,0:T(8,128)(2,1)}, bf16[8,64,512]{2,1,0:T(8,128)(2,1)S(1)}, u32[]{:S(2)}, u32[]{:S(2)}) collective-permute-start(bf16[8,64,512]{2,1,0:T(8,128)(2,1)} %collective-permute-done.15.refs_3_), channel_id=1, source_target_pairs={{0,1},{1,0},{2,3},{3,2},{4,5},{5,4},{6,7},{7,6},{8,9},{9,8},{10,11... | collective-permute-start | bytes 1572872 | tf_op jit(solution)/shard_map/ppermute | solution.py:47
  78.9 2.6 %collective-permute-start.18 = (bf16[8,64,512]{2,1,0:T(8,128)(2,1)}, bf16[8,64,512]{2,1,0:T(8,128)(2,1)S(1)}, u32[]{:S(2)}, u32[]{:S(2)}) collective-permute-start(bf16[8,64,512]{2,1,0:T(8,128)(2,1)} %collective-permute-done.14.refs_2_), channel_id=1, source_target_pairs={{0,1},{1,0},{2,3},{3,2},{4,5},{5,4},{6,7},{7,6},{8,9},{9,8},{10,11... | collective-permute-start | bytes 1572872 | tf_op jit(solution)/shard_map/ppermute | solution.py:47
  79.8 2.5 %collective-permute-start.17 = (bf16[8,64,512]{2,1,0:T(8,128)(2,1)}, bf16[8,64,512]{2,1,0:T(8,128)(2,1)S(1)}, u32[]{:S(2)}, u32[]{:S(2)}) collective-permute-start(bf16[8,64,512]{2,1,0:T(8,128)(2,1)} %collective-permute-done.13.refs_1_), channel_id=1, source_target_pairs={{0,1},{1,0},{2,3},{3,2},{4,5},{5,4},{6,7},{7,6},{8,9},{9,8},{10,11... | collective-permute-start | bytes 1572872 | tf_op jit(solution)/shard_map/ppermute | solution.py:47
  86.1 19.2 %all-to-all-start.1 = ((bf16[8,128,512]{2,1,0:T(8,128)(2,1)}), bf16[8,128,512]{2,1,0:T(8,128)(2,1)}, u32[]{:S(2)}, u32[]{:S(2)}) async-start(bf16[8,128,512]{2,1,0:T(8,128)(2,1)} %bitcast.10), calls=%async_computation.1 | async-start | bytes 2097152 | tf_op jit(solution)/shard_map/all_to_all | solution.py:440
  113.0 18.2 %all-to-all-start.3 = ((bf16[8,128,512]{2,1,0:T(8,128)(2,1)}), bf16[8,128,512]{2,1,0:T(8,128)(2,1)}, u32[]{:S(2)}, u32[]{:S(2)}) async-start(bf16[8,128,512]{2,1,0:T(8,128)(2,1)} %get-tuple-element.40), calls=%async_computation.3 | async-start | bytes 2097152 | tf_op jit(solution)/shard_map/all_to_all | solution.py:440
  131.3 17.4 %all-to-all-start.2 = ((bf16[8,128,512]{2,1,0:T(8,128)(2,1)}), bf16[8,128,512]{2,1,0:T(8,128)(2,1)}, u32[]{:S(2)}, u32[]{:S(2)}) async-start(bf16[8,128,512]{2,1,0:T(8,128)(2,1)} %get-tuple-element.39), calls=%async_computation.2 | async-start | bytes 2097152 | tf_op jit(solution)/shard_map/all_to_all | solution.py:440
  135.5 5.4 %collective-permute-start.20 = (bf16[16,64,512]{2,1,0:T(8,128)(2,1)}, bf16[16,64,512]{2,1,0:T(8,128)(2,1)}, u32[]{:S(2)}, u32[]{:S(2)}) collective-permute-start(bf16[16,64,512]{2,1,0:T(8,128)(2,1)} %bitcast.17.mine_ref), channel_id=1, source_target_pairs={{0,1},{1,0},{2,3},{3,2},{4,5},{5,4},{6,7},{7,6},{8,9},{9,8},{10,11... | collective-permute-start | bytes 3145736 | tf_op jit(solution)/shard_map/ppermute | solution.py:47
  148.6 6.3 %collective-permute-start.21 = (bf16[16,64,512]{2,1,0:T(8,128)(2,1)}, bf16[16,64,512]{2,1,0:T(8,128)(2,1)}, u32[]{:S(2)}, u32[]{:S(2)}) collective-permute-start(bf16[16,64,512]{2,1,0:T(8,128)(2,1)} %bitcast.16.mine_ref), channel_id=1, source_target_pairs={{0,1},{1,0},{2,3},{3,2},{4,5},{5,4},{6,7},{7,6},{8,9},{9,8},{10,11... | collective-permute-start | bytes 3145736 | tf_op jit(solution)/shard_map/ppermute | solution.py:47
  152.3 15.1 %collective-permute-start.29 = (bf16[8,64,512]{2,1,0:T(8,128)(2,1)}, bf16[8,64,512]{2,1,0:T(8,128)(2,1)}, u32[]{:S(2)}, u32[]{:S(2)}) collective-permute-start(bf16[8,64,512]{2,1,0:T(8,128)(2,1)} %get-tuple-element.42), channel_id=1, source_target_pairs={{0,2},{2,4},{4,6},{6,0},{1,3},{3,5},{5,7},{7,1},{8,10},{10,12},{12... | collective-permute-start | bytes 1572872 | tf_op jit(solution)/shard_map/ppermute | solution.py:47
  153.3 14.1 %collective-permute-start.30 = (bf16[8,64,512]{2,1,0:T(8,128)(2,1)}, bf16[8,64,512]{2,1,0:T(8,128)(2,1)S(1)}, u32[]{:S(2)}, u32[]{:S(2)}) collective-permute-start(bf16[8,64,512]{2,1,0:T(8,128)(2,1)} %get-tuple-element.43), channel_id=1, source_target_pairs={{0,6},{2,0},{4,2},{6,4},{1,7},{3,1},{5,3},{7,5},{8,14},{10,8},{12,... | collective-permute-start | bytes 1572872 | tf_op jit(solution)/shard_map/ppermute | solution.py:47
  158.7 33.2 %copy-start.1 = (bf16[8,64,512]{2,1,0:T(8,128)(2,1)S(1)}, bf16[8,64,512]{2,1,0:T(8,128)(2,1)}, u32[]{:S(2)}) copy-start(bf16[8,64,512]{2,1,0:T(8,128)(2,1)} %get-tuple-element.48) | copy-start | bytes 1572868
  158.7 19.3 %collective-permute-start.22 = (bf16[8,64,512]{2,1,0:T(8,128)(2,1)}, bf16[8,64,512]{2,1,0:T(8,128)(2,1)S(1)}, u32[]{:S(2)}, u32[]{:S(2)}) collective-permute-start(bf16[8,64,512]{2,1,0:T(8,128)(2,1)} %get-tuple-element.49), channel_id=1, source_target_pairs={{0,6},{2,0},{4,2},{6,4},{1,7},{3,1},{5,3},{7,5},{8,14},{10,8},{12,... | collective-permute-start | bytes 1572872 | tf_op jit(solution)/shard_map/ppermute | solution.py:47
  160.5 21.4 %collective-permute-start.23 = (bf16[8,64,512]{2,1,0:T(8,128)(2,1)}, bf16[8,64,512]{2,1,0:T(8,128)(2,1)S(1)}, u32[]{:S(2)}, u32[]{:S(2)}) collective-permute-start(bf16[8,64,512]{2,1,0:T(8,128)(2,1)} %get-tuple-element.51), channel_id=1, source_target_pairs={{0,2},{2,4},{4,6},{6,0},{1,3},{3,5},{5,7},{7,1},{8,10},{10,12},{12... | collective-permute-start | bytes 1572872 | tf_op jit(solution)/shard_map/ppermute | solution.py:47
  168.4 15.2 %collective-permute-start.33 = (bf16[4,64,512]{2,1,0:T(8,128)(2,1)S(1)}, bf16[4,64,512]{2,1,0:T(8,128)(2,1)S(1)}, u32[]{:S(2)}, u32[]{:S(2)}) collective-permute-start(bf16[4,64,512]{2,1,0:T(8,128)(2,1)S(1)} %add_convert_fusion), channel_id=1, source_target_pairs={{0,6},{2,0},{4,2},{6,4},{1,7},{3,1},{5,3},{7,5},{8,14},{10,8},{12,... | collective-permute-start | bytes 786440 | tf_op jit(solution)/shard_map/ppermute | solution.py:47
  171.8 12.3 %collective-permute-start.31 = (bf16[4,64,512]{2,1,0:T(8,128)(2,1)S(1)}, bf16[4,64,512]{2,1,0:T(8,128)(2,1)S(1)}, u32[]{:S(2)}, u32[]{:S(2)}) collective-permute-start(bf16[4,64,512]{2,1,0:T(8,128)(2,1)S(1)} %add_convert_fusion.1), channel_id=1, source_target_pairs={{0,2},{2,4},{4,6},{6,0},{1,3},{3,5},{5,7},{7,1},{8,10},{10,12},{12... | collective-permute-start | bytes 786440 | tf_op jit(solution)/shard_map/ppermute | solution.py:47
  179.0 12.9 %collective-permute-start.26 = (bf16[4,64,512]{2,1,0:T(8,128)(2,1)S(1)}, bf16[4,64,512]{2,1,0:T(8,128)(2,1)S(1)}, u32[]{:S(2)}, u32[]{:S(2)}) collective-permute-start(bf16[4,64,512]{2,1,0:T(8,128)(2,1)S(1)} %add_convert_fusion.2), channel_id=1, source_target_pairs={{0,6},{2,0},{4,2},{6,4},{1,7},{3,1},{5,3},{7,5},{8,14},{10,8},{12,... | collective-permute-start | bytes 786440 | tf_op jit(solution)/shard_map/ppermute | solution.py:47
  183.0 8.9 %collective-permute-start.24 = (bf16[4,64,512]{2,1,0:T(8,128)(2,1)S(1)}, bf16[4,64,512]{2,1,0:T(8,128)(2,1)S(1)}, u32[]{:S(2)}, u32[]{:S(2)}) collective-permute-start(bf16[4,64,512]{2,1,0:T(8,128)(2,1)S(1)} %add_convert_fusion.3), channel_id=1, source_target_pairs={{0,2},{2,4},{4,6},{6,0},{1,3},{3,5},{5,7},{7,1},{8,10},{10,12},{12... | collective-permute-start | bytes 786440 | tf_op jit(solution)/shard_map/ppermute | solution.py:47
  185.4 12.8 %collective-permute-start.34 = (bf16[2,64,512]{2,1,0:T(8,128)(2,1)S(1)}, bf16[2,64,512]{2,1,0:T(8,128)(2,1)S(1)}, u32[]{:S(2)}, u32[]{:S(2)}) collective-permute-start(bf16[2,64,512]{2,1,0:T(8,128)(2,1)S(1)} %get-tuple-element.62), channel_id=1, source_target_pairs={{0,16},{8,24},{16,0},{24,8},{1,17},{9,25},{17,1},{25,9},{2,18},{10... | collective-permute-start | bytes 393224 | tf_op jit(solution)/shard_map/ppermute | solution.py:47
  189.5 22.4 %collective-permute-start.35 = (bf16[2,64,512]{2,1,0:T(8,128)(2,1)S(1)}, bf16[2,64,512]{2,1,0:T(8,128)(2,1)S(1)}, u32[]{:S(2)}, u32[]{:S(2)}) collective-permute-start(bf16[2,64,512]{2,1,0:T(8,128)(2,1)S(1)} %get-tuple-element.63), channel_id=1, source_target_pairs={{0,24},{8,0},{16,8},{24,16},{1,25},{9,1},{17,9},{25,17},{2,26},{10... | collective-permute-start | bytes 393224 | tf_op jit(solution)/shard_map/ppermute | solution.py:47
  190.2 21.7 %collective-permute-start.32 = (bf16[2,64,512]{2,1,0:T(8,128)(2,1)S(1)}, bf16[2,64,512]{2,1,0:T(8,128)(2,1)S(1)}, u32[]{:S(2)}, u32[]{:S(2)}) collective-permute-start(bf16[2,64,512]{2,1,0:T(8,128)(2,1)S(1)} %get-tuple-element.66), channel_id=1, source_target_pairs={{0,8},{8,16},{16,24},{24,0},{1,9},{9,17},{17,25},{25,1},{2,10},{10... | collective-permute-start | bytes 393224 | tf_op jit(solution)/shard_map/ppermute | solution.py:47
  192.1 21.5 %collective-permute-start.27 = (bf16[2,64,512]{2,1,0:T(8,128)(2,1)S(1)}, bf16[2,64,512]{2,1,0:T(8,128)(2,1)S(1)}, u32[]{:S(2)}, u32[]{:S(2)}) collective-permute-start(bf16[2,64,512]{2,1,0:T(8,128)(2,1)S(1)} %get-tuple-element.64), channel_id=1, source_target_pairs={{0,16},{8,24},{16,0},{24,8},{1,17},{9,25},{17,1},{25,9},{2,18},{10... | collective-permute-start | bytes 393224 | tf_op jit(solution)/shard_map/ppermute | solution.py:47
  194.7 20.1 %collective-permute-start.28 = (bf16[2,64,512]{2,1,0:T(8,128)(2,1)S(1)}, bf16[2,64,512]{2,1,0:T(8,128)(2,1)S(1)}, u32[]{:S(2)}, u32[]{:S(2)}) collective-permute-start(bf16[2,64,512]{2,1,0:T(8,128)(2,1)S(1)} %get-tuple-element.65), channel_id=1, source_target_pairs={{0,24},{8,0},{16,8},{24,16},{1,25},{9,1},{17,9},{25,17},{2,26},{10... | collective-permute-start | bytes 393224 | tf_op jit(solution)/shard_map/ppermute | solution.py:47
  198.2 16.5 %collective-permute-start.25 = (bf16[2,64,512]{2,1,0:T(8,128)(2,1)S(1)}, bf16[2,64,512]{2,1,0:T(8,128)(2,1)S(1)}, u32[]{:S(2)}, u32[]{:S(2)}) collective-permute-start(bf16[2,64,512]{2,1,0:T(8,128)(2,1)S(1)} %get-tuple-element.67), channel_id=1, source_target_pairs={{0,8},{8,16},{16,24},{24,0},{1,9},{9,17},{17,25},{25,1},{2,10},{10... | collective-permute-start | bytes 393224 | tf_op jit(solution)/shard_map/ppermute | solution.py:47

commit v2 on v1

--- a/solution.py
+++ b/solution.py
@@ -34,6 +34,18 @@
     return pl.BlockSpec()
 
 
+def in_hbm(value):
+    return pltpu.with_memory_space_constraint(value, pltpu.HBM)
+
+
+def in_vmem(value):
+    return pltpu.with_memory_space_constraint(value, pltpu.VMEM)
+
+
+def resident():
+    return pl.BlockSpec(memory_space=pltpu.VMEM)
+
+
 def smem():
     return pl.BlockSpec(memory_space=pltpu.SMEM)
 
@@ -147,7 +159,7 @@
         raised = jnp.exp(scores - jnp.max(scores, axis=0, keepdims=True))
         weights = raised / jnp.sum(raised, axis=0, keepdims=True)
         weight_ref[0, pair] = weights
-        narrow_ref[0, pair] = weights.astype(jnp.bfloat16)
+        narrow_ref[frame, pair] = weights.astype(jnp.bfloat16)
 
 
 def attend_weights(counts, queries, keys):
@@ -155,19 +167,22 @@
         weights_kernel,
         grid=(FRAMES,),
         out_shape=(
-            jax.ShapeDtypeStruct((FRAMES, PAIRS, ROWS, 2 * ROWS), jnp.float32),
-            jax.ShapeDtypeStruct((FRAMES, PAIRS, ROWS, 2 * ROWS), jnp.bfloat16),
+            pltpu.HBM((FRAMES, PAIRS, ROWS, 2 * ROWS), jnp.float32),
+            pltpu.VMEM((FRAMES, PAIRS, ROWS, 2 * ROWS), jnp.bfloat16),
         ),
         in_specs=[
             smem(),
             pl.BlockSpec((ROWS, WIDTH), lambda f: (0, 0)),
             pl.BlockSpec((1, ROWS, WIDTH), lambda f: (f, 0, 0)),
         ],
-        out_specs=(pl.BlockSpec((1, PAIRS, ROWS, 2 * ROWS), lambda f: (f, 0, 0, 0)),) * 2,
+        out_specs=(
+            pl.BlockSpec((1, PAIRS, ROWS, 2 * ROWS), lambda f: (f, 0, 0, 0)),
+            resident(),
+        ),
         scratch_shapes=[pltpu.VMEM((WIDTH, ROWS), jnp.bfloat16)],
-        compiler_params=params(),
+        compiler_params=params(8 * 1024 * 1024),
         name="attend_weights",
-    )(counts, queries, keys)
+    )(counts, queries, in_hbm(keys))
 
 
 def pool_kernel(
@@ -251,11 +266,11 @@
     return pl.pallas_call(
         pool_kernel,
         out_shape=(
-            jax.ShapeDtypeStruct((ROWS, WIDTH), jnp.bfloat16),
-            jax.ShapeDtypeStruct((FRAMES, WIDTH, ROWS), jnp.bfloat16),
-            jax.ShapeDtypeStruct((FRAMES, ROWS, WIDTH), jnp.bfloat16),
+            pltpu.HBM((ROWS, WIDTH), jnp.bfloat16),
+            pltpu.HBM((FRAMES, WIDTH, ROWS), jnp.bfloat16),
+            pltpu.HBM((FRAMES, ROWS, WIDTH), jnp.bfloat16),
         ),
-        in_specs=[smem()] + [whole()] * 6,
+        in_specs=[smem(), resident()] + [whole()] * 5,
         out_specs=(whole(), whole(), whole()),
         scratch_shapes=[
             pltpu.VMEM(wide, jnp.bfloat16),
@@ -267,16 +282,16 @@
             pltpu.VMEM((WIDTH, ROWS), jnp.bfloat16),
             pltpu.VMEM(wide, jnp.float32),
         ],
-        compiler_params=params(),
+        compiler_params=params(18 * 1024 * 1024),
         name="pool_frames",
     )(
         frame_now.reshape(1),
-        weights,
-        values,
-        w_query,
-        w_key,
-        w_value,
-        upstream,
+        in_vmem(weights),
+        in_hbm(values),
+        in_hbm(w_query),
+        in_hbm(w_key),
+        in_hbm(w_value),
+        in_hbm(upstream),
     )
 
 
@@ -309,8 +324,8 @@
         back_kernel,
         grid=(FRAMES,),
         out_shape=(
-            jax.ShapeDtypeStruct((ROWS, WIDTH), jnp.bfloat16),
-            jax.ShapeDtypeStruct((FRAMES, ROWS, WIDTH), jnp.bfloat16),
+            pltpu.HBM((ROWS, WIDTH), jnp.bfloat16),
+            pltpu.HBM((FRAMES, ROWS, WIDTH), jnp.bfloat16),
         ),
         in_specs=[
             fixed,
@@ -324,9 +339,9 @@
             pltpu.VMEM((WIDTH, ROWS), jnp.bfloat16),
             pltpu.VMEM((WIDTH, ROWS), jnp.float32),
         ],
-        compiler_params=params(),
+        compiler_params=params(10 * 1024 * 1024),
         name="attend_back",
-    )(queries, keys, values, weights, grad_traj)
+    )(queries, in_hbm(keys), in_hbm(values), in_hbm(weights), in_hbm(grad_traj))
 
 
 def merge_kernel(place_ref, mine_ref, theirs_ref, *refs):

time: 217 us -> 216 us (level)
  no operation moved by 1% of the time
where the time goes in v2:
time: 216 us; the launch traced here: 215 us
  waiting for transfers between devices  81.1 us (38%)
  starting transfers between devices  80.8 us (37%)
  Pallas kernels  40 us (19%)
  other arithmetic  10.7 us (5%)
    ppermute x36, waiting for transfers between devices, shift(): lax.ppermute(value, axis, [(i, (i + step) % size) for i in range(size)])  66.6 us
    ppermute x36, starting transfers between devices, shift(): lax.ppermute(value, axis, [(i, (i + step) % size) for i in range(size)])  64.2 us
    all_to_all x4, starting transfers between devices, exchange(): lax.all_to_all(chosen.reshape(FRAMES, SLOTS * TILE, WIDTH), TM, split_axi...  16.6 us
    all_to_all x4, waiting for transfers between devices, exchange(): lax.all_to_all(chosen.reshape(FRAMES, SLOTS * TILE, WIDTH), TM, split_axi...  14.5 us
    pallas_call x1, Pallas kernels, attend_back(): pl.pallas_call(back_kernel, grid=(FRAMES,), out_shape=(pltpu.HBM((ROWS, W...  10.5 us
    convert_element_type x8, other arithmetic, add_wide(): return total.astype(jnp.bfloat16)  8.04 us
    pallas_call x2, Pallas kernels, merge_slots(): pl.pallas_call(merge_kernel, out_shape=tuple((jax.ShapeDtypeStruct((n, TI...  7.57 us
    pallas_call x2, Pallas kernels, select_tiles(): pl.pallas_call(select_kernel, out_shape=jax.ShapeDtypeStruct((FRAMES * SL...  7.45 us
  transfers between devices with their start and end apart: 40, of which 19 were waited for; matrix products, arithmetic and copies ran while one was open for 5% of the time, Pallas kernels for 15%

profile of v2, /device:TPU:1, one launch (start us, length us, event | category | flops | bytes accessed | tf_op | source)
XLA Modules:
  0.0 214.6 jit_solution(7735933178536885482)
XLA Ops:
  0.6 3.9 %collective-permute-start.2 = (bf16[2,64,512]{2,1,0:T(8,128)(2,1)}, bf16[2,64,512]{2,1,0:T(8,128)(2,1)S(1)}, u32[]{:S(2)}, u32[]{:S(2)}) collective-permute-start(bf16[2,64,512]{2,1,0:T(8,128)(2,1)} %bitcast.55), channel_id=1, source_target_pairs={{0,8},{8,16},{16,24},{24,0},{1,9},{9,17},{17,25},{25,1},{2,10},{10... | collective-permute-start | bytes 393224 | tf_op jit(solution)/shard_map/ppermute | solution.py:59
  4.5 5.1 %collective-permute-start.1 = (bf16[2,64,512]{2,1,0:T(8,128)(2,1)}, bf16[2,64,512]{2,1,0:T(8,128)(2,1)S(1)}, u32[]{:S(2)}, u32[]{:S(2)}) collective-permute-start(bf16[2,64,512]{2,1,0:T(8,128)(2,1)} %bitcast.56), channel_id=1, source_target_pairs={{0,16},{8,24},{16,0},{24,8},{1,17},{9,25},{17,1},{25,9},{2,18},{10... | collective-permute-start | bytes 393224 | tf_op jit(solution)/shard_map/ppermute | solution.py:59
  9.7 2.4 %collective-permute-start = (bf16[2,64,512]{2,1,0:T(8,128)(2,1)}, bf16[2,64,512]{2,1,0:T(8,128)(2,1)S(1)}, u32[]{:S(2)}, u32[]{:S(2)}) collective-permute-start(bf16[2,64,512]{2,1,0:T(8,128)(2,1)} %bitcast.57), channel_id=1, source_target_pairs={{0,24},{8,0},{16,8},{24,16},{1,25},{9,1},{17,9},{25,17},{2,26},{10... | collective-permute-start | bytes 393224 | tf_op jit(solution)/shard_map/ppermute | solution.py:59
  12.0 6.4 %collective-permute-done.1 = bf16[2,64,512]{2,1,0:T(8,128)(2,1)S(1)} collective-permute-done((bf16[2,64,512]{2,1,0:T(8,128)(2,1)}, bf16[2,64,512]{2,1,0:T(8,128)(2,1)S(1)}, u32[]{:S(2)}, u32[]{:S(2)}) %collective-permute-start.1) | collective-permute-done | bytes 131104 | tf_op jit(solution)/shard_map/ppermute | solution.py:59
  18.5 4.3 %collective-permute-done = bf16[2,64,512]{2,1,0:T(8,128)(2,1)S(1)} collective-permute-done((bf16[2,64,512]{2,1,0:T(8,128)(2,1)}, bf16[2,64,512]{2,1,0:T(8,128)(2,1)S(1)}, u32[]{:S(2)}, u32[]{:S(2)}) %collective-permute-start) | collective-permute-done | bytes 131104 | tf_op jit(solution)/shard_map/ppermute | solution.py:59
  22.8 1.0 pad_maximum_fusion.refs_0_
  23.8 1.3 collective-permute-start.5
  25.1 2.5 %collective-permute-start.4 = (bf16[8,64,512]{2,1,0:T(8,128)(2,1)S(1)}, bf16[8,64,512]{2,1,0:T(8,128)(2,1)S(1)}, u32[]{:S(2)}, u32[]{:S(2)}) collective-permute-start(bf16[8,64,512]{2,1,0:T(8,128)(2,1)S(1)} %pad_maximum_fusion.refs_0_), channel_id=1, source_target_pairs={{0,4},{2,6},{4,0},{6,2},{1,5},{3,7},{5,1},{7,3},{8,12},{10,14},{12... | collective-permute-start | bytes 1572872 | tf_op jit(solution)/shard_map/ppermute | solution.py:59
  27.5 1.2 collective-permute-start.3
  28.7 0.9 collective-permute-start.8
  29.6 4.5 %collective-permute-start.7 = (bf16[2,64,512]{2,1,0:T(8,128)(2,1)}, bf16[2,64,512]{2,1,0:T(8,128)(2,1)S(1)}, u32[]{:S(2)}, u32[]{:S(2)}) collective-permute-start(bf16[2,64,512]{2,1,0:T(8,128)(2,1)} %bitcast.60), channel_id=1, source_target_pairs={{0,16},{8,24},{16,0},{24,8},{1,17},{9,25},{17,1},{25,9},{2,18},{10... | collective-permute-start | bytes 393224 | tf_op jit(solution)/shard_map/ppermute | solution.py:59
  34.1 2.5 %collective-permute-done.8 = bf16[2,64,512]{2,1,0:T(8,128)(2,1)S(1)} collective-permute-done((bf16[2,64,512]{2,1,0:T(8,128)(2,1)}, bf16[2,64,512]{2,1,0:T(8,128)(2,1)S(1)}, u32[]{:S(2)}, u32[]{:S(2)}) %collective-permute-start.8) | collective-permute-done | bytes 131104 | tf_op jit(solution)/shard_map/ppermute | solution.py:59
  36.6 1.3 collective-permute-start.6
  37.8 3.7 %collective-permute-done.7 = bf16[2,64,512]{2,1,0:T(8,128)(2,1)S(1)} collective-permute-done((bf16[2,64,512]{2,1,0:T(8,128)(2,1)}, bf16[2,64,512]{2,1,0:T(8,128)(2,1)S(1)}, u32[]{:S(2)}, u32[]{:S(2)}) %collective-permute-start.7) | collective-permute-done | bytes 131104 | tf_op jit(solution)/shard_map/ppermute | solution.py:59
  41.6 2.2 %collective-permute-start.9 = (bf16[8,64,512]{2,1,0:T(8,128)(2,1)S(1)}, bf16[8,64,512]{2,1,0:T(8,128)(2,1)}, u32[]{:S(2)}, u32[]{:S(2)}) collective-permute-start(bf16[8,64,512]{2,1,0:T(8,128)(2,1)S(1)} %pad_maximum_fusion.refs_0_), channel_id=1, source_target_pairs={{0,1},{1,0},{2,3},{3,2},{4,5},{5,4},{6,7},{7,6},{8,9},{9,8},{10,11... | collective-permute-start | bytes 1572872 | tf_op jit(solution)/shard_map/ppermute | solution.py:59
  43.8 1.0 pad_maximum_fusion.1.refs_0_
  44.8 5.5 %collective-permute-done.4.refs_2_ = bf16[8,64,512]{2,1,0:T(8,128)(2,1)S(1)} collective-permute-done((bf16[8,64,512]{2,1,0:T(8,128)(2,1)S(1)}, bf16[8,64,512]{2,1,0:T(8,128)(2,1)S(1)}, u32[]{:S(2)}, u32[]{:S(2)}) %collective-permute-start.4) | collective-permute-done | bytes 524320 | tf_op jit(solution)/shard_map/ppermute | solution.py:59
  50.3 1.3 collective-permute-start.10
  52.4 1.1 collective-permute-start.15
  53.5 2.1 collective-permute-start.14
  55.6 1.3 collective-permute-start.13
  57.0 3.5 %select_tiles.2 = bf16[16,64,512]{2,1,0:T(8,128)(2,1)} custom-call(s32[16]{0:T(128)S(1)} %fusion.2.piece_ref, s32[16]{0:T(128)S(1)} %get-tuple-element.59.row_ref, bf16[8,64,512]{2,1,0:T(8,128)(2,1)S(1)} %pad_maximum_fusion.refs_0_, bf16[8,64,512]{2,1,0:T(8,128)(2,1)S(1)} %collective-permute-done.3.refs_1_, ...), custom_call_target="tpu_custom_call" | custom-call | tf_op jit(solution)/shard_map/select_tiles/pallas_call | solution.py:109
  60.5 4.4 %all-to-all-start = ((bf16[8,128,512]{2,1,0:T(8,128)(2,1)}), bf16[8,128,512]{2,1,0:T(8,128)(2,1)S(1)}, u32[]{:S(2)}, u32[]{:S(2)}) async-start(bf16[8,128,512]{2,1,0:T(8,128)(2,1)} %bitcast.9), calls=%async_computation | async-start | bytes 2097152 | tf_op jit(solution)/shard_map/all_to_all | solution.py:455
  64.9 0.8 collective-permute-start.16
  65.7 1.5 collective-permute-done.15.refs_3_
  67.2 0.9 collective-permute-start.19
  68.1 10.8 %collective-permute-done.14.refs_2_ = bf16[8,64,512]{2,1,0:T(8,128)(2,1)} collective-permute-done((bf16[8,64,512]{2,1,0:T(8,128)(2,1)S(1)}, bf16[8,64,512]{2,1,0:T(8,128)(2,1)}, u32[]{:S(2)}, u32[]{:S(2)}) %collective-permute-start.14) | collective-permute-done | bytes 524320 | tf_op jit(solution)/shard_map/ppermute | solution.py:59
  78.9 0.9 collective-permute-start.18
  79.9 1.6 collective-permute-done.18.refs_6_
  82.3 3.9 %select_tiles.3 = bf16[16,64,512]{2,1,0:T(8,128)(2,1)} custom-call(s32[16]{0:T(128)S(1)} %fusion.2.piece_ref, s32[16]{0:T(128)S(1)} %get-tuple-element.59.row_ref, bf16[8,64,512]{2,1,0:T(8,128)(2,1)S(1)} %pad_maximum_fusion.1.refs_0_, bf16[8,64,512]{2,1,0:T(8,128)(2,1)} %collective-permute-done.13.refs_1_, ...), custom_call_target="tpu_custom_call" | custom-call | flops 12999999488 | tf_op jit(solution)/shard_map/select_tiles/pallas_call | solution.py:109
  86.3 4.3 %all-to-all-start.1 = ((bf16[8,128,512]{2,1,0:T(8,128)(2,1)}), bf16[8,128,512]{2,1,0:T(8,128)(2,1)}, u32[]{:S(2)}, u32[]{:S(2)}) async-start(bf16[8,128,512]{2,1,0:T(8,128)(2,1)} %bitcast.10), calls=%async_computation.1 | async-start | bytes 2097152 | tf_op jit(solution)/shard_map/all_to_all | solution.py:455
  90.5 0.9 dynamic-slice_reduce_fusion.count_ref
  91.4 7.2 %attend_weights.1 = (f32[8,4,128,256]{3,2,1,0:T(8,128)}, bf16[8,4,128,256]{3,2,1,0:T(8,128)(2,1)S(1)}) custom-call(s32[8]{0:T(128)S(1)} %dynamic-slice_reduce_fusion.count_ref, bf16[128,512]{1,0:T(8,128)(2,1)S(1)} %bitcast.48, bf16[8,128,512]{2,1,0:T(8,128)(2,1)} %copy-done.2), custom_call_target="tpu_custom_call" | custom-call | tf_op jit(solution)/shard_map/attend_weights/pallas_call | solution.py:166
  98.7 6.8 %all-to-all-done.1.value_ref = bf16[8,128,512]{2,1,0:T(8,128)(2,1)} async-done(((bf16[8,128,512]{2,1,0:T(8,128)(2,1)}), bf16[8,128,512]{2,1,0:T(8,128)(2,1)}, u32[]{:S(2)}, u32[]{:S(2)}) %all-to-all-start.1) | async-done | bytes 1048608 | tf_op jit(solution)/shard_map/all_to_all | solution.py:455
  105.5 7.2 %pool_frames.1 = (bf16[128,512]{1,0:T(8,128)(2,1)}, bf16[8,512,128]{2,1,0:T(8,128)(2,1)}, bf16[8,128,512]{2,1,0:T(8,128)(2,1)}) custom-call(s32[1]{0:T(128)} %bitcast.frame_ref, bf16[8,4,128,256]{3,2,1,0:T(8,128)(2,1)S(1)} %get-tuple-element.34.weight_ref, bf16[8,128,512]{2,1,0:T(8,128)(2,1)} %all-to-all-done.1.value_ref, bf16[512,512]{1,0:T(8,128)(2,1)} %wq_ref.1, ...), custom_call_target="tpu_custom_call" | custom-call | tf_op jit(solution)/shard_map/pool_frames/pallas_call | solution.py:266
  112.6 3.7 %all-to-all-start.3 = ((bf16[8,128,512]{2,1,0:T(8,128)(2,1)}), bf16[8,128,512]{2,1,0:T(8,128)(2,1)S(1)}, u32[]{:S(2)}, u32[]{:S(2)}) async-start(bf16[8,128,512]{2,1,0:T(8,128)(2,1)} %get-tuple-element.40), calls=%async_computation.3 | async-start | bytes 2097152 | tf_op jit(solution)/shard_map/all_to_all | solution.py:455
  116.3 10.5 %attend_back.1 = (bf16[128,512]{1,0:T(8,128)(2,1)}, bf16[8,128,512]{2,1,0:T(8,128)(2,1)}) custom-call(bf16[128,512]{1,0:T(8,128)(2,1)S(1)} %bitcast.49, bf16[8,128,512]{2,1,0:T(8,128)(2,1)} %copy-done.2, bf16[8,128,512]{2,1,0:T(8,128)(2,1)} %all-to-all-done.1.value_ref, f32[8,4,128,256]{3,2,1,0:T(8,128)} %get-tuple-element.36.weight_ref, ...), custom_call_target="tpu_custom_call" | custom-call | tf_op jit(solution)/shard_map/attend_back/pallas_call | solution.py:323
  126.9 3.5 %all-to-all-done.3 = bf16[8,128,512]{2,1,0:T(8,128)(2,1)S(1)} async-done(((bf16[8,128,512]{2,1,0:T(8,128)(2,1)}), bf16[8,128,512]{2,1,0:T(8,128)(2,1)S(1)}, u32[]{:S(2)}, u32[]{:S(2)}) %all-to-all-start.3) | async-done | bytes 1048608 | tf_op jit(solution)/shard_map/all_to_all | solution.py:455
  130.3 4.3 %all-to-all-start.2 = ((bf16[8,128,512]{2,1,0:T(8,128)(2,1)}), bf16[8,128,512]{2,1,0:T(8,128)(2,1)}, u32[]{:S(2)}, u32[]{:S(2)}) async-start(bf16[8,128,512]{2,1,0:T(8,128)(2,1)} %get-tuple-element.39), calls=%async_computation.2 | async-start | bytes 2097152 | tf_op jit(solution)/shard_map/all_to_all | solution.py:455
  134.6 2.7 %collective-permute-start.20 = (bf16[16,64,512]{2,1,0:T(8,128)(2,1)S(1)}, bf16[16,64,512]{2,1,0:T(8,128)(2,1)}, u32[]{:S(2)}, u32[]{:S(2)}) collective-permute-start(bf16[16,64,512]{2,1,0:T(8,128)(2,1)S(1)} %bitcast.50), channel_id=1, source_target_pairs={{0,1},{1,0},{2,3},{3,2},{4,5},{5,4},{6,7},{7,6},{8,9},{9,8},{10,11... | collective-permute-start | bytes 3145736 | tf_op jit(solution)/shard_map/ppermute | solution.py:59
  138.1 1.7 collective-permute-done.20.theirs_ref
  139.8 3.8 %merge_slots.2 = (bf16[8,64,512]{2,1,0:T(8,128)(2,1)}, bf16[8,64,512]{2,1,0:T(8,128)(2,1)}, bf16[4,64,512]{2,1,0:T(8,128)(2,1)}, bf16[4,64,512]{2,1,0:T(8,128)(2,1)}, bf16[8,64,512]{2,1,0:T(8,128)(2,1)}) custom-call(s32[32]{0:T(128)} %pad_add_fusion.place_ref, bf16[16,64,512]{2,1,0:T(8,128)(2,1)} %bitcast.51, ...), custom_call_target="tpu_custom_call" | custom-call | tf_op jit(solution)/shard_map/merge_slots/pallas_call | solution.py:369
  143.6 4.2 %all-to-all-done.2 = bf16[8,128,512]{2,1,0:T(8,128)(2,1)} async-done(((bf16[8,128,512]{2,1,0:T(8,128)(2,1)}), bf16[8,128,512]{2,1,0:T(8,128)(2,1)}, u32[]{:S(2)}, u32[]{:S(2)}) %all-to-all-start.2) | async-done | bytes 1048608 | tf_op jit(solution)/shard_map/all_to_all | solution.py:455
  147.8 3.6 %collective-permute-start.21 = (bf16[16,64,512]{2,1,0:T(8,128)(2,1)}, bf16[16,64,512]{2,1,0:T(8,128)(2,1)}, u32[]{:S(2)}, u32[]{:S(2)}) collective-permute-start(bf16[16,64,512]{2,1,0:T(8,128)(2,1)} %bitcast.16.mine_ref), channel_id=1, source_target_pairs={{0,1},{1,0},{2,3},{3,2},{4,5},{5,4},{6,7},{7,6},{8,9},{9,8},{10,11... | collective-permute-start | bytes 3145736 | tf_op jit(solution)/shard_map/ppermute | solution.py:59
  152.1 1.9 collective-permute-start.30
  154.0 3.8 %merge_slots.3 = (bf16[8,64,512]{2,1,0:T(8,128)(2,1)}, bf16[8,64,512]{2,1,0:T(8,128)(2,1)}, bf16[4,64,512]{2,1,0:T(8,128)(2,1)}, bf16[4,64,512]{2,1,0:T(8,128)(2,1)}, bf16[8,64,512]{2,1,0:T(8,128)(2,1)}) custom-call(s32[32]{0:T(128)} %pad_add_fusion.place_ref, bf16[16,64,512]{2,1,0:T(8,128)(2,1)} %bitcast.16.mine_ref, ...), custom_call_target="tpu_custom_call" | custom-call | tf_op jit(solution)/shard_map/merge_slots/pallas_call | solution.py:369
  157.8 2.1 collective-permute-start.22
  159.9 6.5 %collective-permute-done.29 = bf16[8,64,512]{2,1,0:T(8,128)(2,1)} collective-permute-done((bf16[8,64,512]{2,1,0:T(8,128)(2,1)}, bf16[8,64,512]{2,1,0:T(8,128)(2,1)}, u32[]{:S(2)}, u32[]{:S(2)}) %collective-permute-start.29) | collective-permute-done | bytes 524320 | tf_op jit(solution)/shard_map/ppermute | solution.py:59
  166.4 1.0 add_convert_fusion
  167.5 2.3 %collective-permute-start.33 = (bf16[4,64,512]{2,1,0:T(8,128)(2,1)S(1)}, bf16[4,64,512]{2,1,0:T(8,128)(2,1)S(1)}, u32[]{:S(2)}, u32[]{:S(2)}) collective-permute-start(bf16[4,64,512]{2,1,0:T(8,128)(2,1)S(1)} %add_convert_fusion), channel_id=1, source_target_pairs={{0,6},{2,0},{4,2},{6,4},{1,7},{3,1},{5,3},{7,5},{8,14},{10,8},{12,... | collective-permute-start | bytes 786440 | tf_op jit(solution)/shard_map/ppermute | solution.py:59
  169.8 1.1 add_convert_fusion.1
  171.0 5.8 %collective-permute-done.22 = bf16[8,64,512]{2,1,0:T(8,128)(2,1)S(1)} collective-permute-done((bf16[8,64,512]{2,1,0:T(8,128)(2,1)}, bf16[8,64,512]{2,1,0:T(8,128)(2,1)S(1)}, u32[]{:S(2)}, u32[]{:S(2)}) %collective-permute-start.22) | collective-permute-done | bytes 524320 | tf_op jit(solution)/shard_map/ppermute | solution.py:59
  176.8 1.0 add_convert_fusion.2
  177.8 3.2 %collective-permute-start.26 = (bf16[4,64,512]{2,1,0:T(8,128)(2,1)S(1)}, bf16[4,64,512]{2,1,0:T(8,128)(2,1)S(1)}, u32[]{:S(2)}, u32[]{:S(2)}) collective-permute-start(bf16[4,64,512]{2,1,0:T(8,128)(2,1)S(1)} %add_convert_fusion.2), channel_id=1, source_target_pairs={{0,6},{2,0},{4,2},{6,4},{1,7},{3,1},{5,3},{7,5},{8,14},{10,8},{12,... | collective-permute-start | bytes 786440 | tf_op jit(solution)/shard_map/ppermute | solution.py:59
  181.0 1.0 add_convert_fusion.3
  183.2 1.3 add_convert_fusion.6
  184.5 3.7 %collective-permute-start.34 = (bf16[2,64,512]{2,1,0:T(8,128)(2,1)S(1)}, bf16[2,64,512]{2,1,0:T(8,128)(2,1)S(1)}, u32[]{:S(2)}, u32[]{:S(2)}) collective-permute-start(bf16[2,64,512]{2,1,0:T(8,128)(2,1)S(1)} %get-tuple-element.62), channel_id=1, source_target_pairs={{0,16},{8,24},{16,0},{24,8},{1,17},{9,25},{17,1},{25,9},{2,18},{10... | collective-permute-start | bytes 393224 | tf_op jit(solution)/shard_map/ppermute | solution.py:59
  188.2 1.1 collective-permute-start.35
  189.3 1.2 collective-permute-start.32
  190.7 3.1 %collective-permute-start.27 = (bf16[2,64,512]{2,1,0:T(8,128)(2,1)S(1)}, bf16[2,64,512]{2,1,0:T(8,128)(2,1)S(1)}, u32[]{:S(2)}, u32[]{:S(2)}) collective-permute-start(bf16[2,64,512]{2,1,0:T(8,128)(2,1)S(1)} %get-tuple-element.64), channel_id=1, source_target_pairs={{0,16},{8,24},{16,0},{24,8},{1,17},{9,25},{17,1},{25,9},{2,18},{10... | collective-permute-start | bytes 393224 | tf_op jit(solution)/shard_map/ppermute | solution.py:59
  193.8 3.6 %collective-permute-start.28 = (bf16[2,64,512]{2,1,0:T(8,128)(2,1)S(1)}, bf16[2,64,512]{2,1,0:T(8,128)(2,1)S(1)}, u32[]{:S(2)}, u32[]{:S(2)}) collective-permute-start(bf16[2,64,512]{2,1,0:T(8,128)(2,1)S(1)} %get-tuple-element.65), channel_id=1, source_target_pairs={{0,24},{8,0},{16,8},{24,16},{1,25},{9,1},{17,9},{25,17},{2,26},{10... | collective-permute-start | bytes 393224 | tf_op jit(solution)/shard_map/ppermute | solution.py:59
  197.9 13.1 %collective-permute-done.35 = bf16[2,64,512]{2,1,0:T(8,128)(2,1)S(1)} collective-permute-done((bf16[2,64,512]{2,1,0:T(8,128)(2,1)S(1)}, bf16[2,64,512]{2,1,0:T(8,128)(2,1)S(1)}, u32[]{:S(2)}, u32[]{:S(2)}) %collective-permute-start.35) | collective-permute-done | bytes 131104 | tf_op jit(solution)/shard_map/ppermute | solution.py:59
  211.0 1.7 add_convert_fusion.4
  212.7 1.1 collective-permute-done.28
  (52 shorter events, 5.9 us)
Async XLA Ops:
  0.6 51.0 %copy-start = (s32[8,32,8,2]{1,3,2,0:T(2,128)S(1)}, s32[8,32,8,2]{1,3,2,0:T(2,128)}, u32[]{:S(2)}) copy-start(s32[8,32,8,2]{1,3,2,0:T(2,128)} %param.16) | copy-start | bytes 49156
  0.6 11.4 %collective-permute-start.2 = (bf16[2,64,512]{2,1,0:T(8,128)(2,1)}, bf16[2,64,512]{2,1,0:T(8,128)(2,1)S(1)}, u32[]{:S(2)}, u32[]{:S(2)}) collective-permute-start(bf16[2,64,512]{2,1,0:T(8,128)(2,1)} %bitcast.55), channel_id=1, source_target_pairs={{0,8},{8,16},{16,24},{24,0},{1,9},{9,17},{17,25},{25,1},{2,10},{10... | collective-permute-start | bytes 393224 | tf_op jit(solution)/shard_map/ppermute | solution.py:59
  4.5 13.9 %collective-permute-start.1 = (bf16[2,64,512]{2,1,0:T(8,128)(2,1)}, bf16[2,64,512]{2,1,0:T(8,128)(2,1)S(1)}, u32[]{:S(2)}, u32[]{:S(2)}) collective-permute-start(bf16[2,64,512]{2,1,0:T(8,128)(2,1)} %bitcast.56), channel_id=1, source_target_pairs={{0,16},{8,24},{16,0},{24,8},{1,17},{9,25},{17,1},{25,9},{2,18},{10... | collective-permute-start | bytes 393224 | tf_op jit(solution)/shard_map/ppermute | solution.py:59
  9.7 13.1 %collective-permute-start = (bf16[2,64,512]{2,1,0:T(8,128)(2,1)}, bf16[2,64,512]{2,1,0:T(8,128)(2,1)S(1)}, u32[]{:S(2)}, u32[]{:S(2)}) collective-permute-start(bf16[2,64,512]{2,1,0:T(8,128)(2,1)} %bitcast.57), channel_id=1, source_target_pairs={{0,24},{8,0},{16,8},{24,16},{1,25},{9,1},{17,9},{25,17},{2,26},{10... | collective-permute-start | bytes 393224 | tf_op jit(solution)/shard_map/ppermute | solution.py:59
  23.8 21.0 %collective-permute-start.5 = (bf16[8,64,512]{2,1,0:T(8,128)(2,1)S(1)}, bf16[8,64,512]{2,1,0:T(8,128)(2,1)S(1)}, u32[]{:S(2)}, u32[]{:S(2)}) collective-permute-start(bf16[8,64,512]{2,1,0:T(8,128)(2,1)S(1)} %pad_maximum_fusion.refs_0_), channel_id=1, source_target_pairs={{0,2},{2,4},{4,6},{6,0},{1,3},{3,5},{5,7},{7,1},{8,10},{10,12},{12... | collective-permute-start | bytes 1572872 | tf_op jit(solution)/shard_map/ppermute | solution.py:59
  25.1 25.2 %collective-permute-start.4 = (bf16[8,64,512]{2,1,0:T(8,128)(2,1)S(1)}, bf16[8,64,512]{2,1,0:T(8,128)(2,1)S(1)}, u32[]{:S(2)}, u32[]{:S(2)}) collective-permute-start(bf16[8,64,512]{2,1,0:T(8,128)(2,1)S(1)} %pad_maximum_fusion.refs_0_), channel_id=1, source_target_pairs={{0,4},{2,6},{4,0},{6,2},{1,5},{3,7},{5,1},{7,3},{8,12},{10,14},{12... | collective-permute-start | bytes 1572872 | tf_op jit(solution)/shard_map/ppermute | solution.py:59
  27.5 22.8 %collective-permute-start.3 = (bf16[8,64,512]{2,1,0:T(8,128)(2,1)S(1)}, bf16[8,64,512]{2,1,0:T(8,128)(2,1)S(1)}, u32[]{:S(2)}, u32[]{:S(2)}) collective-permute-start(bf16[8,64,512]{2,1,0:T(8,128)(2,1)S(1)} %pad_maximum_fusion.refs_0_), channel_id=1, source_target_pairs={{0,6},{2,0},{4,2},{6,4},{1,7},{3,1},{5,3},{7,5},{8,14},{10,8},{12,... | collective-permute-start | bytes 1572872 | tf_op jit(solution)/shard_map/ppermute | solution.py:59
  28.7 7.9 %collective-permute-start.8 = (bf16[2,64,512]{2,1,0:T(8,128)(2,1)}, bf16[2,64,512]{2,1,0:T(8,128)(2,1)S(1)}, u32[]{:S(2)}, u32[]{:S(2)}) collective-permute-start(bf16[2,64,512]{2,1,0:T(8,128)(2,1)} %bitcast.59), channel_id=1, source_target_pairs={{0,8},{8,16},{16,24},{24,0},{1,9},{9,17},{17,25},{25,1},{2,10},{10... | collective-permute-start | bytes 393224 | tf_op jit(solution)/shard_map/ppermute | solution.py:59
  29.6 12.0 %collective-permute-start.7 = (bf16[2,64,512]{2,1,0:T(8,128)(2,1)}, bf16[2,64,512]{2,1,0:T(8,128)(2,1)S(1)}, u32[]{:S(2)}, u32[]{:S(2)}) collective-permute-start(bf16[2,64,512]{2,1,0:T(8,128)(2,1)} %bitcast.60), channel_id=1, source_target_pairs={{0,16},{8,24},{16,0},{24,8},{1,17},{9,25},{17,1},{25,9},{2,18},{10... | collective-permute-start | bytes 393224 | tf_op jit(solution)/shard_map/ppermute | solution.py:59
  36.6 7.2 %collective-permute-start.6 = (bf16[2,64,512]{2,1,0:T(8,128)(2,1)}, bf16[2,64,512]{2,1,0:T(8,128)(2,1)S(1)}, u32[]{:S(2)}, u32[]{:S(2)}) collective-permute-start(bf16[2,64,512]{2,1,0:T(8,128)(2,1)} %bitcast.61), channel_id=1, source_target_pairs={{0,24},{8,0},{16,8},{24,16},{1,25},{9,1},{17,9},{25,17},{2,26},{10... | collective-permute-start | bytes 393224 | tf_op jit(solution)/shard_map/ppermute | solution.py:59
  41.6 11.9 %collective-permute-start.9 = (bf16[8,64,512]{2,1,0:T(8,128)(2,1)S(1)}, bf16[8,64,512]{2,1,0:T(8,128)(2,1)}, u32[]{:S(2)}, u32[]{:S(2)}) collective-permute-start(bf16[8,64,512]{2,1,0:T(8,128)(2,1)S(1)} %pad_maximum_fusion.refs_0_), channel_id=1, source_target_pairs={{0,1},{1,0},{2,3},{3,2},{4,5},{5,4},{6,7},{7,6},{8,9},{9,8},{10,11... | collective-permute-start | bytes 1572872 | tf_op jit(solution)/shard_map/ppermute | solution.py:59
  50.3 5.3 %collective-permute-start.10 = (bf16[8,64,512]{2,1,0:T(8,128)(2,1)S(1)}, bf16[8,64,512]{2,1,0:T(8,128)(2,1)}, u32[]{:S(2)}, u32[]{:S(2)}) collective-permute-start(bf16[8,64,512]{2,1,0:T(8,128)(2,1)S(1)} %collective-permute-done.3.refs_1_), channel_id=1, source_target_pairs={{0,1},{1,0},{2,3},{3,2},{4,5},{5,4},{6,7},{7,6},{8,9},{9,8},{10,11... | collective-permute-start | bytes 1572872 | tf_op jit(solution)/shard_map/ppermute | solution.py:59
  51.7 5.2 %collective-permute-start.11 = (bf16[8,64,512]{2,1,0:T(8,128)(2,1)S(1)}, bf16[8,64,512]{2,1,0:T(8,128)(2,1)}, u32[]{:S(2)}, u32[]{:S(2)}) collective-permute-start(bf16[8,64,512]{2,1,0:T(8,128)(2,1)S(1)} %collective-permute-done.4.refs_2_), channel_id=1, source_target_pairs={{0,1},{1,0},{2,3},{3,2},{4,5},{5,4},{6,7},{7,6},{8,9},{9,8},{10,11... | collective-permute-start | bytes 1572872 | tf_op jit(solution)/shard_map/ppermute | solution.py:59
  51.7 5.2 %collective-permute-start.12 = (bf16[8,64,512]{2,1,0:T(8,128)(2,1)S(1)}, bf16[8,64,512]{2,1,0:T(8,128)(2,1)}, u32[]{:S(2)}, u32[]{:S(2)}) collective-permute-start(bf16[8,64,512]{2,1,0:T(8,128)(2,1)S(1)} %collective-permute-done.5.refs_3_), channel_id=1, source_target_pairs={{0,1},{1,0},{2,3},{3,2},{4,5},{5,4},{6,7},{7,6},{8,9},{9,8},{10,11... | collective-permute-start | bytes 1572872 | tf_op jit(solution)/shard_map/ppermute | solution.py:59
  52.4 14.8 %collective-permute-start.15 = (bf16[8,64,512]{2,1,0:T(8,128)(2,1)S(1)}, bf16[8,64,512]{2,1,0:T(8,128)(2,1)}, u32[]{:S(2)}, u32[]{:S(2)}) collective-permute-start(bf16[8,64,512]{2,1,0:T(8,128)(2,1)S(1)} %pad_maximum_fusion.1.refs_0_), channel_id=1, source_target_pairs={{0,2},{2,4},{4,6},{6,0},{1,3},{3,5},{5,7},{7,1},{8,10},{10,12},{12... | collective-permute-start | bytes 1572872 | tf_op jit(solution)/shard_map/ppermute | solution.py:59
  53.5 25.4 %collective-permute-start.14 = (bf16[8,64,512]{2,1,0:T(8,128)(2,1)S(1)}, bf16[8,64,512]{2,1,0:T(8,128)(2,1)}, u32[]{:S(2)}, u32[]{:S(2)}) collective-permute-start(bf16[8,64,512]{2,1,0:T(8,128)(2,1)S(1)} %pad_maximum_fusion.1.refs_0_), channel_id=1, source_target_pairs={{0,4},{2,6},{4,0},{6,2},{1,5},{3,7},{5,1},{7,3},{8,12},{10,14},{12... | collective-permute-start | bytes 1572872 | tf_op jit(solution)/shard_map/ppermute | solution.py:59
  55.6 24.2 %collective-permute-start.13 = (bf16[8,64,512]{2,1,0:T(8,128)(2,1)S(1)}, bf16[8,64,512]{2,1,0:T(8,128)(2,1)}, u32[]{:S(2)}, u32[]{:S(2)}) collective-permute-start(bf16[8,64,512]{2,1,0:T(8,128)(2,1)S(1)} %pad_maximum_fusion.1.refs_0_), channel_id=1, source_target_pairs={{0,6},{2,0},{4,2},{6,4},{1,7},{3,1},{5,3},{7,5},{8,14},{10,8},{12,... | collective-permute-start | bytes 1572872 | tf_op jit(solution)/shard_map/ppermute | solution.py:59
  60.5 25.8 %all-to-all-start = ((bf16[8,128,512]{2,1,0:T(8,128)(2,1)}), bf16[8,128,512]{2,1,0:T(8,128)(2,1)S(1)}, u32[]{:S(2)}, u32[]{:S(2)}) async-start(bf16[8,128,512]{2,1,0:T(8,128)(2,1)} %bitcast.9), calls=%async_computation | async-start | bytes 2097152 | tf_op jit(solution)/shard_map/all_to_all | solution.py:455
  64.9 26.5 %copy-start.1 = (bf16[1,128,512]{2,1,0:T(8,128)(2,1)S(1)}, bf16[1,128,512]{2,1,0:T(8,128)(2,1)}, u32[]{:S(2)}) copy-start(bf16[1,128,512]{2,1,0:T(8,128)(2,1)} %param.9) | copy-start | bytes 393220
  64.9 15.1 %collective-permute-start.16 = (bf16[8,64,512]{2,1,0:T(8,128)(2,1)S(1)}, bf16[8,64,512]{2,1,0:T(8,128)(2,1)S(1)}, u32[]{:S(2)}, u32[]{:S(2)}) collective-permute-start(bf16[8,64,512]{2,1,0:T(8,128)(2,1)S(1)} %pad_maximum_fusion.1.refs_0_), channel_id=1, source_target_pairs={{0,1},{1,0},{2,3},{3,2},{4,5},{5,4},{6,7},{7,6},{8,9},{9,8},{10,11... | collective-permute-start | bytes 1572872 | tf_op jit(solution)/shard_map/ppermute | solution.py:59
  67.2 12.7 %collective-permute-start.19 = (bf16[8,64,512]{2,1,0:T(8,128)(2,1)}, bf16[8,64,512]{2,1,0:T(8,128)(2,1)S(1)}, u32[]{:S(2)}, u32[]{:S(2)}) collective-permute-start(bf16[8,64,512]{2,1,0:T(8,128)(2,1)} %collective-permute-done.15.refs_3_), channel_id=1, source_target_pairs={{0,1},{1,0},{2,3},{3,2},{4,5},{5,4},{6,7},{7,6},{8,9},{9,8},{10,11... | collective-permute-start | bytes 1572872 | tf_op jit(solution)/shard_map/ppermute | solution.py:59
  78.9 2.6 %collective-permute-start.18 = (bf16[8,64,512]{2,1,0:T(8,128)(2,1)}, bf16[8,64,512]{2,1,0:T(8,128)(2,1)S(1)}, u32[]{:S(2)}, u32[]{:S(2)}) collective-permute-start(bf16[8,64,512]{2,1,0:T(8,128)(2,1)} %collective-permute-done.14.refs_2_), channel_id=1, source_target_pairs={{0,1},{1,0},{2,3},{3,2},{4,5},{5,4},{6,7},{7,6},{8,9},{9,8},{10,11... | collective-permute-start | bytes 1572872 | tf_op jit(solution)/shard_map/ppermute | solution.py:59
  79.8 2.5 %collective-permute-start.17 = (bf16[8,64,512]{2,1,0:T(8,128)(2,1)}, bf16[8,64,512]{2,1,0:T(8,128)(2,1)S(1)}, u32[]{:S(2)}, u32[]{:S(2)}) collective-permute-start(bf16[8,64,512]{2,1,0:T(8,128)(2,1)} %collective-permute-done.13.refs_1_), channel_id=1, source_target_pairs={{0,1},{1,0},{2,3},{3,2},{4,5},{5,4},{6,7},{7,6},{8,9},{9,8},{10,11... | collective-permute-start | bytes 1572872 | tf_op jit(solution)/shard_map/ppermute | solution.py:59
  86.3 5.2 %copy-start.2 = (bf16[8,128,512]{2,1,0:T(8,128)(2,1)}, bf16[8,128,512]{2,1,0:T(8,128)(2,1)S(1)}, u32[]{:S(2)}) copy-start(bf16[8,128,512]{2,1,0:T(8,128)(2,1)S(1)} %all-to-all-done.key_ref) | copy-start | bytes 3145732
  86.3 19.2 %all-to-all-start.1 = ((bf16[8,128,512]{2,1,0:T(8,128)(2,1)}), bf16[8,128,512]{2,1,0:T(8,128)(2,1)}, u32[]{:S(2)}, u32[]{:S(2)}) async-start(bf16[8,128,512]{2,1,0:T(8,128)(2,1)} %bitcast.10), calls=%async_computation.1 | async-start | bytes 2097152 | tf_op jit(solution)/shard_map/all_to_all | solution.py:455
  112.6 17.7 %all-to-all-start.3 = ((bf16[8,128,512]{2,1,0:T(8,128)(2,1)}), bf16[8,128,512]{2,1,0:T(8,128)(2,1)S(1)}, u32[]{:S(2)}, u32[]{:S(2)}) async-start(bf16[8,128,512]{2,1,0:T(8,128)(2,1)} %get-tuple-element.40), calls=%async_computation.3 | async-start | bytes 2097152 | tf_op jit(solution)/shard_map/all_to_all | solution.py:455
  130.3 4.3 %copy-start.3 = (bf16[8,128,512]{2,1,0:T(8,128)(2,1)}, bf16[8,128,512]{2,1,0:T(8,128)(2,1)S(1)}, u32[]{:S(2)}) copy-start(bf16[8,128,512]{2,1,0:T(8,128)(2,1)S(1)} %all-to-all-done.3) | copy-start | bytes 3145732
  130.3 17.4 %all-to-all-start.2 = ((bf16[8,128,512]{2,1,0:T(8,128)(2,1)}), bf16[8,128,512]{2,1,0:T(8,128)(2,1)}, u32[]{:S(2)}, u32[]{:S(2)}) async-start(bf16[8,128,512]{2,1,0:T(8,128)(2,1)} %get-tuple-element.39), calls=%async_computation.2 | async-start | bytes 2097152 | tf_op jit(solution)/shard_map/all_to_all | solution.py:455
  134.6 5.2 %collective-permute-start.20 = (bf16[16,64,512]{2,1,0:T(8,128)(2,1)S(1)}, bf16[16,64,512]{2,1,0:T(8,128)(2,1)}, u32[]{:S(2)}, u32[]{:S(2)}) collective-permute-start(bf16[16,64,512]{2,1,0:T(8,128)(2,1)S(1)} %bitcast.50), channel_id=1, source_target_pairs={{0,1},{1,0},{2,3},{3,2},{4,5},{5,4},{6,7},{7,6},{8,9},{9,8},{10,11... | collective-permute-start | bytes 3145736 | tf_op jit(solution)/shard_map/ppermute | solution.py:59
  147.8 6.3 %collective-permute-start.21 = (bf16[16,64,512]{2,1,0:T(8,128)(2,1)}, bf16[16,64,512]{2,1,0:T(8,128)(2,1)}, u32[]{:S(2)}, u32[]{:S(2)}) collective-permute-start(bf16[16,64,512]{2,1,0:T(8,128)(2,1)} %bitcast.16.mine_ref), channel_id=1, source_target_pairs={{0,1},{1,0},{2,3},{3,2},{4,5},{5,4},{6,7},{7,6},{8,9},{9,8},{10,11... | collective-permute-start | bytes 3145736 | tf_op jit(solution)/shard_map/ppermute | solution.py:59
  151.4 15.1 %collective-permute-start.29 = (bf16[8,64,512]{2,1,0:T(8,128)(2,1)}, bf16[8,64,512]{2,1,0:T(8,128)(2,1)}, u32[]{:S(2)}, u32[]{:S(2)}) collective-permute-start(bf16[8,64,512]{2,1,0:T(8,128)(2,1)} %get-tuple-element.42), channel_id=1, source_target_pairs={{0,2},{2,4},{4,6},{6,0},{1,3},{3,5},{5,7},{7,1},{8,10},{10,12},{12... | collective-permute-start | bytes 1572872 | tf_op jit(solution)/shard_map/ppermute | solution.py:59
  152.1 14.3 %collective-permute-start.30 = (bf16[8,64,512]{2,1,0:T(8,128)(2,1)}, bf16[8,64,512]{2,1,0:T(8,128)(2,1)S(1)}, u32[]{:S(2)}, u32[]{:S(2)}) collective-permute-start(bf16[8,64,512]{2,1,0:T(8,128)(2,1)} %get-tuple-element.43), channel_id=1, source_target_pairs={{0,6},{2,0},{4,2},{6,4},{1,7},{3,1},{5,3},{7,5},{8,14},{10,8},{12,... | collective-permute-start | bytes 1572872 | tf_op jit(solution)/shard_map/ppermute | solution.py:59
  157.8 32.7 %copy-start.4 = (bf16[8,64,512]{2,1,0:T(8,128)(2,1)S(1)}, bf16[8,64,512]{2,1,0:T(8,128)(2,1)}, u32[]{:S(2)}) copy-start(bf16[8,64,512]{2,1,0:T(8,128)(2,1)} %get-tuple-element.48) | copy-start | bytes 1572868
  157.8 19.0 %collective-permute-start.22 = (bf16[8,64,512]{2,1,0:T(8,128)(2,1)}, bf16[8,64,512]{2,1,0:T(8,128)(2,1)S(1)}, u32[]{:S(2)}, u32[]{:S(2)}) collective-permute-start(bf16[8,64,512]{2,1,0:T(8,128)(2,1)} %get-tuple-element.49), channel_id=1, source_target_pairs={{0,6},{2,0},{4,2},{6,4},{1,7},{3,1},{5,3},{7,5},{8,14},{10,8},{12,... | collective-permute-start | bytes 1572872 | tf_op jit(solution)/shard_map/ppermute | solution.py:59
  159.9 21.1 %collective-permute-start.23 = (bf16[8,64,512]{2,1,0:T(8,128)(2,1)}, bf16[8,64,512]{2,1,0:T(8,128)(2,1)S(1)}, u32[]{:S(2)}, u32[]{:S(2)}) collective-permute-start(bf16[8,64,512]{2,1,0:T(8,128)(2,1)} %get-tuple-element.51), channel_id=1, source_target_pairs={{0,2},{2,4},{4,6},{6,0},{1,3},{3,5},{5,7},{7,1},{8,10},{10,12},{12... | collective-permute-start | bytes 1572872 | tf_op jit(solution)/shard_map/ppermute | solution.py:59
  167.5 15.0 %collective-permute-start.33 = (bf16[4,64,512]{2,1,0:T(8,128)(2,1)S(1)}, bf16[4,64,512]{2,1,0:T(8,128)(2,1)S(1)}, u32[]{:S(2)}, u32[]{:S(2)}) collective-permute-start(bf16[4,64,512]{2,1,0:T(8,128)(2,1)S(1)} %add_convert_fusion), channel_id=1, source_target_pairs={{0,6},{2,0},{4,2},{6,4},{1,7},{3,1},{5,3},{7,5},{8,14},{10,8},{12,... | collective-permute-start | bytes 786440 | tf_op jit(solution)/shard_map/ppermute | solution.py:59
  170.9 12.3 %collective-permute-start.31 = (bf16[4,64,512]{2,1,0:T(8,128)(2,1)S(1)}, bf16[4,64,512]{2,1,0:T(8,128)(2,1)S(1)}, u32[]{:S(2)}, u32[]{:S(2)}) collective-permute-start(bf16[4,64,512]{2,1,0:T(8,128)(2,1)S(1)} %add_convert_fusion.1), channel_id=1, source_target_pairs={{0,2},{2,4},{4,6},{6,0},{1,3},{3,5},{5,7},{7,1},{8,10},{10,12},{12... | collective-permute-start | bytes 786440 | tf_op jit(solution)/shard_map/ppermute | solution.py:59
  177.8 12.7 %collective-permute-start.26 = (bf16[4,64,512]{2,1,0:T(8,128)(2,1)S(1)}, bf16[4,64,512]{2,1,0:T(8,128)(2,1)S(1)}, u32[]{:S(2)}, u32[]{:S(2)}) collective-permute-start(bf16[4,64,512]{2,1,0:T(8,128)(2,1)S(1)} %add_convert_fusion.2), channel_id=1, source_target_pairs={{0,6},{2,0},{4,2},{6,4},{1,7},{3,1},{5,3},{7,5},{8,14},{10,8},{12,... | collective-permute-start | bytes 786440 | tf_op jit(solution)/shard_map/ppermute | solution.py:59
  182.0 8.5 %collective-permute-start.24 = (bf16[4,64,512]{2,1,0:T(8,128)(2,1)S(1)}, bf16[4,64,512]{2,1,0:T(8,128)(2,1)S(1)}, u32[]{:S(2)}, u32[]{:S(2)}) collective-permute-start(bf16[4,64,512]{2,1,0:T(8,128)(2,1)S(1)} %add_convert_fusion.3), channel_id=1, source_target_pairs={{0,2},{2,4},{4,6},{6,0},{1,3},{3,5},{5,7},{7,1},{8,10},{10,12},{12... | collective-permute-start | bytes 786440 | tf_op jit(solution)/shard_map/ppermute | solution.py:59
  184.5 12.9 %collective-permute-start.34 = (bf16[2,64,512]{2,1,0:T(8,128)(2,1)S(1)}, bf16[2,64,512]{2,1,0:T(8,128)(2,1)S(1)}, u32[]{:S(2)}, u32[]{:S(2)}) collective-permute-start(bf16[2,64,512]{2,1,0:T(8,128)(2,1)S(1)} %get-tuple-element.62), channel_id=1, source_target_pairs={{0,16},{8,24},{16,0},{24,8},{1,17},{9,25},{17,1},{25,9},{2,18},{10... | collective-permute-start | bytes 393224 | tf_op jit(solution)/shard_map/ppermute | solution.py:59
  188.2 22.8 %collective-permute-start.35 = (bf16[2,64,512]{2,1,0:T(8,128)(2,1)S(1)}, bf16[2,64,512]{2,1,0:T(8,128)(2,1)S(1)}, u32[]{:S(2)}, u32[]{:S(2)}) collective-permute-start(bf16[2,64,512]{2,1,0:T(8,128)(2,1)S(1)} %get-tuple-element.63), channel_id=1, source_target_pairs={{0,24},{8,0},{16,8},{24,16},{1,25},{9,1},{17,9},{25,17},{2,26},{10... | collective-permute-start | bytes 393224 | tf_op jit(solution)/shard_map/ppermute | solution.py:59
  189.3 21.7 %collective-permute-start.32 = (bf16[2,64,512]{2,1,0:T(8,128)(2,1)S(1)}, bf16[2,64,512]{2,1,0:T(8,128)(2,1)S(1)}, u32[]{:S(2)}, u32[]{:S(2)}) collective-permute-start(bf16[2,64,512]{2,1,0:T(8,128)(2,1)S(1)} %get-tuple-element.66), channel_id=1, source_target_pairs={{0,8},{8,16},{16,24},{24,0},{1,9},{9,17},{17,25},{25,1},{2,10},{10... | collective-permute-start | bytes 393224 | tf_op jit(solution)/shard_map/ppermute | solution.py:59
  190.7 22.0 %collective-permute-start.27 = (bf16[2,64,512]{2,1,0:T(8,128)(2,1)S(1)}, bf16[2,64,512]{2,1,0:T(8,128)(2,1)S(1)}, u32[]{:S(2)}, u32[]{:S(2)}) collective-permute-start(bf16[2,64,512]{2,1,0:T(8,128)(2,1)S(1)} %get-tuple-element.64), channel_id=1, source_target_pairs={{0,16},{8,24},{16,0},{24,8},{1,17},{9,25},{17,1},{25,9},{2,18},{10... | collective-permute-start | bytes 393224 | tf_op jit(solution)/shard_map/ppermute | solution.py:59
  193.8 20.0 %collective-permute-start.28 = (bf16[2,64,512]{2,1,0:T(8,128)(2,1)S(1)}, bf16[2,64,512]{2,1,0:T(8,128)(2,1)S(1)}, u32[]{:S(2)}, u32[]{:S(2)}) collective-permute-start(bf16[2,64,512]{2,1,0:T(8,128)(2,1)S(1)} %get-tuple-element.65), channel_id=1, source_target_pairs={{0,24},{8,0},{16,8},{24,16},{1,25},{9,1},{17,9},{25,17},{2,26},{10... | collective-permute-start | bytes 393224 | tf_op jit(solution)/shard_map/ppermute | solution.py:59
  197.4 16.5 %collective-permute-start.25 = (bf16[2,64,512]{2,1,0:T(8,128)(2,1)S(1)}, bf16[2,64,512]{2,1,0:T(8,128)(2,1)S(1)}, u32[]{:S(2)}, u32[]{:S(2)}) collective-permute-start(bf16[2,64,512]{2,1,0:T(8,128)(2,1)S(1)} %get-tuple-element.67), channel_id=1, source_target_pairs={{0,8},{8,16},{16,24},{24,0},{1,9},{9,17},{17,25},{25,1},{2,10},{10... | collective-permute-start | bytes 393224 | tf_op jit(solution)/shard_map/ppermute | solution.py:59

commit v3 on v2

--- a/solution.py
+++ b/solution.py
@@ -366,12 +366,15 @@
 
 def merge_slots(places, mine, theirs):
     sizes = (8, 8, 4, 4, 8)
+    half = WIDTH // 2
+    slots = pl.BlockSpec((FRAMES * SLOTS, TILE, half), lambda i: (0, 0, i))
     return pl.pallas_call(
         merge_kernel,
+        grid=(2,),
         out_shape=tuple(jax.ShapeDtypeStruct((n, TILE, WIDTH), jnp.bfloat16) for n in sizes),
-        in_specs=[smem(), whole(), whole()],
-        out_specs=(whole(),) * 5,
-        scratch_shapes=[pltpu.VMEM((32, TILE, WIDTH), jnp.float32)],
+        in_specs=[smem(), slots, slots],
+        out_specs=tuple(pl.BlockSpec((n, TILE, half), lambda i: (0, 0, i)) for n in sizes),
+        scratch_shapes=[pltpu.VMEM((32, TILE, half), jnp.float32)],
         compiler_params=params(),
         name="merge_slots",
     )(places, mine, theirs)

time: 216 us -> 216 us (level)
  waiting for transfers between devices: 81.1 us -> 83.4 us
  starting transfers between devices: 80.8 us -> 78.5 us
where the time goes in v3:
time: 216 us; the launch traced here: 215 us
  waiting for transfers between devices  83.4 us (39%)
  starting transfers between devices  78.5 us (36%)
  Pallas kernels  40 us (19%)
  other arithmetic  10.7 us (5%)
    ppermute x36, waiting for transfers between devices, shift(): lax.ppermute(value, axis, [(i, (i + step) % size) for i in range(size)])  67.5 us
    ppermute x36, starting transfers between devices, shift(): lax.ppermute(value, axis, [(i, (i + step) % size) for i in range(size)])  62.2 us
    all_to_all x4, starting transfers between devices, exchange(): lax.all_to_all(chosen.reshape(FRAMES, SLOTS * TILE, WIDTH), TM, split_axi...  16.3 us
    all_to_all x4, waiting for transfers between devices, exchange(): lax.all_to_all(chosen.reshape(FRAMES, SLOTS * TILE, WIDTH), TM, split_axi...  15.9 us
    pallas_call x1, Pallas kernels, attend_back(): pl.pallas_call(back_kernel, grid=(FRAMES,), out_shape=(pltpu.HBM((ROWS, W...  10.5 us
    convert_element_type x8, other arithmetic, add_wide(): return total.astype(jnp.bfloat16)  8.04 us
    pallas_call x2, Pallas kernels, select_tiles(): pl.pallas_call(select_kernel, out_shape=jax.ShapeDtypeStruct((FRAMES * SL...  7.6 us
    pallas_call x2, Pallas kernels, merge_slots(): pl.pallas_call(merge_kernel, grid=(2,), out_shape=tuple((jax.ShapeDtypeSt...  7.46 us
  transfers between devices with their start and end apart: 40, of which 19 were waited for; matrix products, arithmetic and copies ran while one was open for 5% of the time, Pallas kernels for 15%

profile of v3, /device:TPU:1, one launch (start us, length us, event | category | flops | bytes accessed | tf_op | source)
XLA Modules:
  0.0 214.6 jit_solution(3893450940214447209)
XLA Ops:
  0.6 3.9 %collective-permute-start.2 = (bf16[2,64,512]{2,1,0:T(8,128)(2,1)}, bf16[2,64,512]{2,1,0:T(8,128)(2,1)S(1)}, u32[]{:S(2)}, u32[]{:S(2)}) collective-permute-start(bf16[2,64,512]{2,1,0:T(8,128)(2,1)} %bitcast.55), channel_id=1, source_target_pairs={{0,8},{8,16},{16,24},{24,0},{1,9},{9,17},{17,25},{25,1},{2,10},{10... | collective-permute-start | bytes 393224 | tf_op jit(solution)/shard_map/ppermute | solution.py:59
  4.5 5.1 %collective-permute-start.1 = (bf16[2,64,512]{2,1,0:T(8,128)(2,1)}, bf16[2,64,512]{2,1,0:T(8,128)(2,1)S(1)}, u32[]{:S(2)}, u32[]{:S(2)}) collective-permute-start(bf16[2,64,512]{2,1,0:T(8,128)(2,1)} %bitcast.56), channel_id=1, source_target_pairs={{0,16},{8,24},{16,0},{24,8},{1,17},{9,25},{17,1},{25,9},{2,18},{10... | collective-permute-start | bytes 393224 | tf_op jit(solution)/shard_map/ppermute | solution.py:59
  9.7 2.4 %collective-permute-start = (bf16[2,64,512]{2,1,0:T(8,128)(2,1)}, bf16[2,64,512]{2,1,0:T(8,128)(2,1)S(1)}, u32[]{:S(2)}, u32[]{:S(2)}) collective-permute-start(bf16[2,64,512]{2,1,0:T(8,128)(2,1)} %bitcast.57), channel_id=1, source_target_pairs={{0,24},{8,0},{16,8},{24,16},{1,25},{9,1},{17,9},{25,17},{2,26},{10... | collective-permute-start | bytes 393224 | tf_op jit(solution)/shard_map/ppermute | solution.py:59
  12.0 6.4 %collective-permute-done.1 = bf16[2,64,512]{2,1,0:T(8,128)(2,1)S(1)} collective-permute-done((bf16[2,64,512]{2,1,0:T(8,128)(2,1)}, bf16[2,64,512]{2,1,0:T(8,128)(2,1)S(1)}, u32[]{:S(2)}, u32[]{:S(2)}) %collective-permute-start.1) | collective-permute-done | bytes 131104 | tf_op jit(solution)/shard_map/ppermute | solution.py:59
  18.5 4.3 %collective-permute-done = bf16[2,64,512]{2,1,0:T(8,128)(2,1)S(1)} collective-permute-done((bf16[2,64,512]{2,1,0:T(8,128)(2,1)}, bf16[2,64,512]{2,1,0:T(8,128)(2,1)S(1)}, u32[]{:S(2)}, u32[]{:S(2)}) %collective-permute-start) | collective-permute-done | bytes 131104 | tf_op jit(solution)/shard_map/ppermute | solution.py:59
  22.8 1.0 pad_maximum_fusion.refs_0_
  23.8 1.3 collective-permute-start.5
  25.1 2.5 %collective-permute-start.4 = (bf16[8,64,512]{2,1,0:T(8,128)(2,1)S(1)}, bf16[8,64,512]{2,1,0:T(8,128)(2,1)S(1)}, u32[]{:S(2)}, u32[]{:S(2)}) collective-permute-start(bf16[8,64,512]{2,1,0:T(8,128)(2,1)S(1)} %pad_maximum_fusion.refs_0_), channel_id=1, source_target_pairs={{0,4},{2,6},{4,0},{6,2},{1,5},{3,7},{5,1},{7,3},{8,12},{10,14},{12... | collective-permute-start | bytes 1572872 | tf_op jit(solution)/shard_map/ppermute | solution.py:59
  27.5 1.2 collective-permute-start.3
  28.7 0.9 collective-permute-start.8
  29.6 4.5 %collective-permute-start.7 = (bf16[2,64,512]{2,1,0:T(8,128)(2,1)}, bf16[2,64,512]{2,1,0:T(8,128)(2,1)S(1)}, u32[]{:S(2)}, u32[]{:S(2)}) collective-permute-start(bf16[2,64,512]{2,1,0:T(8,128)(2,1)} %bitcast.60), channel_id=1, source_target_pairs={{0,16},{8,24},{16,0},{24,8},{1,17},{9,25},{17,1},{25,9},{2,18},{10... | collective-permute-start | bytes 393224 | tf_op jit(solution)/shard_map/ppermute | solution.py:59
  34.1 2.5 %collective-permute-done.8 = bf16[2,64,512]{2,1,0:T(8,128)(2,1)S(1)} collective-permute-done((bf16[2,64,512]{2,1,0:T(8,128)(2,1)}, bf16[2,64,512]{2,1,0:T(8,128)(2,1)S(1)}, u32[]{:S(2)}, u32[]{:S(2)}) %collective-permute-start.8) | collective-permute-done | bytes 131104 | tf_op jit(solution)/shard_map/ppermute | solution.py:59
  36.6 1.3 collective-permute-start.6
  37.8 3.7 %collective-permute-done.7 = bf16[2,64,512]{2,1,0:T(8,128)(2,1)S(1)} collective-permute-done((bf16[2,64,512]{2,1,0:T(8,128)(2,1)}, bf16[2,64,512]{2,1,0:T(8,128)(2,1)S(1)}, u32[]{:S(2)}, u32[]{:S(2)}) %collective-permute-start.7) | collective-permute-done | bytes 131104 | tf_op jit(solution)/shard_map/ppermute | solution.py:59
  41.6 2.2 %collective-permute-start.9 = (bf16[8,64,512]{2,1,0:T(8,128)(2,1)S(1)}, bf16[8,64,512]{2,1,0:T(8,128)(2,1)}, u32[]{:S(2)}, u32[]{:S(2)}) collective-permute-start(bf16[8,64,512]{2,1,0:T(8,128)(2,1)S(1)} %pad_maximum_fusion.refs_0_), channel_id=1, source_target_pairs={{0,1},{1,0},{2,3},{3,2},{4,5},{5,4},{6,7},{7,6},{8,9},{9,8},{10,11... | collective-permute-start | bytes 1572872 | tf_op jit(solution)/shard_map/ppermute | solution.py:59
  43.8 1.0 pad_maximum_fusion.1.refs_0_
  44.8 5.5 %collective-permute-done.4.refs_2_ = bf16[8,64,512]{2,1,0:T(8,128)(2,1)S(1)} collective-permute-done((bf16[8,64,512]{2,1,0:T(8,128)(2,1)S(1)}, bf16[8,64,512]{2,1,0:T(8,128)(2,1)S(1)}, u32[]{:S(2)}, u32[]{:S(2)}) %collective-permute-start.4) | collective-permute-done | bytes 524320 | tf_op jit(solution)/shard_map/ppermute | solution.py:59
  50.3 1.3 collective-permute-start.10
  52.4 1.1 collective-permute-start.15
  53.5 2.1 collective-permute-start.14
  55.6 1.3 collective-permute-start.13
  57.0 3.7 %select_tiles.2 = bf16[16,64,512]{2,1,0:T(8,128)(2,1)} custom-call(s32[16]{0:T(128)S(1)} %fusion.2.piece_ref, s32[16]{0:T(128)S(1)} %get-tuple-element.59.row_ref, bf16[8,64,512]{2,1,0:T(8,128)(2,1)S(1)} %pad_maximum_fusion.refs_0_, bf16[8,64,512]{2,1,0:T(8,128)(2,1)S(1)} %collective-permute-done.3.refs_1_, ...), custom_call_target="tpu_custom_call" | custom-call | tf_op jit(solution)/shard_map/select_tiles/pallas_call | solution.py:109
  60.6 4.2 %all-to-all-start = ((bf16[8,128,512]{2,1,0:T(8,128)(2,1)}), bf16[8,128,512]{2,1,0:T(8,128)(2,1)S(1)}, u32[]{:S(2)}, u32[]{:S(2)}) async-start(bf16[8,128,512]{2,1,0:T(8,128)(2,1)} %bitcast.9), calls=%async_computation | async-start | bytes 2097152 | tf_op jit(solution)/shard_map/all_to_all | solution.py:458
  64.9 1.3 collective-permute-start.16
  66.2 1.0 collective-permute-done.15.refs_3_
  67.2 0.9 collective-permute-start.19
  68.1 10.8 %collective-permute-done.14.refs_2_ = bf16[8,64,512]{2,1,0:T(8,128)(2,1)} collective-permute-done((bf16[8,64,512]{2,1,0:T(8,128)(2,1)S(1)}, bf16[8,64,512]{2,1,0:T(8,128)(2,1)}, u32[]{:S(2)}, u32[]{:S(2)}) %collective-permute-start.14) | collective-permute-done | bytes 524320 | tf_op jit(solution)/shard_map/ppermute | solution.py:59
  78.9 0.9 collective-permute-start.18
  79.9 1.6 collective-permute-done.18.refs_6_
  82.3 3.9 %select_tiles.3 = bf16[16,64,512]{2,1,0:T(8,128)(2,1)} custom-call(s32[16]{0:T(128)S(1)} %fusion.2.piece_ref, s32[16]{0:T(128)S(1)} %get-tuple-element.59.row_ref, bf16[8,64,512]{2,1,0:T(8,128)(2,1)S(1)} %pad_maximum_fusion.1.refs_0_, bf16[8,64,512]{2,1,0:T(8,128)(2,1)} %collective-permute-done.13.refs_1_, ...), custom_call_target="tpu_custom_call" | custom-call | flops 12999999488 | tf_op jit(solution)/shard_map/select_tiles/pallas_call | solution.py:109
  86.3 4.3 %all-to-all-start.1 = ((bf16[8,128,512]{2,1,0:T(8,128)(2,1)}), bf16[8,128,512]{2,1,0:T(8,128)(2,1)}, u32[]{:S(2)}, u32[]{:S(2)}) async-start(bf16[8,128,512]{2,1,0:T(8,128)(2,1)} %bitcast.10), calls=%async_computation.1 | async-start | bytes 2097152 | tf_op jit(solution)/shard_map/all_to_all | solution.py:458
  90.5 0.9 dynamic-slice_reduce_fusion.count_ref
  91.4 7.2 %attend_weights.1 = (f32[8,4,128,256]{3,2,1,0:T(8,128)}, bf16[8,4,128,256]{3,2,1,0:T(8,128)(2,1)S(1)}) custom-call(s32[8]{0:T(128)S(1)} %dynamic-slice_reduce_fusion.count_ref, bf16[128,512]{1,0:T(8,128)(2,1)S(1)} %bitcast.48, bf16[8,128,512]{2,1,0:T(8,128)(2,1)} %copy-done.2), custom_call_target="tpu_custom_call" | custom-call | tf_op jit(solution)/shard_map/attend_weights/pallas_call | solution.py:166
  98.7 7.5 %all-to-all-done.1.value_ref = bf16[8,128,512]{2,1,0:T(8,128)(2,1)} async-done(((bf16[8,128,512]{2,1,0:T(8,128)(2,1)}), bf16[8,128,512]{2,1,0:T(8,128)(2,1)}, u32[]{:S(2)}, u32[]{:S(2)}) %all-to-all-start.1) | async-done | bytes 1048608 | tf_op jit(solution)/shard_map/all_to_all | solution.py:458
  106.1 7.2 %pool_frames.1 = (bf16[128,512]{1,0:T(8,128)(2,1)}, bf16[8,512,128]{2,1,0:T(8,128)(2,1)}, bf16[8,128,512]{2,1,0:T(8,128)(2,1)}) custom-call(s32[1]{0:T(128)} %bitcast.frame_ref, bf16[8,4,128,256]{3,2,1,0:T(8,128)(2,1)S(1)} %get-tuple-element.34.weight_ref, bf16[8,128,512]{2,1,0:T(8,128)(2,1)} %all-to-all-done.1.value_ref, bf16[512,512]{1,0:T(8,128)(2,1)} %wq_ref.1, ...), custom_call_target="tpu_custom_call" | custom-call | tf_op jit(solution)/shard_map/pool_frames/pallas_call | solution.py:266
  113.3 3.6 %all-to-all-start.3 = ((bf16[8,128,512]{2,1,0:T(8,128)(2,1)}), bf16[8,128,512]{2,1,0:T(8,128)(2,1)S(1)}, u32[]{:S(2)}, u32[]{:S(2)}) async-start(bf16[8,128,512]{2,1,0:T(8,128)(2,1)} %get-tuple-element.40), calls=%async_computation.3 | async-start | bytes 2097152 | tf_op jit(solution)/shard_map/all_to_all | solution.py:458
  116.8 10.5 %attend_back.1 = (bf16[128,512]{1,0:T(8,128)(2,1)}, bf16[8,128,512]{2,1,0:T(8,128)(2,1)}) custom-call(bf16[128,512]{1,0:T(8,128)(2,1)S(1)} %bitcast.49, bf16[8,128,512]{2,1,0:T(8,128)(2,1)} %copy-done.2, bf16[8,128,512]{2,1,0:T(8,128)(2,1)} %all-to-all-done.1.value_ref, f32[8,4,128,256]{3,2,1,0:T(8,128)} %get-tuple-element.36.weight_ref, ...), custom_call_target="tpu_custom_call" | custom-call | tf_op jit(solution)/shard_map/attend_back/pallas_call | solution.py:323
  127.4 3.6 %all-to-all-done.3 = bf16[8,128,512]{2,1,0:T(8,128)(2,1)S(1)} async-done(((bf16[8,128,512]{2,1,0:T(8,128)(2,1)}), bf16[8,128,512]{2,1,0:T(8,128)(2,1)S(1)}, u32[]{:S(2)}, u32[]{:S(2)}) %all-to-all-start.3) | async-done | bytes 1048608 | tf_op jit(solution)/shard_map/all_to_all | solution.py:458
  131.0 4.3 %all-to-all-start.2 = ((bf16[8,128,512]{2,1,0:T(8,128)(2,1)}), bf16[8,128,512]{2,1,0:T(8,128)(2,1)}, u32[]{:S(2)}, u32[]{:S(2)}) async-start(bf16[8,128,512]{2,1,0:T(8,128)(2,1)} %get-tuple-element.39), calls=%async_computation.2 | async-start | bytes 2097152 | tf_op jit(solution)/shard_map/all_to_all | solution.py:458
  135.3 2.5 %collective-permute-start.20 = (bf16[16,64,512]{2,1,0:T(8,128)(2,1)S(1)}, bf16[16,64,512]{2,1,0:T(8,128)(2,1)}, u32[]{:S(2)}, u32[]{:S(2)}) collective-permute-start(bf16[16,64,512]{2,1,0:T(8,128)(2,1)S(1)} %bitcast.50), channel_id=1, source_target_pairs={{0,1},{1,0},{2,3},{3,2},{4,5},{5,4},{6,7},{7,6},{8,9},{9,8},{10,11... | collective-permute-start | bytes 3145736 | tf_op jit(solution)/shard_map/ppermute | solution.py:59
  138.5 1.7 collective-permute-done.20.theirs_ref
  140.2 3.7 %merge_slots.2 = (bf16[8,64,512]{2,1,0:T(8,128)(2,1)}, bf16[8,64,512]{2,1,0:T(8,128)(2,1)}, bf16[4,64,512]{2,1,0:T(8,128)(2,1)}, bf16[4,64,512]{2,1,0:T(8,128)(2,1)}, bf16[8,64,512]{2,1,0:T(8,128)(2,1)}) custom-call(s32[32]{0:T(128)} %pad_add_fusion.place_ref, bf16[16,64,512]{2,1,0:T(8,128)(2,1)} %bitcast.51, ...), custom_call_target="tpu_custom_call" | custom-call | tf_op jit(solution)/shard_map/merge_slots/pallas_call | solution.py:371
  143.9 4.8 %all-to-all-done.2 = bf16[8,128,512]{2,1,0:T(8,128)(2,1)} async-done(((bf16[8,128,512]{2,1,0:T(8,128)(2,1)}), bf16[8,128,512]{2,1,0:T(8,128)(2,1)}, u32[]{:S(2)}, u32[]{:S(2)}) %all-to-all-start.2) | async-done | bytes 1048608 | tf_op jit(solution)/shard_map/all_to_all | solution.py:458
  148.7 3.3 %collective-permute-start.21 = (bf16[16,64,512]{2,1,0:T(8,128)(2,1)}, bf16[16,64,512]{2,1,0:T(8,128)(2,1)}, u32[]{:S(2)}, u32[]{:S(2)}) collective-permute-start(bf16[16,64,512]{2,1,0:T(8,128)(2,1)} %bitcast.16.mine_ref), channel_id=1, source_target_pairs={{0,1},{1,0},{2,3},{3,2},{4,5},{5,4},{6,7},{7,6},{8,9},{9,8},{10,11... | collective-permute-start | bytes 3145736 | tf_op jit(solution)/shard_map/ppermute | solution.py:59
  152.0 2.6 %collective-permute-start.30 = (bf16[8,64,512]{2,1,0:T(8,128)(2,1)}, bf16[8,64,512]{2,1,0:T(8,128)(2,1)S(1)}, u32[]{:S(2)}, u32[]{:S(2)}) collective-permute-start(bf16[8,64,512]{2,1,0:T(8,128)(2,1)} %get-tuple-element.43), channel_id=1, source_target_pairs={{0,6},{2,0},{4,2},{6,4},{1,7},{3,1},{5,3},{7,5},{8,14},{10,8},{12,... | collective-permute-start | bytes 1572872 | tf_op jit(solution)/shard_map/ppermute | solution.py:59
  154.7 3.7 %merge_slots.3 = (bf16[8,64,512]{2,1,0:T(8,128)(2,1)}, bf16[8,64,512]{2,1,0:T(8,128)(2,1)}, bf16[4,64,512]{2,1,0:T(8,128)(2,1)}, bf16[4,64,512]{2,1,0:T(8,128)(2,1)}, bf16[8,64,512]{2,1,0:T(8,128)(2,1)}) custom-call(s32[32]{0:T(128)} %pad_add_fusion.place_ref, bf16[16,64,512]{2,1,0:T(8,128)(2,1)} %bitcast.16.mine_ref, ...), custom_call_target="tpu_custom_call" | custom-call | tf_op jit(solution)/shard_map/merge_slots/pallas_call | solution.py:371
  158.4 1.1 collective-permute-start.22
  160.0 7.1 %collective-permute-done.29 = bf16[8,64,512]{2,1,0:T(8,128)(2,1)} collective-permute-done((bf16[8,64,512]{2,1,0:T(8,128)(2,1)}, bf16[8,64,512]{2,1,0:T(8,128)(2,1)}, u32[]{:S(2)}, u32[]{:S(2)}) %collective-permute-start.29) | collective-permute-done | bytes 524320 | tf_op jit(solution)/shard_map/ppermute | solution.py:59
  167.1 1.0 add_convert_fusion
  168.1 2.5 %collective-permute-start.33 = (bf16[4,64,512]{2,1,0:T(8,128)(2,1)S(1)}, bf16[4,64,512]{2,1,0:T(8,128)(2,1)S(1)}, u32[]{:S(2)}, u32[]{:S(2)}) collective-permute-start(bf16[4,64,512]{2,1,0:T(8,128)(2,1)S(1)} %add_convert_fusion), channel_id=1, source_target_pairs={{0,6},{2,0},{4,2},{6,4},{1,7},{3,1},{5,3},{7,5},{8,14},{10,8},{12,... | collective-permute-start | bytes 786440 | tf_op jit(solution)/shard_map/ppermute | solution.py:59
  170.7 1.1 add_convert_fusion.1
  171.9 5.8 %collective-permute-done.22 = bf16[8,64,512]{2,1,0:T(8,128)(2,1)S(1)} collective-permute-done((bf16[8,64,512]{2,1,0:T(8,128)(2,1)}, bf16[8,64,512]{2,1,0:T(8,128)(2,1)S(1)}, u32[]{:S(2)}, u32[]{:S(2)}) %collective-permute-start.22) | collective-permute-done | bytes 524320 | tf_op jit(solution)/shard_map/ppermute | solution.py:59
  177.6 1.0 add_convert_fusion.2
  178.6 3.0 %collective-permute-start.26 = (bf16[4,64,512]{2,1,0:T(8,128)(2,1)S(1)}, bf16[4,64,512]{2,1,0:T(8,128)(2,1)S(1)}, u32[]{:S(2)}, u32[]{:S(2)}) collective-permute-start(bf16[4,64,512]{2,1,0:T(8,128)(2,1)S(1)} %add_convert_fusion.2), channel_id=1, source_target_pairs={{0,6},{2,0},{4,2},{6,4},{1,7},{3,1},{5,3},{7,5},{8,14},{10,8},{12,... | collective-permute-start | bytes 786440 | tf_op jit(solution)/shard_map/ppermute | solution.py:59
  181.7 1.0 add_convert_fusion.3
  183.8 1.3 add_convert_fusion.6
  185.2 3.1 %collective-permute-start.34 = (bf16[2,64,512]{2,1,0:T(8,128)(2,1)S(1)}, bf16[2,64,512]{2,1,0:T(8,128)(2,1)S(1)}, u32[]{:S(2)}, u32[]{:S(2)}) collective-permute-start(bf16[2,64,512]{2,1,0:T(8,128)(2,1)S(1)} %get-tuple-element.62), channel_id=1, source_target_pairs={{0,16},{8,24},{16,0},{24,8},{1,17},{9,25},{17,1},{25,9},{2,18},{10... | collective-permute-start | bytes 393224 | tf_op jit(solution)/shard_map/ppermute | solution.py:59
  188.9 1.8 collective-permute-start.32
  190.9 2.7 %collective-permute-start.27 = (bf16[2,64,512]{2,1,0:T(8,128)(2,1)S(1)}, bf16[2,64,512]{2,1,0:T(8,128)(2,1)S(1)}, u32[]{:S(2)}, u32[]{:S(2)}) collective-permute-start(bf16[2,64,512]{2,1,0:T(8,128)(2,1)S(1)} %get-tuple-element.64), channel_id=1, source_target_pairs={{0,16},{8,24},{16,0},{24,8},{1,17},{9,25},{17,1},{25,9},{2,18},{10... | collective-permute-start | bytes 393224 | tf_op jit(solution)/shard_map/ppermute | solution.py:59
  193.6 3.6 %collective-permute-start.28 = (bf16[2,64,512]{2,1,0:T(8,128)(2,1)S(1)}, bf16[2,64,512]{2,1,0:T(8,128)(2,1)S(1)}, u32[]{:S(2)}, u32[]{:S(2)}) collective-permute-start(bf16[2,64,512]{2,1,0:T(8,128)(2,1)S(1)} %get-tuple-element.65), channel_id=1, source_target_pairs={{0,24},{8,0},{16,8},{24,16},{1,25},{9,1},{17,9},{25,17},{2,26},{10... | collective-permute-start | bytes 393224 | tf_op jit(solution)/shard_map/ppermute | solution.py:59
  197.2 13.9 %collective-permute-done.35 = bf16[2,64,512]{2,1,0:T(8,128)(2,1)S(1)} collective-permute-done((bf16[2,64,512]{2,1,0:T(8,128)(2,1)S(1)}, bf16[2,64,512]{2,1,0:T(8,128)(2,1)S(1)}, u32[]{:S(2)}, u32[]{:S(2)}) %collective-permute-start.35) | collective-permute-done | bytes 131104 | tf_op jit(solution)/shard_map/ppermute | solution.py:59
  211.1 1.7 add_convert_fusion.4
  212.7 1.1 collective-permute-done.28
  213.9 0.8 add_convert_fusion.9
  (52 shorter events, 4.8 us)
Async XLA Ops:
  0.6 51.0 %copy-start = (s32[8,32,8,2]{1,3,2,0:T(2,128)S(1)}, s32[8,32,8,2]{1,3,2,0:T(2,128)}, u32[]{:S(2)}) copy-start(s32[8,32,8,2]{1,3,2,0:T(2,128)} %param.16) | copy-start | bytes 49156
  0.6 11.4 %collective-permute-start.2 = (bf16[2,64,512]{2,1,0:T(8,128)(2,1)}, bf16[2,64,512]{2,1,0:T(8,128)(2,1)S(1)}, u32[]{:S(2)}, u32[]{:S(2)}) collective-permute-start(bf16[2,64,512]{2,1,0:T(8,128)(2,1)} %bitcast.55), channel_id=1, source_target_pairs={{0,8},{8,16},{16,24},{24,0},{1,9},{9,17},{17,25},{25,1},{2,10},{10... | collective-permute-start | bytes 393224 | tf_op jit(solution)/shard_map/ppermute | solution.py:59
  4.5 13.9 %collective-permute-start.1 = (bf16[2,64,512]{2,1,0:T(8,128)(2,1)}, bf16[2,64,512]{2,1,0:T(8,128)(2,1)S(1)}, u32[]{:S(2)}, u32[]{:S(2)}) collective-permute-start(bf16[2,64,512]{2,1,0:T(8,128)(2,1)} %bitcast.56), channel_id=1, source_target_pairs={{0,16},{8,24},{16,0},{24,8},{1,17},{9,25},{17,1},{25,9},{2,18},{10... | collective-permute-start | bytes 393224 | tf_op jit(solution)/shard_map/ppermute | solution.py:59
  9.7 13.1 %collective-permute-start = (bf16[2,64,512]{2,1,0:T(8,128)(2,1)}, bf16[2,64,512]{2,1,0:T(8,128)(2,1)S(1)}, u32[]{:S(2)}, u32[]{:S(2)}) collective-permute-start(bf16[2,64,512]{2,1,0:T(8,128)(2,1)} %bitcast.57), channel_id=1, source_target_pairs={{0,24},{8,0},{16,8},{24,16},{1,25},{9,1},{17,9},{25,17},{2,26},{10... | collective-permute-start | bytes 393224 | tf_op jit(solution)/shard_map/ppermute | solution.py:59
  23.8 21.0 %collective-permute-start.5 = (bf16[8,64,512]{2,1,0:T(8,128)(2,1)S(1)}, bf16[8,64,512]{2,1,0:T(8,128)(2,1)S(1)}, u32[]{:S(2)}, u32[]{:S(2)}) collective-permute-start(bf16[8,64,512]{2,1,0:T(8,128)(2,1)S(1)} %pad_maximum_fusion.refs_0_), channel_id=1, source_target_pairs={{0,2},{2,4},{4,6},{6,0},{1,3},{3,5},{5,7},{7,1},{8,10},{10,12},{12... | collective-permute-start | bytes 1572872 | tf_op jit(solution)/shard_map/ppermute | solution.py:59
  25.1 25.2 %collective-permute-start.4 = (bf16[8,64,512]{2,1,0:T(8,128)(2,1)S(1)}, bf16[8,64,512]{2,1,0:T(8,128)(2,1)S(1)}, u32[]{:S(2)}, u32[]{:S(2)}) collective-permute-start(bf16[8,64,512]{2,1,0:T(8,128)(2,1)S(1)} %pad_maximum_fusion.refs_0_), channel_id=1, source_target_pairs={{0,4},{2,6},{4,0},{6,2},{1,5},{3,7},{5,1},{7,3},{8,12},{10,14},{12... | collective-permute-start | bytes 1572872 | tf_op jit(solution)/shard_map/ppermute | solution.py:59
  27.5 22.8 %collective-permute-start.3 = (bf16[8,64,512]{2,1,0:T(8,128)(2,1)S(1)}, bf16[8,64,512]{2,1,0:T(8,128)(2,1)S(1)}, u32[]{:S(2)}, u32[]{:S(2)}) collective-permute-start(bf16[8,64,512]{2,1,0:T(8,128)(2,1)S(1)} %pad_maximum_fusion.refs_0_), channel_id=1, source_target_pairs={{0,6},{2,0},{4,2},{6,4},{1,7},{3,1},{5,3},{7,5},{8,14},{10,8},{12,... | collective-permute-start | bytes 1572872 | tf_op jit(solution)/shard_map/ppermute | solution.py:59
  28.7 7.9 %collective-permute-start.8 = (bf16[2,64,512]{2,1,0:T(8,128)(2,1)}, bf16[2,64,512]{2,1,0:T(8,128)(2,1)S(1)}, u32[]{:S(2)}, u32[]{:S(2)}) collective-permute-start(bf16[2,64,512]{2,1,0:T(8,128)(2,1)} %bitcast.59), channel_id=1, source_target_pairs={{0,8},{8,16},{16,24},{24,0},{1,9},{9,17},{17,25},{25,1},{2,10},{10... | collective-permute-start | bytes 393224 | tf_op jit(solution)/shard_map/ppermute | solution.py:59
  29.6 12.0 %collective-permute-start.7 = (bf16[2,64,512]{2,1,0:T(8,128)(2,1)}, bf16[2,64,512]{2,1,0:T(8,128)(2,1)S(1)}, u32[]{:S(2)}, u32[]{:S(2)}) collective-permute-start(bf16[2,64,512]{2,1,0:T(8,128)(2,1)} %bitcast.60), channel_id=1, source_target_pairs={{0,16},{8,24},{16,0},{24,8},{1,17},{9,25},{17,1},{25,9},{2,18},{10... | collective-permute-start | bytes 393224 | tf_op jit(solution)/shard_map/ppermute | solution.py:59
  36.6 7.2 %collective-permute-start.6 = (bf16[2,64,512]{2,1,0:T(8,128)(2,1)}, bf16[2,64,512]{2,1,0:T(8,128)(2,1)S(1)}, u32[]{:S(2)}, u32[]{:S(2)}) collective-permute-start(bf16[2,64,512]{2,1,0:T(8,128)(2,1)} %bitcast.61), channel_id=1, source_target_pairs={{0,24},{8,0},{16,8},{24,16},{1,25},{9,1},{17,9},{25,17},{2,26},{10... | collective-permute-start | bytes 393224 | tf_op jit(solution)/shard_map/ppermute | solution.py:59
  41.6 11.9 %collective-permute-start.9 = (bf16[8,64,512]{2,1,0:T(8,128)(2,1)S(1)}, bf16[8,64,512]{2,1,0:T(8,128)(2,1)}, u32[]{:S(2)}, u32[]{:S(2)}) collective-permute-start(bf16[8,64,512]{2,1,0:T(8,128)(2,1)S(1)} %pad_maximum_fusion.refs_0_), channel_id=1, source_target_pairs={{0,1},{1,0},{2,3},{3,2},{4,5},{5,4},{6,7},{7,6},{8,9},{9,8},{10,11... | collective-permute-start | bytes 1572872 | tf_op jit(solution)/shard_map/ppermute | solution.py:59
  50.3 5.3 %collective-permute-start.10 = (bf16[8,64,512]{2,1,0:T(8,128)(2,1)S(1)}, bf16[8,64,512]{2,1,0:T(8,128)(2,1)}, u32[]{:S(2)}, u32[]{:S(2)}) collective-permute-start(bf16[8,64,512]{2,1,0:T(8,128)(2,1)S(1)} %collective-permute-done.3.refs_1_), channel_id=1, source_target_pairs={{0,1},{1,0},{2,3},{3,2},{4,5},{5,4},{6,7},{7,6},{8,9},{9,8},{10,11... | collective-permute-start | bytes 1572872 | tf_op jit(solution)/shard_map/ppermute | solution.py:59
  51.7 5.2 %collective-permute-start.11 = (bf16[8,64,512]{2,1,0:T(8,128)(2,1)S(1)}, bf16[8,64,512]{2,1,0:T(8,128)(2,1)}, u32[]{:S(2)}, u32[]{:S(2)}) collective-permute-start(bf16[8,64,512]{2,1,0:T(8,128)(2,1)S(1)} %collective-permute-done.4.refs_2_), channel_id=1, source_target_pairs={{0,1},{1,0},{2,3},{3,2},{4,5},{5,4},{6,7},{7,6},{8,9},{9,8},{10,11... | collective-permute-start | bytes 1572872 | tf_op jit(solution)/shard_map/ppermute | solution.py:59
  51.7 5.2 %collective-permute-start.12 = (bf16[8,64,512]{2,1,0:T(8,128)(2,1)S(1)}, bf16[8,64,512]{2,1,0:T(8,128)(2,1)}, u32[]{:S(2)}, u32[]{:S(2)}) collective-permute-start(bf16[8,64,512]{2,1,0:T(8,128)(2,1)S(1)} %collective-permute-done.5.refs_3_), channel_id=1, source_target_pairs={{0,1},{1,0},{2,3},{3,2},{4,5},{5,4},{6,7},{7,6},{8,9},{9,8},{10,11... | collective-permute-start | bytes 1572872 | tf_op jit(solution)/shard_map/ppermute | solution.py:59
  52.4 14.8 %collective-permute-start.15 = (bf16[8,64,512]{2,1,0:T(8,128)(2,1)S(1)}, bf16[8,64,512]{2,1,0:T(8,128)(2,1)}, u32[]{:S(2)}, u32[]{:S(2)}) collective-permute-start(bf16[8,64,512]{2,1,0:T(8,128)(2,1)S(1)} %pad_maximum_fusion.1.refs_0_), channel_id=1, source_target_pairs={{0,2},{2,4},{4,6},{6,0},{1,3},{3,5},{5,7},{7,1},{8,10},{10,12},{12... | collective-permute-start | bytes 1572872 | tf_op jit(solution)/shard_map/ppermute | solution.py:59
  53.5 25.4 %collective-permute-start.14 = (bf16[8,64,512]{2,1,0:T(8,128)(2,1)S(1)}, bf16[8,64,512]{2,1,0:T(8,128)(2,1)}, u32[]{:S(2)}, u32[]{:S(2)}) collective-permute-start(bf16[8,64,512]{2,1,0:T(8,128)(2,1)S(1)} %pad_maximum_fusion.1.refs_0_), channel_id=1, source_target_pairs={{0,4},{2,6},{4,0},{6,2},{1,5},{3,7},{5,1},{7,3},{8,12},{10,14},{12... | collective-permute-start | bytes 1572872 | tf_op jit(solution)/shard_map/ppermute | solution.py:59
  55.6 24.2 %collective-permute-start.13 = (bf16[8,64,512]{2,1,0:T(8,128)(2,1)S(1)}, bf16[8,64,512]{2,1,0:T(8,128)(2,1)}, u32[]{:S(2)}, u32[]{:S(2)}) collective-permute-start(bf16[8,64,512]{2,1,0:T(8,128)(2,1)S(1)} %pad_maximum_fusion.1.refs_0_), channel_id=1, source_target_pairs={{0,6},{2,0},{4,2},{6,4},{1,7},{3,1},{5,3},{7,5},{8,14},{10,8},{12,... | collective-permute-start | bytes 1572872 | tf_op jit(solution)/shard_map/ppermute | solution.py:59
  60.6 25.6 %all-to-all-start = ((bf16[8,128,512]{2,1,0:T(8,128)(2,1)}), bf16[8,128,512]{2,1,0:T(8,128)(2,1)S(1)}, u32[]{:S(2)}, u32[]{:S(2)}) async-start(bf16[8,128,512]{2,1,0:T(8,128)(2,1)} %bitcast.9), calls=%async_computation | async-start | bytes 2097152 | tf_op jit(solution)/shard_map/all_to_all | solution.py:458
  64.9 26.5 %copy-start.1 = (bf16[1,128,512]{2,1,0:T(8,128)(2,1)S(1)}, bf16[1,128,512]{2,1,0:T(8,128)(2,1)}, u32[]{:S(2)}) copy-start(bf16[1,128,512]{2,1,0:T(8,128)(2,1)} %param.9) | copy-start | bytes 393220
  64.9 15.1 %collective-permute-start.16 = (bf16[8,64,512]{2,1,0:T(8,128)(2,1)S(1)}, bf16[8,64,512]{2,1,0:T(8,128)(2,1)S(1)}, u32[]{:S(2)}, u32[]{:S(2)}) collective-permute-start(bf16[8,64,512]{2,1,0:T(8,128)(2,1)S(1)} %pad_maximum_fusion.1.refs_0_), channel_id=1, source_target_pairs={{0,1},{1,0},{2,3},{3,2},{4,5},{5,4},{6,7},{7,6},{8,9},{9,8},{10,11... | collective-permute-start | bytes 1572872 | tf_op jit(solution)/shard_map/ppermute | solution.py:59
  67.2 12.7 %collective-permute-start.19 = (bf16[8,64,512]{2,1,0:T(8,128)(2,1)}, bf16[8,64,512]{2,1,0:T(8,128)(2,1)S(1)}, u32[]{:S(2)}, u32[]{:S(2)}) collective-permute-start(bf16[8,64,512]{2,1,0:T(8,128)(2,1)} %collective-permute-done.15.refs_3_), channel_id=1, source_target_pairs={{0,1},{1,0},{2,3},{3,2},{4,5},{5,4},{6,7},{7,6},{8,9},{9,8},{10,11... | collective-permute-start | bytes 1572872 | tf_op jit(solution)/shard_map/ppermute | solution.py:59
  78.9 2.6 %collective-permute-start.18 = (bf16[8,64,512]{2,1,0:T(8,128)(2,1)}, bf16[8,64,512]{2,1,0:T(8,128)(2,1)S(1)}, u32[]{:S(2)}, u32[]{:S(2)}) collective-permute-start(bf16[8,64,512]{2,1,0:T(8,128)(2,1)} %collective-permute-done.14.refs_2_), channel_id=1, source_target_pairs={{0,1},{1,0},{2,3},{3,2},{4,5},{5,4},{6,7},{7,6},{8,9},{9,8},{10,11... | collective-permute-start | bytes 1572872 | tf_op jit(solution)/shard_map/ppermute | solution.py:59
  79.8 2.5 %collective-permute-start.17 = (bf16[8,64,512]{2,1,0:T(8,128)(2,1)}, bf16[8,64,512]{2,1,0:T(8,128)(2,1)S(1)}, u32[]{:S(2)}, u32[]{:S(2)}) collective-permute-start(bf16[8,64,512]{2,1,0:T(8,128)(2,1)} %collective-permute-done.13.refs_1_), channel_id=1, source_target_pairs={{0,1},{1,0},{2,3},{3,2},{4,5},{5,4},{6,7},{7,6},{8,9},{9,8},{10,11... | collective-permute-start | bytes 1572872 | tf_op jit(solution)/shard_map/ppermute | solution.py:59
  86.3 5.2 %copy-start.2 = (bf16[8,128,512]{2,1,0:T(8,128)(2,1)}, bf16[8,128,512]{2,1,0:T(8,128)(2,1)S(1)}, u32[]{:S(2)}) copy-start(bf16[8,128,512]{2,1,0:T(8,128)(2,1)S(1)} %all-to-all-done.key_ref) | copy-start | bytes 3145732
  86.3 19.9 %all-to-all-start.1 = ((bf16[8,128,512]{2,1,0:T(8,128)(2,1)}), bf16[8,128,512]{2,1,0:T(8,128)(2,1)}, u32[]{:S(2)}, u32[]{:S(2)}) async-start(bf16[8,128,512]{2,1,0:T(8,128)(2,1)} %bitcast.10), calls=%async_computation.1 | async-start | bytes 2097152 | tf_op jit(solution)/shard_map/all_to_all | solution.py:458
  113.3 17.7 %all-to-all-start.3 = ((bf16[8,128,512]{2,1,0:T(8,128)(2,1)}), bf16[8,128,512]{2,1,0:T(8,128)(2,1)S(1)}, u32[]{:S(2)}, u32[]{:S(2)}) async-start(bf16[8,128,512]{2,1,0:T(8,128)(2,1)} %get-tuple-element.40), calls=%async_computation.3 | async-start | bytes 2097152 | tf_op jit(solution)/shard_map/all_to_all | solution.py:458
  131.0 4.3 %copy-start.3 = (bf16[8,128,512]{2,1,0:T(8,128)(2,1)}, bf16[8,128,512]{2,1,0:T(8,128)(2,1)S(1)}, u32[]{:S(2)}) copy-start(bf16[8,128,512]{2,1,0:T(8,128)(2,1)S(1)} %all-to-all-done.3) | copy-start | bytes 3145732
  131.0 17.7 %all-to-all-start.2 = ((bf16[8,128,512]{2,1,0:T(8,128)(2,1)}), bf16[8,128,512]{2,1,0:T(8,128)(2,1)}, u32[]{:S(2)}, u32[]{:S(2)}) async-start(bf16[8,128,512]{2,1,0:T(8,128)(2,1)} %get-tuple-element.39), calls=%async_computation.2 | async-start | bytes 2097152 | tf_op jit(solution)/shard_map/all_to_all | solution.py:458
  135.3 4.9 %collective-permute-start.20 = (bf16[16,64,512]{2,1,0:T(8,128)(2,1)S(1)}, bf16[16,64,512]{2,1,0:T(8,128)(2,1)}, u32[]{:S(2)}, u32[]{:S(2)}) collective-permute-start(bf16[16,64,512]{2,1,0:T(8,128)(2,1)S(1)} %bitcast.50), channel_id=1, source_target_pairs={{0,1},{1,0},{2,3},{3,2},{4,5},{5,4},{6,7},{7,6},{8,9},{9,8},{10,11... | collective-permute-start | bytes 3145736 | tf_op jit(solution)/shard_map/ppermute | solution.py:59
  148.7 6.0 %collective-permute-start.21 = (bf16[16,64,512]{2,1,0:T(8,128)(2,1)}, bf16[16,64,512]{2,1,0:T(8,128)(2,1)}, u32[]{:S(2)}, u32[]{:S(2)}) collective-permute-start(bf16[16,64,512]{2,1,0:T(8,128)(2,1)} %bitcast.16.mine_ref), channel_id=1, source_target_pairs={{0,1},{1,0},{2,3},{3,2},{4,5},{5,4},{6,7},{7,6},{8,9},{9,8},{10,11... | collective-permute-start | bytes 3145736 | tf_op jit(solution)/shard_map/ppermute | solution.py:59
  152.0 15.1 %collective-permute-start.29 = (bf16[8,64,512]{2,1,0:T(8,128)(2,1)}, bf16[8,64,512]{2,1,0:T(8,128)(2,1)}, u32[]{:S(2)}, u32[]{:S(2)}) collective-permute-start(bf16[8,64,512]{2,1,0:T(8,128)(2,1)} %get-tuple-element.42), channel_id=1, source_target_pairs={{0,2},{2,4},{4,6},{6,0},{1,3},{3,5},{5,7},{7,1},{8,10},{10,12},{12... | collective-permute-start | bytes 1572872 | tf_op jit(solution)/shard_map/ppermute | solution.py:59
  152.0 15.1 %collective-permute-start.30 = (bf16[8,64,512]{2,1,0:T(8,128)(2,1)}, bf16[8,64,512]{2,1,0:T(8,128)(2,1)S(1)}, u32[]{:S(2)}, u32[]{:S(2)}) collective-permute-start(bf16[8,64,512]{2,1,0:T(8,128)(2,1)} %get-tuple-element.43), channel_id=1, source_target_pairs={{0,6},{2,0},{4,2},{6,4},{1,7},{3,1},{5,3},{7,5},{8,14},{10,8},{12,... | collective-permute-start | bytes 1572872 | tf_op jit(solution)/shard_map/ppermute | solution.py:59
  158.4 32.2 %copy-start.4 = (bf16[8,64,512]{2,1,0:T(8,128)(2,1)S(1)}, bf16[8,64,512]{2,1,0:T(8,128)(2,1)}, u32[]{:S(2)}) copy-start(bf16[8,64,512]{2,1,0:T(8,128)(2,1)} %get-tuple-element.48) | copy-start | bytes 1572868
  158.4 19.2 %collective-permute-start.22 = (bf16[8,64,512]{2,1,0:T(8,128)(2,1)}, bf16[8,64,512]{2,1,0:T(8,128)(2,1)S(1)}, u32[]{:S(2)}, u32[]{:S(2)}) collective-permute-start(bf16[8,64,512]{2,1,0:T(8,128)(2,1)} %get-tuple-element.49), channel_id=1, source_target_pairs={{0,6},{2,0},{4,2},{6,4},{1,7},{3,1},{5,3},{7,5},{8,14},{10,8},{12,... | collective-permute-start | bytes 1572872 | tf_op jit(solution)/shard_map/ppermute | solution.py:59
  159.6 22.1 %collective-permute-start.23 = (bf16[8,64,512]{2,1,0:T(8,128)(2,1)}, bf16[8,64,512]{2,1,0:T(8,128)(2,1)S(1)}, u32[]{:S(2)}, u32[]{:S(2)}) collective-permute-start(bf16[8,64,512]{2,1,0:T(8,128)(2,1)} %get-tuple-element.51), channel_id=1, source_target_pairs={{0,2},{2,4},{4,6},{6,0},{1,3},{3,5},{5,7},{7,1},{8,10},{10,12},{12... | collective-permute-start | bytes 1572872 | tf_op jit(solution)/shard_map/ppermute | solution.py:59
  168.1 15.1 %collective-permute-start.33 = (bf16[4,64,512]{2,1,0:T(8,128)(2,1)S(1)}, bf16[4,64,512]{2,1,0:T(8,128)(2,1)S(1)}, u32[]{:S(2)}, u32[]{:S(2)}) collective-permute-start(bf16[4,64,512]{2,1,0:T(8,128)(2,1)S(1)} %add_convert_fusion), channel_id=1, source_target_pairs={{0,6},{2,0},{4,2},{6,4},{1,7},{3,1},{5,3},{7,5},{8,14},{10,8},{12,... | collective-permute-start | bytes 786440 | tf_op jit(solution)/shard_map/ppermute | solution.py:59
  171.8 12.1 %collective-permute-start.31 = (bf16[4,64,512]{2,1,0:T(8,128)(2,1)S(1)}, bf16[4,64,512]{2,1,0:T(8,128)(2,1)S(1)}, u32[]{:S(2)}, u32[]{:S(2)}) collective-permute-start(bf16[4,64,512]{2,1,0:T(8,128)(2,1)S(1)} %add_convert_fusion.1), channel_id=1, source_target_pairs={{0,2},{2,4},{4,6},{6,0},{1,3},{3,5},{5,7},{7,1},{8,10},{10,12},{12... | collective-permute-start | bytes 786440 | tf_op jit(solution)/shard_map/ppermute | solution.py:59
  178.6 12.0 %collective-permute-start.26 = (bf16[4,64,512]{2,1,0:T(8,128)(2,1)S(1)}, bf16[4,64,512]{2,1,0:T(8,128)(2,1)S(1)}, u32[]{:S(2)}, u32[]{:S(2)}) collective-permute-start(bf16[4,64,512]{2,1,0:T(8,128)(2,1)S(1)} %add_convert_fusion.2), channel_id=1, source_target_pairs={{0,6},{2,0},{4,2},{6,4},{1,7},{3,1},{5,3},{7,5},{8,14},{10,8},{12,... | collective-permute-start | bytes 786440 | tf_op jit(solution)/shard_map/ppermute | solution.py:59
  182.7 8.0 %collective-permute-start.24 = (bf16[4,64,512]{2,1,0:T(8,128)(2,1)S(1)}, bf16[4,64,512]{2,1,0:T(8,128)(2,1)S(1)}, u32[]{:S(2)}, u32[]{:S(2)}) collective-permute-start(bf16[4,64,512]{2,1,0:T(8,128)(2,1)S(1)} %add_convert_fusion.3), channel_id=1, source_target_pairs={{0,2},{2,4},{4,6},{6,0},{1,3},{3,5},{5,7},{7,1},{8,10},{10,12},{12... | collective-permute-start | bytes 786440 | tf_op jit(solution)/shard_map/ppermute | solution.py:59
  185.2 12.0 %collective-permute-start.34 = (bf16[2,64,512]{2,1,0:T(8,128)(2,1)S(1)}, bf16[2,64,512]{2,1,0:T(8,128)(2,1)S(1)}, u32[]{:S(2)}, u32[]{:S(2)}) collective-permute-start(bf16[2,64,512]{2,1,0:T(8,128)(2,1)S(1)} %get-tuple-element.62), channel_id=1, source_target_pairs={{0,16},{8,24},{16,0},{24,8},{1,17},{9,25},{17,1},{25,9},{2,18},{10... | collective-permute-start | bytes 393224 | tf_op jit(solution)/shard_map/ppermute | solution.py:59
  188.3 22.8 %collective-permute-start.35 = (bf16[2,64,512]{2,1,0:T(8,128)(2,1)S(1)}, bf16[2,64,512]{2,1,0:T(8,128)(2,1)S(1)}, u32[]{:S(2)}, u32[]{:S(2)}) collective-permute-start(bf16[2,64,512]{2,1,0:T(8,128)(2,1)S(1)} %get-tuple-element.63), channel_id=1, source_target_pairs={{0,24},{8,0},{16,8},{24,16},{1,25},{9,1},{17,9},{25,17},{2,26},{10... | collective-permute-start | bytes 393224 | tf_op jit(solution)/shard_map/ppermute | solution.py:59
  188.9 22.2 %collective-permute-start.32 = (bf16[2,64,512]{2,1,0:T(8,128)(2,1)S(1)}, bf16[2,64,512]{2,1,0:T(8,128)(2,1)S(1)}, u32[]{:S(2)}, u32[]{:S(2)}) collective-permute-start(bf16[2,64,512]{2,1,0:T(8,128)(2,1)S(1)} %get-tuple-element.66), channel_id=1, source_target_pairs={{0,8},{8,16},{16,24},{24,0},{1,9},{9,17},{17,25},{25,1},{2,10},{10... | collective-permute-start | bytes 393224 | tf_op jit(solution)/shard_map/ppermute | solution.py:59
  190.9 21.9 %collective-permute-start.27 = (bf16[2,64,512]{2,1,0:T(8,128)(2,1)S(1)}, bf16[2,64,512]{2,1,0:T(8,128)(2,1)S(1)}, u32[]{:S(2)}, u32[]{:S(2)}) collective-permute-start(bf16[2,64,512]{2,1,0:T(8,128)(2,1)S(1)} %get-tuple-element.64), channel_id=1, source_target_pairs={{0,16},{8,24},{16,0},{24,8},{1,17},{9,25},{17,1},{25,9},{2,18},{10... | collective-permute-start | bytes 393224 | tf_op jit(solution)/shard_map/ppermute | solution.py:59
  193.6 20.3 %collective-permute-start.28 = (bf16[2,64,512]{2,1,0:T(8,128)(2,1)S(1)}, bf16[2,64,512]{2,1,0:T(8,128)(2,1)S(1)}, u32[]{:S(2)}, u32[]{:S(2)}) collective-permute-start(bf16[2,64,512]{2,1,0:T(8,128)(2,1)S(1)} %get-tuple-element.65), channel_id=1, source_target_pairs={{0,24},{8,0},{16,8},{24,16},{1,25},{9,1},{17,9},{25,17},{2,26},{10... | collective-permute-start | bytes 393224 | tf_op jit(solution)/shard_map/ppermute | solution.py:59
  197.2 16.7 %collective-permute-start.25 = (bf16[2,64,512]{2,1,0:T(8,128)(2,1)S(1)}, bf16[2,64,512]{2,1,0:T(8,128)(2,1)S(1)}, u32[]{:S(2)}, u32[]{:S(2)}) collective-permute-start(bf16[2,64,512]{2,1,0:T(8,128)(2,1)S(1)} %get-tuple-element.67), channel_id=1, source_target_pairs={{0,8},{8,16},{16,24},{24,0},{1,9},{9,17},{17,25},{25,1},{2,10},{10... | collective-permute-start | bytes 393224 | tf_op jit(solution)/shard_map/ppermute | solution.py:59
